TPU v7x, 128 devices: a whole 4x4x4 slice. The times are simulated.
128 devices in a mesh: row: 8 (over z, core), col: 16 (over x, y).
Axes of the slice: x: 4, y: 4, z: 4, core: 2. Of those that a mesh axis runs over, the one named last changes fastest.
Arguments:
- gradient: bfloat16 [8192, 8192], P('row', 'col'), may hold values from -1.5 to 1.5
- stat_old: float32 [8192, 8192], P('row', 'col'), may hold values from -6 to 6
- inv_root: bfloat16 [8192, 8192], P('row'), may hold values from -0.0625 to 0.0625
Outputs:
- stat_new: float32 [8192, 8192], P('row', 'col')
- preconditioned: bfloat16 [8192, 8192], P('row', 'col')
All inputs are finite; a program needn't handle non-finite values.
Results may differ from a plain program's by a relative error of at most 0.012.
Values may be sent and summed in bfloat16 or wider, within the bound.
No kernel may reach another device: no remote copies, remote signals or barrier semaphores. Data moves between devices by JAX's collectives and lax.ppermute only.
A program may use at most 192 MiB of HBM per device.

v0:
```python
import jax
import jax.numpy as jnp
from jax import lax
from jax.sharding import PartitionSpec as P


def on_device(gradient, stat_old, inv_root):
    columns = lax.all_gather(gradient, "row", axis=0, tiled=True)
    shares = lax.psum_scatter(
        lax.dot_general(
            columns, gradient, (((1,), (1,)), ((), ())), preferred_element_type=jnp.float32
        ).astype(jnp.bfloat16),
        "col",
        scatter_dimension=0,
        tiled=True,
    ).astype(jnp.float32)
    tile = shares.T
    stat_new = 0.9 * stat_old + 0.1 * tile
    product = jnp.dot(inv_root, columns, preferred_element_type=jnp.float32)
    return (stat_new, product.astype(jnp.bfloat16))


def solution(mesh):
    placed = (P("row", "col"), P("row", "col"), P("row", None))
    return jax.shard_map(
        on_device,
        mesh=mesh,
        in_specs=placed,
        out_specs=(P("row", "col"), P("row", "col")),
        check_vma=False,
    )
```

profile of v0, /device:TPU:1, one launch (start us, length us, event | category | flops | bytes accessed | tf_op | source)
XLA Modules:
  0.0 202.0 jit_solution(18012445078632376771)
XLA Ops:
  7.2 0.0 all-gather.2.cloned.1.call-start
  7.2 0.7 all-gather.2.cloned.1.call-update
  7.9 0.0 reduce-scatter.2.cloned.1.call-start
  7.9 55.4 %all-gather.2.cloned.1.call-done = bf16[8192,512]{1,0:T(8,128)(2,1)} async-done(((bf16[1024,512]{1,0:T(8,128)(2,1)}), bf16[8192,512]{1,0:T(8,128)(2,1)}) %all-gather.2.cloned.1.call-update) | async-done | bytes 8388624 | tf_op jit(solution)/shard_map/all_gather | solution.py:8
  63.3 16.1 %convolution_convert_fusion = bf16[8192,1024]{1,0:T(8,128)(2,1)} fusion(bf16[8192,512]{1,0:T(8,128)(2,1)} %all-gather.2.cloned.1.call-done, bf16[1024,512]{1,0:T(8,128)(2,1)} %param.3), kind=kOutput, calls=%fused_computation | convolution fusion | flops 8598323200 | bytes 26214400 | tf_op jit(solution)/shard_map/dot_general | solution.py:10
  79.4 0.0 reduce-scatter.2.cloned.1.call-update
  79.4 1.9 copy.5
  81.4 15.6 %convolution_convert_fusion.1 = bf16[1024,512]{1,0:T(8,128)(2,1)} fusion(bf16[1024,8192]{1,0:T(8,128)(2,1)} %param.5, bf16[8192,512]{1,0:T(8,128)(2,1)} %all-gather.2.cloned.1.call-done), kind=kOutput, calls=%fused_computation.2 | convolution fusion | flops 8590458880 | bytes 26214400 | tf_op jit(solution)/shard_map/dot_general | solution.py:19
  96.9 92.4 %reduce-scatter.2.cloned.1.call-done = bf16[512,1024]{1,0:T(8,128)(2,1)} async-done(((bf16[8192,1024]{1,0:T(8,128)(2,1)}), bf16[512,1024]{1,0:T(8,128)(2,1)}) %reduce-scatter.2.cloned.1.call-update) | async-done | bytes 1048592 | tf_op jit(solution)/shard_map/reduce_scatter | solution.py:9
  189.3 2.9 %bitcast_add_fusion = f32[1024,512]{0,1:T(8,128)} fusion(bf16[512,1024]{1,0:T(8,128)(2,1)} %reduce-scatter.2.cloned.1.call-done, f32[1024,512]{0,1:T(8,128)S(1)} %copy.5), kind=kLoop, calls=%fused_computation.1 | loop fusion | flops 2097152 | bytes 5242880 | tf_op jit(solution)/shard_map/add | solution.py:18
  192.3 2.9 %copy.6 = f32[1024,512]{1,0:T(8,128)} copy(f32[1024,512]{0,1:T(8,128)} %bitcast_add_fusion) | data formatting | bytes 4194304
Async XLA Ops:
  7.2 56.2 %all-gather.2.cloned.1.call-start = ((), (), s32[]{:S(2)}) async-start(), calls=%async_computation.1 | async-start | bytes 9437184 | tf_op jit(solution)/shard_map/all_gather | solution.py:8
  7.9 181.4 %reduce-scatter.2.cloned.1.call-start = ((), (), s32[]{:S(2)}) async-start(), calls=%async_computation.2 | async-start | bytes 17825792 | tf_op jit(solution)/shard_map/reduce_scatter | solution.py:9
Sparse Core Ops, SparseCore 0:
  9.7 53.5 all-gather.1
  79.5 109.7 reduce-scatter.1
where the time goes:
time: 202 us
  waiting for transfers between devices  148 us (73%)
  matrix products  31.6 us (16%)
  between operations  14 us (7%)
  local copies, waits for them, and re-layouts  4.8 us (2%)
  other arithmetic  2.93 us (1%)
    reduce_scatter x1, waiting for transfers between devices, on_device(): lax.psum_scatter(lax.dot_general(columns, gradient, (((1,), (1,)), ((), (...  92.4 us
    all_gather x1, waiting for transfers between devices, on_device(): columns = lax.all_gather(gradient, 'row', axis=0, tiled=True)  55.4 us
    dot_general x1, matrix products, on_device(): lax.dot_general(columns, gradient, (((1,), (1,)), ((), ())), preferred_el...  16.1 us
    dot_general x1, matrix products, on_device(): product = jnp.dot(inv_root, columns, preferred_element_type=jnp.float32)  15.6 us
    unnamed x2, local copies, waits for them, and re-layouts  4.8 us
  transfers between devices with their start and end apart: 2, of which 2 were waited for; matrix products, arithmetic and copies ran while one was open for 9% of the time, Pallas kernels for 0%

commit v1 on v0

v1 whole, which is shorter than its diff:
```python
import functools

import jax
import jax.numpy as jnp
import numpy as np
from jax import lax
from jax.experimental import pallas as pl
from jax.experimental.pallas import tpu as pltpu
from jax.sharding import Mesh
from jax.sharding import PartitionSpec as P

N = 4
AXES = ("z", "core", "x", "y")
OFFSETS = (1, 3, 2, 0)
F32 = jnp.float32
BF16 = jnp.bfloat16


def linear(z, k, x, y):
    return (((z % N) * 2 + k) * N + x % N) * N + y % N


def devices():
    return [(z, k, x, y) for z in range(N) for k in range(2) for x in range(N) for y in range(N)]


def send(value, where):
    return lax.ppermute(value, AXES, [(linear(*device), linear(*where(*device))) for device in devices()])


def up(n):
    return lambda z, k, x, y: (z + n, k, x, y)


def other_core(value):
    return send(value, lambda z, k, x, y: (z, 1 - k, x, y))


def block_row(z, k, j, q):
    return (q + jnp.where(j < z, 1, 0) + (k + jnp.where(q >= 2, 1, 0)) % 2) % N


def place(distance):
    return jnp.where(distance == 1, 0, jnp.where(distance == 3, 1, jnp.where(distance == 2, 2, 3)))


def shares(mine, theirs, others, turns, diagonal):
    rows, lat = mine.shape
    H = rows // 2
    Q = H // N
    E = Q // 2 if diagonal else 0
    n = len(turns)
    tall = Q + E

    def kernel(mine_ref, theirs_ref, *refs):
        out_ref = refs[-1]
        z, k, x, y = (lax.axis_index(name) for name in AXES)

        def rows_of(block, part, parts):
            start = pl.multiple_of((block % 2) * H + part * (H // parts), H // parts)
            window = pl.ds(start, H // parts)
            return jnp.where(block // 2 == k, mine_ref[window, :], theirs_ref[window, :])

        for t, turn in enumerate(turns):
            j = (z + turn) % N
            for i in range(N):
                q = 2 * (k if i < 2 else 1 - k) + i % 2
                p = block_row(z, k, j, q)
                right = (refs[2 * t + i // 2])[(i % 2) * H : (i % 2 + 1) * H, :]
                left = []
                for offset in OFFSETS:
                    c = (x + offset) % N
                    left.append(rows_of(p, c, N))
                    if diagonal:
                        left.append(rows_of((q + 2) % N, k * N + c, 2 * N))
                result = lax.dot_general(
                    jnp.concatenate(left, 0), right, (((1,), (1,)), ((), ())), preferred_element_type=F32
                ).astype(BF16)
                mark = place((q - y) % N)
                for m in range(N):
                    first, second = jnp.where(k == 0, m, mark), jnp.where(k == 0, mark, m)
                    out_ref[first, second, t * tall : (t + 1) * tall, :] = result[m * tall : (m + 1) * tall]

    whole = pl.BlockSpec(memory_space=pltpu.VMEM)
    flat = [a for pair in others for a in pair]
    return pl.pallas_call(
        kernel,
        out_shape=jax.ShapeDtypeStruct((N, N, n * tall, H), BF16),
        in_specs=[whole] * (2 + len(flat)),
        out_specs=whole,
        compiler_params=pltpu.CompilerParams(vmem_limit_bytes=40 * 2**20),
        cost_estimate=pl.CostEstimate(flops=2 * 16 * n * tall * H * lat, bytes_accessed=2 * lat * rows * 4 * n, transcendentals=0),
        name="shares",
    )(mine, theirs, *flat)


def add(terms):
    total = terms[0].astype(F32)
    for term in terms[1:]:
        total = total + term.astype(F32)
    return total.astype(BF16)


def reduce(parts, stage):
    def where(z, k, x, y, n):
        return (z, k, x + n, y) if k == stage else (z, k, x, y + n)

    got = [send(parts[r], functools.partial(where, n=OFFSETS[r])) for r in range(N - 1)]
    return add([*got, parts[N - 1]])


def pick(stacked, index):
    return lax.dynamic_index_in_dim(stacked, index, 0, keepdims=False)


@functools.cache
def final_plan():
    edges = []
    for z, k, x, y in devices():
        late = (k + (1 if y >= 2 else 0)) % 2
        p = (y + (1 if x < z else 0) + late) % N
        edges.append(((z, k, x, y), (z, p // 2, x, y), p % 2, 0))
        if x == z and late == 0:
            edges.append(((z, k, x, y), (z, 1 - k, x, y), y % 2, 4))
        else:
            edges.append(((z, k, x, y), (x, y // 2, z, p), y % 2, 1))
    touching = {}
    for n, (source, target, _, _) in enumerate(edges):
        touching.setdefault(("from", source), []).append(n)
        touching.setdefault(("to", target), []).append(n)
    colour = {}
    for start in range(len(edges)):
        stack = [] if start in colour else [(start, 0)]
        while stack:
            n, c = stack.pop()
            if n in colour:
                assert colour[n] == c
                continue
            colour[n] = c
            for end in (("from", edges[n][0]), ("to", edges[n][1])):
                assert len(touching[end]) == 2
                stack.extend((m, 1 - c) for m in touching[end] if m != n)
    routes = [{}, {}]
    view = np.full((2 * N**3, 2), -1, np.int32)
    special = np.full((2 * N**3,), 2, np.int32)
    for n, (source, target, slot, kind) in enumerate(edges):
        c = colour[n]
        assert source not in routes[c] and view[linear(*target), slot] == -1
        routes[c][source] = target
        view[linear(*target), slot] = c + (2 if kind == 1 else kind)
        if kind == 4:
            special[linear(*source)] = c
    assert (view >= 0).all()
    return routes, np.concatenate([view, special[:, None]], 1)


def on_device(gradient, stat_old, inv_root):
    rows, lat = gradient.shape
    H = rows // 2
    Q = H // N
    z, k, x, y = (lax.axis_index(name) for name in AXES)

    def term(tile, turn, core):
        block = 2 * ((z + turn) % N) + core
        columns = lax.dynamic_slice_in_dim(inv_root, block * rows, rows, 1)
        return jnp.dot(columns, tile, preferred_element_type=F32)

    above = send(gradient, up(-1))
    below = send(gradient, up(1))
    partner = other_core(gradient)
    far = send(jnp.where(k == 0, below, above), lambda z, k, x, y: (z + 1 - 2 * k, k, x, y))
    above_partner, below_partner = other_core(jnp.stack([above, below]))
    far_partner = other_core(far)

    near = shares(gradient, partner, [(gradient, partner)], (0,), True)
    near = reduce(near, 0)
    near = reduce(near, 1)
    middle = shares(gradient, partner, [(above, above_partner), (below, below_partner)], (1, 3), False)
    middle = reduce(middle, 0)
    last = shares(gradient, partner, [(far, far_partner)], (2,), False)
    last = reduce(last, 0)
    middle = reduce(middle, 1)
    last = reduce(last, 1)

    product = term(gradient, 0, k) + term(partner, 0, 1 - k)
    product = product + (term(above, 1, k) + term(above_partner, 1, 1 - k))
    product = product + (term(below, 3, k) + term(below_partner, 3, 1 - k))
    product = product + (term(far, 2, k) + term(far_partner, 2, 1 - k))

    pieces = jnp.stack([near[:Q], middle[:Q], last, middle[Q:]])
    got = []
    for d in range(N):
        piece = jnp.concatenate([pick(pieces, (x + d - z) % N), near[Q:]], 0)
        got.append(send(piece, lambda z, k, x, y, d=d: (z, k, x + d, y)) if d else piece)
    got = jnp.stack(got)
    got = jnp.stack([pick(got, (x - c) % N) for c in range(N)])
    block = got[:, :Q].reshape(H, H)
    half = got[:, Q:].reshape(H // 2, H)

    routes, view = final_plan()
    here = jnp.asarray(view)[((z * 2 + k) * N + x) * N + y]
    padded = jnp.concatenate([half, half], 0)
    arrived = [send(jnp.where(here[2] == c, padded, block), lambda *device, c=c: routes[c][device]) for c in range(2)]
    stat = []
    for slot in range(2):
        which = here[slot]
        value = jnp.where(which % 2 == 0, arrived[0], arrived[1])
        diagonal = jnp.where(k == 0, jnp.concatenate([half, value[: H // 2]]), jnp.concatenate([value[: H // 2], half]))
        value = jnp.where(which >= 4, diagonal, jnp.where(which >= 2, value.T, value))
        stat.append(0.9 * stat_old[slot * H : (slot + 1) * H] + 0.1 * value.astype(F32))
    return jnp.concatenate(stat), product.astype(BF16)


def solution(mesh):
    fine = Mesh(mesh.devices.reshape(N, 2, N, N), AXES)
    row, col = ("z", "core"), ("x", "y")
    return jax.shard_map(
        on_device,
        mesh=fine,
        in_specs=(P(row, col), P(row, col), P(row, None)),
        out_specs=(P(row, col), P(row, col)),
        check_vma=False,
    )
```

time: 202 us -> 190 us (0.941)
  the two profiles are of different devices: /device:TPU:1 before, /device:TPU:14 now
where the time goes in v1:
time: 190 us; the launch traced here: 189 us
  waiting for transfers between devices  87.8 us (46%)
  starting transfers between devices  46.9 us (25%)
  matrix products  25.9 us (14%)
  between operations  8.91 us (5%)
  other arithmetic  7.33 us (4%)
  local copies, waits for them, and re-layouts  6.93 us (4%)
  Pallas kernels  5.5 us (3%)
    ppermute x29, waiting for transfers between devices, send(): lax.ppermute(value, AXES, [(linear(*device), linear(*where(*device))) for...  87.8 us
    ppermute x29, starting transfers between devices, send(): lax.ppermute(value, AXES, [(linear(*device), linear(*where(*device))) for...  46.9 us
    dot_general x8, matrix products, term(): return jnp.dot(columns, tile, preferred_element_type=F32)  25.9 us
    pallas_call x3, Pallas kernels, shares(): pl.pallas_call(kernel, out_shape=jax.ShapeDtypeStruct((N, N, n * tall, H)...  5.5 us
  transfers between devices with their start and end apart: 29, of which 15 were waited for; matrix products, arithmetic and copies ran while one was open for 17% of the time, Pallas kernels for 3%

profile of v1, /device:TPU:14, one launch (start us, length us, event | category | flops | bytes accessed | tf_op | source)
XLA Modules:
  0.0 189.3 jit_solution(14619425098674006798)
XLA Ops:
  0.6 4.1 %collective-permute-start.7 = (bf16[1024,512]{1,0:T(8,128)(2,1)}, bf16[1024,512]{1,0:T(8,128)(2,1)S(1)}, u32[]{:S(2)}, u32[]{:S(2)}) collective-permute-start(bf16[1024,512]{1,0:T(8,128)(2,1)} %mine_ref.5), channel_id=1, source_target_pairs={{0,96},{1,97},{2,98},{3,99},{4,100},{5,101},{6,102},{7,103},{8,104... | collective-permute-start | bytes 3145736 | tf_op jit(solution)/shard_map/ppermute | solution.py:28
  13.9 3.1 %fusion.15 = f32[1024,512]{1,0:T(8,128)S(1)} fusion(bf16[1024,512]{1,0:T(8,128)(2,1)} %mine_ref.5, bf16[1024,8192]{1,0:T(8,128)(2,1)} %param.6, s32[]{:T(128)S(6)} %select_n.229), kind=kOutput, calls=%fused_computation.19 | convolution fusion | flops 1073741824 | bytes 5242884 | tf_op jit(solution)/shard_map/dot_general | solution.py:166
  17.1 10.4 %collective-permute-done.7.refs_0_ = bf16[1024,512]{1,0:T(8,128)(2,1)S(1)} collective-permute-done((bf16[1024,512]{1,0:T(8,128)(2,1)}, bf16[1024,512]{1,0:T(8,128)(2,1)S(1)}, u32[]{:S(2)}, u32[]{:S(2)}) %collective-permute-start.7) | collective-permute-done | bytes 1048608 | tf_op jit(solution)/shard_map/ppermute | solution.py:28
  27.5 3.3 %collective-permute-done.8.refs_2_ = bf16[1024,512]{1,0:T(8,128)(2,1)S(1)} collective-permute-done((bf16[1024,512]{1,0:T(8,128)(2,1)}, bf16[1024,512]{1,0:T(8,128)(2,1)S(1)}, u32[]{:S(2)}, u32[]{:S(2)}) %collective-permute-start.8) | collective-permute-done | bytes 1048608 | tf_op jit(solution)/shard_map/ppermute | solution.py:28
  36.8 2.8 %fusion.11 = f32[1024,512]{1,0:T(8,128)S(1)} fusion(bf16[1024,512]{1,0:T(8,128)(2,1)S(1)} %collective-permute-done.7.refs_0_, bf16[1024,8192]{1,0:T(8,128)(2,1)} %param.6, s32[]{:T(128)S(6)} %select_n.232), kind=kOutput, calls=%fused_computation.15 | convolution fusion | flops 1073741824 | bytes 5242884 | tf_op jit(solution)/shard_map/dot_general | solution.py:166
  39.6 4.2 %fusion.7 = f32[1024,512]{1,0:T(8,128)} fusion(bf16[1024,512]{1,0:T(8,128)(2,1)S(1)} %collective-permute-done.8.refs_2_, bf16[1024,8192]{1,0:T(8,128)(2,1)} %param.6, s32[]{:T(128)S(6)} %select_n.235), kind=kOutput, calls=%fused_computation.11 | convolution fusion | flops 1073741824 | bytes 5242884 | tf_op jit(solution)/shard_map/dot_general | solution.py:166
  43.8 3.2 %collective-permute-done.16.refs_0_ = bf16[1024,512]{1,0:T(8,128)(2,1)S(1)} collective-permute-done((bf16[1024,512]{1,0:T(8,128)(2,1)S(1)}, bf16[1024,512]{1,0:T(8,128)(2,1)S(1)}, u32[]{:S(2)}, u32[]{:S(2)}) %collective-permute-start.16) | collective-permute-done | bytes 1048608 | tf_op jit(solution)/shard_map/ppermute | solution.py:28
  47.0 8.2 %collective-permute-done.2 = bf16[4,192,512]{2,1,0:T(8,128)(2,1)S(1)} collective-permute-done((bf16[4,192,512]{2,1,0:T(8,128)(2,1)S(1)}, bf16[4,192,512]{2,1,0:T(8,128)(2,1)S(1)}, u32[]{:S(2)}, u32[]{:S(2)}) %collective-permute-start.2) | collective-permute-done | bytes 786464 | tf_op jit(solution)/shard_map/ppermute | solution.py:28
  57.7 2.3 %collective-permute-start.6 = (bf16[192,512]{1,0:T(8,128)(2,1)S(1)}, bf16[192,512]{1,0:T(8,128)(2,1)S(1)}, u32[]{:S(2)}, u32[]{:S(2)}) collective-permute-start(bf16[192,512]{1,0:T(8,128)(2,1)S(1)} %get-tuple-element.27), channel_id=1, source_target_pairs={{0,2},{1,3},{2,0},{3,1},{4,6},{5,7},{6,4},{7,5},{8,10},{9,11},{10,... | collective-permute-start | bytes 589832 | tf_op jit(solution)/shard_map/ppermute | solution.py:28
  60.0 2.8 %fusion.13 = f32[1024,512]{1,0:T(8,128)S(1)} fusion(bf16[1024,512]{1,0:T(8,128)(2,1)S(1)} %collective-permute-done.theirs_ref.refs_1_, bf16[1024,8192]{1,0:T(8,128)(2,1)} %param.6, s32[]{:T(128)S(6)} %select_n.230), kind=kOutput, calls=%fused_computation.17 | convolution fusion | flops 1073741824 | bytes 5242884 | tf_op jit(solution)/shard_map/dot_general | solution.py:166
  63.0 2.8 %collective-permute-done.6 = bf16[192,512]{1,0:T(8,128)(2,1)S(1)} collective-permute-done((bf16[192,512]{1,0:T(8,128)(2,1)S(1)}, bf16[192,512]{1,0:T(8,128)(2,1)S(1)}, u32[]{:S(2)}, u32[]{:S(2)}) %collective-permute-start.6) | collective-permute-done | bytes 196640 | tf_op jit(solution)/shard_map/ppermute | solution.py:28
  72.4 2.4 %shares.4 = bf16[4,4,256,512]{3,2,1,0:T(8,128)(2,1)S(1)} custom-call(bf16[1024,512]{1,0:T(8,128)(2,1)S(1)} %copy-done, bf16[1024,512]{1,0:T(8,128)(2,1)S(1)} %collective-permute-done.theirs_ref.refs_1_, bf16[1024,512]{1,0:T(8,128)(2,1)S(1)} %collective-permute-done.7.refs_0_, bf16[1024,512]{1,0:T(8,128)(2,1)S(1)} %get-tuple-element.14.refs_1_, ...), custom_call_target="tpu_custom_call" | custom-call | flops 2147483648 | bytes 8388608 | tf_op jit(solution)/shard_map/shares/pallas_call | solution.py:86
  79.8 2.9 %fusion.3 = f32[1024,512]{1,0:T(8,128)S(1)} fusion(bf16[1024,512]{1,0:T(8,128)(2,1)S(1)} %collective-permute-done.16.refs_0_, bf16[1024,8192]{1,0:T(8,128)(2,1)} %param.6, s32[]{:T(128)S(6)} %select_n.238), kind=kOutput, calls=%fused_computation.7 | convolution fusion | flops 1073741824 | bytes 5242884 | tf_op jit(solution)/shard_map/dot_general | solution.py:166
  82.6 3.1 %collective-permute-done.19 = bf16[4,128,512]{2,1,0:T(8,128)(2,1)} collective-permute-done((bf16[4,128,512]{2,1,0:T(8,128)(2,1)}, bf16[4,128,512]{2,1,0:T(8,128)(2,1)}, u32[]{:S(2)}, u32[]{:S(2)}) %collective-permute-start.19) | collective-permute-done | bytes 524320 | tf_op jit(solution)/shard_map/ppermute | solution.py:28
  89.5 8.0 %collective-permute-done.10 = bf16[4,256,512]{2,1,0:T(8,128)(2,1)S(1)} collective-permute-done((bf16[4,256,512]{2,1,0:T(8,128)(2,1)S(1)}, bf16[4,256,512]{2,1,0:T(8,128)(2,1)S(1)}, u32[]{:S(2)}, u32[]{:S(2)}) %collective-permute-start.10) | collective-permute-done | bytes 1048608 | tf_op jit(solution)/shard_map/ppermute | solution.py:28
  98.9 12.1 %collective-permute-done.11 = bf16[4,256,512]{2,1,0:T(8,128)(2,1)S(1)} collective-permute-done((bf16[4,256,512]{2,1,0:T(8,128)(2,1)S(1)}, bf16[4,256,512]{2,1,0:T(8,128)(2,1)S(1)}, u32[]{:S(2)}, u32[]{:S(2)}) %collective-permute-start.11) | collective-permute-done | bytes 1048608 | tf_op jit(solution)/shard_map/ppermute | solution.py:28
  115.2 2.8 %fusion.5 = f32[1024,512]{1,0:T(8,128)S(1)} fusion(bf16[1024,8192]{1,0:T(8,128)(2,1)} %param.6, s32[]{:T(128)S(6)} %select_n.236, bf16[2,1024,512]{2,1,0:T(8,128)(2,1)S(1)} %collective-permute-done.9), kind=kOutput, calls=%fused_computation.9 | convolution fusion | flops 1073741824 | bytes 5242884 | tf_op jit(solution)/shard_map/dot_general | solution.py:166
  119.1 3.2 %collective-permute-done.15 = bf16[256,512]{1,0:T(8,128)(2,1)S(1)} collective-permute-done((bf16[256,512]{1,0:T(8,128)(2,1)S(1)}, bf16[256,512]{1,0:T(8,128)(2,1)S(1)}, u32[]{:S(2)}, u32[]{:S(2)}) %collective-permute-start.15) | collective-permute-done | bytes 262176 | tf_op jit(solution)/shard_map/ppermute | solution.py:28
  125.9 2.8 %fusion.9 = f32[1024,512]{1,0:T(8,128)S(1)} fusion(bf16[1024,8192]{1,0:T(8,128)(2,1)} %param.6, s32[]{:T(128)S(6)} %select_n.233, bf16[2,1024,512]{2,1,0:T(8,128)(2,1)S(1)} %collective-permute-done.9), kind=kOutput, calls=%fused_computation.13 | convolution fusion | flops 1073741824 | bytes 5242884 | tf_op jit(solution)/shard_map/dot_general | solution.py:166
  130.6 2.0 %collective-permute-done.26 = bf16[192,512]{1,0:T(8,128)(2,1)S(1)} collective-permute-done((bf16[192,512]{1,0:T(8,128)(2,1)S(1)}, bf16[192,512]{1,0:T(8,128)(2,1)S(1)}, u32[]{:S(2)}, u32[]{:S(2)}) %collective-permute-start.26) | collective-permute-done | bytes 196640 | tf_op jit(solution)/shard_map/ppermute | solution.py:28
  133.9 15.9 %collective-permute-start.28 = (bf16[512,512]{1,0:T(8,128)(2,1)S(1)}, bf16[512,512]{1,0:T(8,128)(2,1)S(1)}, u32[]{:S(2)}, u32[]{:S(2)}) collective-permute-start(bf16[512,512]{1,0:T(8,128)(2,1)S(1)} %get-tuple-element.20), channel_id=1, source_target_pairs={{0,16},{1,1},{2,18},{3,3},{4,32},{5,33},{6,51},{7,48},{8,64},{9,65... | collective-permute-start | bytes 1572872 | tf_op jit(solution)/shard_map/ppermute | solution.py:28
  149.8 4.4 %add_convert_fusion = bf16[1024,512]{1,0:T(8,128)(2,1)} fusion(f32[1024,512]{1,0:T(8,128)S(1)} %fusion.3, f32[1024,512]{1,0:T(8,128)S(1)} %copy-done.2, f32[1024,512]{1,0:T(8,128)S(1)} %fusion.5, f32[1024,512]{1,0:T(8,128)S(1)} %fusion.11, f32[1024,512]{1,0:T(8,128)S(1)} %fusion.9, f32[1024,512]{1,0:T(8,128)S(1)} %fusion.15, f32[1024,512]{1,0:T(8,128)S(1)} %fusion.13, ...), kind=kOutput, calls=%fused_computation.4 | convolution fusion | flops 1077936128 | bytes 18874372 | tf_op jit(solution)/shard_map/dot_general | solution.py:166
  154.3 28.0 %collective-permute-done.28 = bf16[512,512]{1,0:T(8,128)(2,1)S(1)} collective-permute-done((bf16[512,512]{1,0:T(8,128)(2,1)S(1)}, bf16[512,512]{1,0:T(8,128)(2,1)S(1)}, u32[]{:S(2)}, u32[]{:S(2)}) %collective-permute-start.28) | collective-permute-done | bytes 524320 | tf_op jit(solution)/shard_map/ppermute | solution.py:28
  185.8 2.0 %multiply_add_fusion.1 = (f32[512,512]{1,0:T(8,128)S(1)}, f32[512,512]{1,0:T(8,128)S(1)}) fusion(f32[1024,512]{1,0:T(8,128)S(1)} %copy-done.1, bf16[256,512]{1,0:T(8,128)(2,1)S(1)} %bitcast.116, bf16[256,512]{1,0:T(8,128)(2,1)} %slice.185, bf16[512,512]{1,0:T(8,128)(2,1)} %copy.6, bf16[512,512]{1,0:T(8,128)(2,1)S(1)} %get-tuple-element.15, pred[]{:T(512)S(6)} %ge.13, ...), kind=kLoop, calls=%fused_computation.32 | loop fusion | flops 7340032 | bytes 7077893 | tf_op jit(solution)/shard_map/add | solution.py:210
  (89 shorter events, 43.5 us)
Async XLA Ops:
  0.6 26.8 %collective-permute-start.7 = (bf16[1024,512]{1,0:T(8,128)(2,1)}, bf16[1024,512]{1,0:T(8,128)(2,1)S(1)}, u32[]{:S(2)}, u32[]{:S(2)}) collective-permute-start(bf16[1024,512]{1,0:T(8,128)(2,1)} %mine_ref.5), channel_id=1, source_target_pairs={{0,96},{1,97},{2,98},{3,99},{4,100},{5,101},{6,102},{7,103},{8,104... | collective-permute-start | bytes 3145736 | tf_op jit(solution)/shard_map/ppermute | solution.py:28
  4.7 26.0 %collective-permute-start.8 = (bf16[1024,512]{1,0:T(8,128)(2,1)}, bf16[1024,512]{1,0:T(8,128)(2,1)S(1)}, u32[]{:S(2)}, u32[]{:S(2)}) collective-permute-start(bf16[1024,512]{1,0:T(8,128)(2,1)} %mine_ref.5), channel_id=1, source_target_pairs={{0,32},{1,33},{2,34},{3,35},{4,36},{5,37},{6,38},{7,39},{8,40},{9,... | collective-permute-start | bytes 3145736 | tf_op jit(solution)/shard_map/ppermute | solution.py:28
  4.7 26.2 %collective-permute-start = (bf16[1024,512]{1,0:T(8,128)(2,1)}, bf16[1024,512]{1,0:T(8,128)(2,1)S(1)}, u32[]{:S(2)}, u32[]{:S(2)}) collective-permute-start(bf16[1024,512]{1,0:T(8,128)(2,1)} %mine_ref.5), channel_id=1, source_target_pairs={{0,16},{1,17},{2,18},{3,19},{4,20},{5,21},{6,22},{7,23},{8,24},{9,... | collective-permute-start | bytes 3145736 | tf_op jit(solution)/shard_map/ppermute | solution.py:28
  30.9 16.1 %collective-permute-start.16 = (bf16[1024,512]{1,0:T(8,128)(2,1)S(1)}, bf16[1024,512]{1,0:T(8,128)(2,1)S(1)}, u32[]{:S(2)}, u32[]{:S(2)}) collective-permute-start(bf16[1024,512]{1,0:T(8,128)(2,1)S(1)} %broadcast_select_fusion), channel_id=1, source_target_pairs={{0,32},{1,33},{2,34},{3,35},{4,36},{5,37},{6,38},{7,39},{8,40},{9,... | collective-permute-start | bytes 3145736 | tf_op jit(solution)/shard_map/ppermute | solution.py:28
  33.0 14.0 %collective-permute-start.1 = (bf16[4,192,512]{2,1,0:T(8,128)(2,1)S(1)}, bf16[4,192,512]{2,1,0:T(8,128)(2,1)S(1)}, u32[]{:S(2)}, u32[]{:S(2)}) collective-permute-start(bf16[4,192,512]{2,1,0:T(8,128)(2,1)S(1)} %get-tuple-element.5), channel_id=1, source_target_pairs={{0,4},{1,5},{2,6},{3,7},{4,8},{5,9},{6,10},{7,11},{8,12},{9,13},{1... | collective-permute-start | bytes 2359304 | tf_op jit(solution)/shard_map/ppermute | solution.py:28
  33.5 21.6 %collective-permute-start.2 = (bf16[4,192,512]{2,1,0:T(8,128)(2,1)S(1)}, bf16[4,192,512]{2,1,0:T(8,128)(2,1)S(1)}, u32[]{:S(2)}, u32[]{:S(2)}) collective-permute-start(bf16[4,192,512]{2,1,0:T(8,128)(2,1)S(1)} %get-tuple-element.7), channel_id=1, source_target_pairs={{0,12},{1,13},{2,14},{3,15},{4,0},{5,1},{6,2},{7,3},{8,4},{9,5},{1... | collective-permute-start | bytes 2359304 | tf_op jit(solution)/shard_map/ppermute | solution.py:28
  35.1 20.1 %collective-permute-start.3 = (bf16[4,192,512]{2,1,0:T(8,128)(2,1)S(1)}, bf16[4,192,512]{2,1,0:T(8,128)(2,1)S(1)}, u32[]{:S(2)}, u32[]{:S(2)}) collective-permute-start(bf16[4,192,512]{2,1,0:T(8,128)(2,1)S(1)} %get-tuple-element.6), channel_id=1, source_target_pairs={{0,8},{1,9},{2,10},{3,11},{4,12},{5,13},{6,14},{7,15},{8,0},{9,1},... | collective-permute-start | bytes 2359304 | tf_op jit(solution)/shard_map/ppermute | solution.py:28
  36.7 35.6 %collective-permute-start.9 = (bf16[2,1024,512]{2,1,0:T(8,128)(2,1)S(1)}, bf16[2,1024,512]{2,1,0:T(8,128)(2,1)S(1)}, u32[]{:S(2)}, u32[]{:S(2)}) collective-permute-start(bf16[2,1024,512]{2,1,0:T(8,128)(2,1)S(1)} %pad_maximum_fusion), channel_id=1, source_target_pairs={{0,16},{1,17},{2,18},{3,19},{4,20},{5,21},{6,22},{7,23},{8,24},{9,... | collective-permute-start | bytes 6291464 | tf_op jit(solution)/shard_map/ppermute | solution.py:28
  47.0 18.9 %collective-permute-start.17 = (bf16[1024,512]{1,0:T(8,128)(2,1)S(1)}, bf16[1024,512]{1,0:T(8,128)(2,1)S(1)}, u32[]{:S(2)}, u32[]{:S(2)}) collective-permute-start(bf16[1024,512]{1,0:T(8,128)(2,1)S(1)} %collective-permute-done.16.refs_0_), channel_id=1, source_target_pairs={{0,16},{1,17},{2,18},{3,19},{4,20},{5,21},{6,22},{7,23},{8,24},{9,... | collective-permute-start | bytes 3145736 | tf_op jit(solution)/shard_map/ppermute | solution.py:28
  57.7 8.0 %collective-permute-start.6 = (bf16[192,512]{1,0:T(8,128)(2,1)S(1)}, bf16[192,512]{1,0:T(8,128)(2,1)S(1)}, u32[]{:S(2)}, u32[]{:S(2)}) collective-permute-start(bf16[192,512]{1,0:T(8,128)(2,1)S(1)} %get-tuple-element.27), channel_id=1, source_target_pairs={{0,2},{1,3},{2,0},{3,1},{4,6},{5,7},{6,4},{7,5},{8,10},{9,11},{10,... | collective-permute-start | bytes 589832 | tf_op jit(solution)/shard_map/ppermute | solution.py:28
  68.4 9.5 %collective-permute-start.18 = (bf16[4,128,512]{2,1,0:T(8,128)(2,1)}, bf16[4,128,512]{2,1,0:T(8,128)(2,1)}, u32[]{:S(2)}, u32[]{:S(2)}) collective-permute-start(bf16[4,128,512]{2,1,0:T(8,128)(2,1)} %get-tuple-element.10), channel_id=1, source_target_pairs={{0,4},{1,5},{2,6},{3,7},{4,8},{5,9},{6,10},{7,11},{8,12},{9,13},{1... | collective-permute-start | bytes 1572872 | tf_op jit(solution)/shard_map/ppermute | solution.py:28
  69.4 16.3 %collective-permute-start.19 = (bf16[4,128,512]{2,1,0:T(8,128)(2,1)}, bf16[4,128,512]{2,1,0:T(8,128)(2,1)}, u32[]{:S(2)}, u32[]{:S(2)}) collective-permute-start(bf16[4,128,512]{2,1,0:T(8,128)(2,1)} %get-tuple-element.12), channel_id=1, source_target_pairs={{0,12},{1,13},{2,14},{3,15},{4,0},{5,1},{6,2},{7,3},{8,4},{9,5},{1... | collective-permute-start | bytes 1572872 | tf_op jit(solution)/shard_map/ppermute | solution.py:28
  70.4 15.3 %collective-permute-start.20 = (bf16[4,128,512]{2,1,0:T(8,128)(2,1)}, bf16[4,128,512]{2,1,0:T(8,128)(2,1)}, u32[]{:S(2)}, u32[]{:S(2)}) collective-permute-start(bf16[4,128,512]{2,1,0:T(8,128)(2,1)} %get-tuple-element.11), channel_id=1, source_target_pairs={{0,8},{1,9},{2,10},{3,11},{4,12},{5,13},{6,14},{7,15},{8,0},{9,1},... | collective-permute-start | bytes 1572872 | tf_op jit(solution)/shard_map/ppermute | solution.py:28
  75.2 22.3 %collective-permute-start.10 = (bf16[4,256,512]{2,1,0:T(8,128)(2,1)S(1)}, bf16[4,256,512]{2,1,0:T(8,128)(2,1)S(1)}, u32[]{:S(2)}, u32[]{:S(2)}) collective-permute-start(bf16[4,256,512]{2,1,0:T(8,128)(2,1)S(1)} %get-tuple-element.2), channel_id=1, source_target_pairs={{0,4},{1,5},{2,6},{3,7},{4,8},{5,9},{6,10},{7,11},{8,12},{9,13},{1... | collective-permute-start | bytes 3145736 | tf_op jit(solution)/shard_map/ppermute | solution.py:28
  76.1 34.9 %collective-permute-start.11 = (bf16[4,256,512]{2,1,0:T(8,128)(2,1)S(1)}, bf16[4,256,512]{2,1,0:T(8,128)(2,1)S(1)}, u32[]{:S(2)}, u32[]{:S(2)}) collective-permute-start(bf16[4,256,512]{2,1,0:T(8,128)(2,1)S(1)} %get-tuple-element.4), channel_id=1, source_target_pairs={{0,12},{1,13},{2,14},{3,15},{4,0},{5,1},{6,2},{7,3},{8,4},{9,5},{1... | collective-permute-start | bytes 3145736 | tf_op jit(solution)/shard_map/ppermute | solution.py:28
  77.9 33.1 %collective-permute-start.12 = (bf16[4,256,512]{2,1,0:T(8,128)(2,1)S(1)}, bf16[4,256,512]{2,1,0:T(8,128)(2,1)S(1)}, u32[]{:S(2)}, u32[]{:S(2)}) collective-permute-start(bf16[4,256,512]{2,1,0:T(8,128)(2,1)S(1)} %get-tuple-element.3), channel_id=1, source_target_pairs={{0,8},{1,9},{2,10},{3,11},{4,12},{5,13},{6,14},{7,15},{8,0},{9,1},... | collective-permute-start | bytes 3145736 | tf_op jit(solution)/shard_map/ppermute | solution.py:28
  87.4 26.4 %collective-permute-start.21 = (bf16[128,512]{1,0:T(8,128)(2,1)S(1)}, bf16[128,512]{1,0:T(8,128)(2,1)S(1)}, u32[]{:S(2)}, u32[]{:S(2)}) collective-permute-start(bf16[128,512]{1,0:T(8,128)(2,1)S(1)} %get-tuple-element.33), channel_id=1, source_target_pairs={{0,1},{1,2},{2,3},{3,0},{4,5},{5,6},{6,7},{7,4},{8,9},{9,10},{10,1... | collective-permute-start | bytes 393224 | tf_op jit(solution)/shard_map/ppermute | solution.py:28
  88.2 29.9 %collective-permute-start.22 = (bf16[128,512]{1,0:T(8,128)(2,1)S(1)}, bf16[128,512]{1,0:T(8,128)(2,1)S(1)}, u32[]{:S(2)}, u32[]{:S(2)}) collective-permute-start(bf16[128,512]{1,0:T(8,128)(2,1)S(1)} %get-tuple-element.35), channel_id=1, source_target_pairs={{0,3},{1,0},{2,1},{3,2},{4,7},{5,4},{6,5},{7,6},{8,11},{9,8},{10,9... | collective-permute-start | bytes 393224 | tf_op jit(solution)/shard_map/ppermute | solution.py:28
  97.5 20.5 %collective-permute-start.23 = (bf16[128,512]{1,0:T(8,128)(2,1)S(1)}, bf16[128,512]{1,0:T(8,128)(2,1)S(1)}, u32[]{:S(2)}, u32[]{:S(2)}) collective-permute-start(bf16[128,512]{1,0:T(8,128)(2,1)S(1)} %get-tuple-element.34), channel_id=1, source_target_pairs={{0,2},{1,3},{2,0},{3,1},{4,6},{5,7},{6,4},{7,5},{8,10},{9,11},{10,... | collective-permute-start | bytes 393224 | tf_op jit(solution)/shard_map/ppermute | solution.py:28
  113.8 8.6 %collective-permute-start.15 = (bf16[256,512]{1,0:T(8,128)(2,1)S(1)}, bf16[256,512]{1,0:T(8,128)(2,1)S(1)}, u32[]{:S(2)}, u32[]{:S(2)}) collective-permute-start(bf16[256,512]{1,0:T(8,128)(2,1)S(1)} %get-tuple-element.18), channel_id=1, source_target_pairs={{0,2},{1,3},{2,0},{3,1},{4,6},{5,7},{6,4},{7,5},{8,10},{9,11},{10,... | collective-permute-start | bytes 786440 | tf_op jit(solution)/shard_map/ppermute | solution.py:28
  123.3 7.3 %collective-permute-start.25 = (bf16[192,512]{1,0:T(8,128)(2,1)S(1)}, bf16[192,512]{1,0:T(8,128)(2,1)S(1)}, u32[]{:S(2)}, u32[]{:S(2)}) collective-permute-start(bf16[192,512]{1,0:T(8,128)(2,1)S(1)} %get-tuple-element.40), channel_id=1, source_target_pairs={{0,8},{1,9},{2,10},{3,11},{4,12},{5,13},{6,14},{7,15},{8,0},{9,1},... | collective-permute-start | bytes 589832 | tf_op jit(solution)/shard_map/ppermute | solution.py:28
  124.5 8.0 %collective-permute-start.26 = (bf16[192,512]{1,0:T(8,128)(2,1)S(1)}, bf16[192,512]{1,0:T(8,128)(2,1)S(1)}, u32[]{:S(2)}, u32[]{:S(2)}) collective-permute-start(bf16[192,512]{1,0:T(8,128)(2,1)S(1)} %get-tuple-element.41), channel_id=1, source_target_pairs={{0,12},{1,13},{2,14},{3,15},{4,0},{5,1},{6,2},{7,3},{8,4},{9,5},{1... | collective-permute-start | bytes 589832 | tf_op jit(solution)/shard_map/ppermute | solution.py:28
  133.1 21.2 %collective-permute-start.27 = (bf16[512,512]{1,0:T(8,128)(2,1)S(1)}, bf16[512,512]{1,0:T(8,128)(2,1)S(1)}, u32[]{:S(2)}, u32[]{:S(2)}) collective-permute-start(bf16[512,512]{1,0:T(8,128)(2,1)S(1)} %get-tuple-element.21), channel_id=1, source_target_pairs={{0,0},{1,17},{2,19},{3,16},{4,4},{5,5},{6,22},{7,7},{8,8},{9,9},{1... | collective-permute-start | bytes 1572872 | tf_op jit(solution)/shard_map/ppermute | solution.py:28
  133.9 48.3 %collective-permute-start.28 = (bf16[512,512]{1,0:T(8,128)(2,1)S(1)}, bf16[512,512]{1,0:T(8,128)(2,1)S(1)}, u32[]{:S(2)}, u32[]{:S(2)}) collective-permute-start(bf16[512,512]{1,0:T(8,128)(2,1)S(1)} %get-tuple-element.20), channel_id=1, source_target_pairs={{0,16},{1,1},{2,18},{3,3},{4,32},{5,33},{6,51},{7,48},{8,64},{9,65... | collective-permute-start | bytes 1572872 | tf_op jit(solution)/shard_map/ppermute | solution.py:28
  (10 other events, 84.6 us)

commit v2 on v0

v2 whole, which is shorter than its diff:
```python
import functools

import jax
import jax.numpy as jnp
from jax import lax
from jax.experimental import pallas as pl
from jax.experimental.pallas import tpu as pltpu
from jax.sharding import Mesh
from jax.sharding import PartitionSpec as P

N = 4
AXES = ("z", "core", "x", "y")
OFFSETS = (1, 3, 2, 0)
F32 = jnp.float32
BF16 = jnp.bfloat16
VMEM = pl.BlockSpec(memory_space=pltpu.VMEM)
ANY = pl.BlockSpec(memory_space=pl.ANY)


def shift(z, j):
    return jnp.where(j < z, 1, 0)


def first_row(z, j, q):
    return (q + shift(z, j)) & 3


def row_of(z, k, j, q):
    u = first_row(z, j, q)
    return (u + (k ^ (u >> 1))) & 3


def mirrored_row(z, k, j, q):
    u = first_row(z, j, q)
    return jnp.where(z == j, (q + 2 + k) & 3, (u + 3 - (k ^ (u >> 1))) & 3)


def linear(z, k, x, y):
    return (((z % N) * 2 + k) * N + x % N) * N + y % N


def devices():
    return [(z, k, x, y) for z in range(N) for k in range(2) for x in range(N) for y in range(N)]


def send(value, where):
    pairs = [(linear(*device), where(*device)) for device in devices()]
    return lax.ppermute(value, AXES, [(source, linear(*to)) for source, to in pairs if to is not None])


def up(n):
    return lambda z, k, x, y: (z + n, k, x, y)


def other_core(value):
    return send(value, lambda z, k, x, y: (z, 1 - k, x, y))


def coordinates():
    return tuple(lax.axis_index(name) for name in AXES)


def call(kernel, outs, operands, after=(), specs=None, scratch=(), vmem=24):
    n = len(operands)

    def body(*refs):
        kernel(*refs[:n], *refs[n + len(after) :])

    return pl.pallas_call(
        body,
        out_shape=outs,
        in_specs=list(specs or [VMEM] * n) + [ANY] * len(after),
        out_specs=[VMEM] * len(outs),
        scratch_shapes=list(scratch),
        compiler_params=pltpu.CompilerParams(vmem_limit_bytes=vmem * 2**20),
        cost_estimate=pl.CostEstimate(flops=1, bytes_accessed=1, transcendentals=0),
    )(*operands, *after)


def array(*shape, dtype=BF16):
    return jax.ShapeDtypeStruct(shape, dtype)


def shares(mine, theirs, others, turns, diagonal, after=()):
    rows, lat = mine.shape
    H = rows // 2
    Q = H // N
    tall = Q + (Q // 2 if diagonal else 0)

    def kernel(mine_ref, theirs_ref, *refs):
        out_refs = refs[-N:]
        z, k, x, y = coordinates()

        def rows_of(block, part, parts):
            start = pl.multiple_of((block & 1) * H + part * (H // parts), H // parts)
            window = pl.ds(start, H // parts)
            return jnp.where((block >> 1) == k, mine_ref[window, :], theirs_ref[window, :])

        for t, turn in enumerate(turns):
            j = (z + turn) & 3
            for i, offset in enumerate(OFFSETS):
                q = (y + offset) & 3
                p = row_of(z, k, j, q)
                window = pl.ds(pl.multiple_of((q & 1) * H, H), H)
                right = jnp.where((q >> 1) == k, refs[2 * t][window, :], refs[2 * t + 1][window, :])
                left = []
                for offset in OFFSETS:
                    c = (x + offset) & 3
                    left.append(rows_of(p, c, N))
                    if diagonal:
                        left.append(rows_of((q + 2) & 3, k * N + c, 2 * N))
                result = lax.dot_general(
                    jnp.concatenate(left, 0), right, (((1,), (1,)), ((), ())), preferred_element_type=F32
                ).astype(BF16)
                here = slice(t * tall, (t + 1) * tall)

                @pl.when(k == 0)
                def _(result=result, i=i, here=here):
                    for m in range(N):
                        out_refs[m][i, here, :] = result[m * tall : (m + 1) * tall]

                @pl.when(k == 1)
                def _(result=result, i=i, here=here):
                    for m in range(N):
                        out_refs[i][m, here, :] = result[m * tall : (m + 1) * tall]

    n = len(turns)
    flat = [a for pair in others for a in pair]
    return call(kernel, [array(N, n * tall, H)] * N, [mine, theirs, *flat], after)


def multiply(inv_root, tiles, blocks, start, dtype, after=()):
    rows, lat = tiles[0].shape
    height = inv_root.shape[0]
    step = height // N

    def kernel(root_ref, *refs):
        tile_refs, refs = refs[: len(tiles)], refs[len(tiles) :]
        out_ref, held, sums, sems = refs[-4:]
        z, k, _, _ = coordinates()

        def copy(i):
            turn, whose = blocks[i]
            block = 2 * ((z + turn) & 3) + (k if whose == 0 else 1 - k)
            columns = pl.ds(pl.multiple_of(block * rows, rows), rows)
            return pltpu.make_async_copy(root_ref.at[:, columns], held.at[i], sems.at[i])

        copy(0).start()
        for i, tile_ref in enumerate(tile_refs):
            if i + 1 < len(tiles):
                copy(i + 1).start()
            copy(i).wait()
            for r in range(N):
                part = slice(r * step, (r + 1) * step)
                term = jnp.dot(held[i, part, :], tile_ref[...], preferred_element_type=F32)
                if i > 0:
                    term = term + sums[part, :]
                elif start is not None:
                    term = term + refs[0][part, :]
                if i + 1 < len(tiles):
                    sums[part, :] = term
                else:
                    out_ref[part, :] = term.astype(dtype)

    more = [] if start is None else [start]
    return call(
        kernel,
        [array(height, lat, dtype=dtype)],
        [inv_root, *tiles, *more],
        after,
        vmem=50,
        specs=[ANY] + [VMEM] * (len(tiles) + len(more)),
        scratch=[pltpu.VMEM((len(tiles), height, rows), BF16), pltpu.VMEM((height, lat), F32), pltpu.SemaphoreType.DMA((len(tiles),))],
    )[0]


def neighbours(above, below, after):
    def kernel(above_ref, below_ref, far_ref, both_ref):
        k = lax.axis_index("core")
        both_ref[0] = above_ref[...]
        both_ref[1] = below_ref[...]
        far_ref[...] = jnp.where(k == 0, below_ref[...], above_ref[...])

    return call(kernel, [array(*above.shape), array(2, *above.shape)], [above, below], after)


def scatter(parts, stage):
    def where(z, k, x, y, n):
        return (z, k, x + n, y) if k == stage else (z, k, x, y + n)

    return [send(parts[r], functools.partial(where, n=OFFSETS[r])) for r in range(N - 1)]


def total(got, own, after=()):
    def kernel(*refs):
        value = refs[N - 1][...].astype(F32)
        for ref in refs[: N - 1]:
            value = value + ref[...].astype(F32)
        value = value.astype(BF16)
        for r, ref in enumerate(refs[N:]):
            ref[...] = value[r] if own.ndim == 3 else value

    outs = [array(*own.shape[1:])] * N if own.ndim == 3 else [array(*own.shape)]
    return call(kernel, outs, [*got, own], after)


def hold(value, after):
    def kernel(value_ref, out_ref):
        out_ref[...] = value_ref[...]

    return call(kernel, [array(*value.shape)], [value], after)[0]


def step(k, n):
    return lambda z, core, x, y: (z, core, x + n, y) if core == k else (z, core, x, y + n)


def onward(parts):
    Q = parts[0].shape[1] // 2
    ahead = jnp.concatenate([parts[2][:, :Q], parts[0][:, Q:]], 1)
    back = jnp.concatenate([parts[1][:, :Q], parts[2][:, Q:]], 1)
    return send(ahead, step(0, 1)), send(back, step(0, -1))


def second_step(came, parts, after):
    Q = parts[0].shape[1] // 2

    def kernel(ahead_ref, back_ref, first_ref, second_ref, to_ref, fro_ref):
        to_ref[...] = (first_ref[:, :Q].astype(F32) + ahead_ref[:, :Q].astype(F32)).astype(BF16)
        fro_ref[...] = (second_ref[:, Q:].astype(F32) + back_ref[:, Q:].astype(F32)).astype(BF16)

    shape = (N, Q, parts[0].shape[2])
    to, fro = call(kernel, [array(*shape)] * 2, [*came, parts[0], parts[1]], after)
    return send(to, step(0, 1)), send(fro, step(0, -1))


def last_step(came, came_again, own, after):
    Q = own.shape[1] // 2

    def kernel(ahead_ref, back_ref, to_ref, fro_ref, own_ref, *out_refs):
        for r, ref in enumerate(out_refs):
            one = own_ref[r, :Q].astype(F32) + back_ref[r, :Q].astype(F32) + to_ref[r].astype(F32)
            two = own_ref[r, Q:].astype(F32) + ahead_ref[r, Q:].astype(F32) + fro_ref[r].astype(F32)
            ref[:Q, :] = one.astype(BF16)
            ref[Q:, :] = two.astype(BF16)

    return call(kernel, [array(*own.shape[1:])] * N, [*came, *came_again, own], after)


def mirror(turn):
    def where(z, k, x, y):
        j = (z + turn) % N
        u = (y + (j < z)) % N
        late = k ^ (u >> 1)
        p = (u + late) % N
        if turn == 0:
            return (z, 1, x, p) if late == 1 else None
        mirrored_u = (p + (z < j)) % N
        return (j, late ^ (mirrored_u >> 1), x, p)

    return where


def messages(near, middle, last, mirrored, other_half):
    Q = last.shape[0]
    H = last.shape[1]

    def kernel(near_ref, middle_ref, last_ref, m0_ref, m1_ref, m2_ref, m3_ref, half_ref, *out_refs):
        z, k, x, _ = coordinates()
        for d, out_ref in enumerate(out_refs):
            t = (x + d - z) & 3

            @pl.when(t == 0)
            def _(out_ref=out_ref):
                out_ref[:Q, :] = near_ref[:Q, :]
                out_ref[Q:, :] = jnp.where(k == 0, jnp.concatenate([near_ref[Q:, :], half_ref[...]], 0), m0_ref[...])

            for turn, (piece, mirrored_ref) in enumerate(
                ((middle_ref.at[:Q], m1_ref), (last_ref, m2_ref), (middle_ref.at[Q:], m3_ref)), 1
            ):

                @pl.when(t == turn)
                def _(out_ref=out_ref, piece=piece, mirrored_ref=mirrored_ref):
                    out_ref[:Q, :] = piece[...]
                    out_ref[Q:, :] = mirrored_ref[...]

    return call(kernel, [array(2 * Q, H)] * N, [near, middle, last, *mirrored, other_half])


def gathered(got):
    Q, H = got[0].shape[0] // 2, got[0].shape[1]

    def kernel(*refs):
        both_ref, wanted_ref = refs[N:]
        z, k, x, y = coordinates()
        for d in range(N):
            start = pl.multiple_of(((x - d) & 3) * Q, Q)
            for half in range(2):
                both_ref[half, pl.ds(start, Q), :] = refs[d][half * Q : (half + 1) * Q, :]
        stays = (row_of(z, k, x, y) >> 1) == k
        wanted_ref[...] = jnp.where(stays, both_ref[1], both_ref[0])

    return call(kernel, [array(2, H, H), array(H, H)], got)


def finish(both, arrived, stat_old):
    H = arrived.shape[0]
    E = H // 8

    def kernel(both_ref, arrived_ref, old_ref, out_ref):
        z, k, x, y = coordinates()

        def put(row, value):
            window = pl.ds(pl.multiple_of((row & 1) * H, H), H)
            out_ref[window, :] = 0.9 * old_ref[window, :] + 0.1 * value

        def turned(row, core, ref):
            whole = (z == x) & (core == 0)

            @pl.when(whole)
            def _():
                order = [2 * c + h for h in range(2) for c in range(N)]
                put(row, jnp.concatenate([ref[n * E : (n + 1) * E, :] for n in order], 0).astype(F32))

            @pl.when(jnp.logical_not(whole))
            def _():
                put(row, ref[...].astype(F32).T)

        plain, mirrored = row_of(z, k, x, y), mirrored_row(z, k, x, y)
        other_plain, other_mirrored = row_of(z, 1 - k, x, y), mirrored_row(z, 1 - k, x, y)

        @pl.when((plain >> 1) == k)
        def _():
            put(plain, both_ref[0].astype(F32))

        @pl.when((mirrored >> 1) == k)
        def _():
            turned(mirrored, k, both_ref.at[1])

        @pl.when((other_plain >> 1) == k)
        def _():
            put(other_plain, arrived_ref[...].astype(F32))

        @pl.when(((other_plain >> 1) != k) & ((other_mirrored >> 1) == k))
        def _():
            turned(other_mirrored, 1 - k, arrived_ref)

    return call(kernel, [array(2 * H, H, dtype=F32)], [both, arrived, stat_old])[0]


def on_device(gradient, stat_old, inv_root):
    Q = gradient.shape[0] // 8

    partner = other_core(gradient)
    above = send(gradient, up(-1))
    below = send(gradient, up(1))

    near = shares(gradient, partner, [(gradient, partner)], (0,), True)
    near_came = scatter(near, 0)
    product = multiply(inv_root, [gradient, partner], [(0, 0), (0, 1)], None, F32, [near[0]])

    far, both = neighbours(above, below, [product, *near_came])
    far = send(far, lambda z, k, x, y: (z + 1 - 2 * k, k, x, y))
    above_partner, below_partner = other_core(both)
    near = total(near_came, near[3], [both])
    near_came = scatter(near, 1)

    middle = shares(gradient, partner, [(above, above_partner), (below, below_partner)], (1, 3), False, [near[0]])
    middle_came = onward(middle)
    (near,) = total(near_came, near[3], [middle[0]])
    mirrored = [send(near[:Q], mirror(0)), None, None, None]
    other_half = send(near[Q:], lambda z, k, x, y: (z, 0, x, y) if k == 1 else None)

    far = hold(far, [near])
    far_partner = other_core(far)
    last = shares(gradient, partner, [(far, far_partner)], (2,), False)
    last_came = scatter(last, 0)
    product = multiply(
        inv_root, [above, above_partner, below, below_partner], [(1, 0), (1, 1), (3, 0), (3, 1)], product, F32, [last[0]]
    )
    middle_again = second_step(middle_came, middle, [product])
    product = multiply(inv_root, [far, far_partner], [(2, 0), (2, 1)], product, BF16, [last[0]])

    middle = last_step(middle_came, middle_again, middle[3], [product])
    middle_came = scatter(middle, 1)
    last = total(last_came, last[3], [middle[0], mirrored[0], other_half])
    last_came = scatter(last, 1)
    (middle,) = total(middle_came, middle[3], [last[0]])
    mirrored[3] = send(middle[:Q], mirror(1))
    mirrored[1] = send(middle[Q:], mirror(3))
    (last,) = total(last_came, last[3], [mirrored[1], mirrored[3]])
    mirrored[2] = send(last, mirror(2))

    out = messages(near, middle, last, mirrored, other_half)
    got = [out[0]] + [send(out[d], lambda z, k, x, y, d=d: (z, k, x + d, y)) for d in range(1, N)]
    both, wanted = gathered(got)
    return finish(both, other_core(wanted), stat_old), product


def solution(mesh):
    fine = Mesh(mesh.devices.reshape(N, 2, N, N), AXES)
    row, col = ("z", "core"), ("x", "y")
    return jax.shard_map(
        on_device,
        mesh=fine,
        in_specs=(P(row, col), P(row, col), P(row, None)),
        out_specs=(P(row, col), P(row, col)),
        check_vma=False,
    )
```

time: 202 us -> 147 us (0.73)
  waiting for transfers between devices: 148 us -> 54.1 us
  starting transfers between devices: 0.08 us -> 47.8 us
  Pallas kernels: 0 us -> 35.1 us
  matrix products: 31.6 us -> 0 us
  between operations: 14 us -> 0.93 us
    reduce_scatter x1 -> x0, waiting for transfers between devices: 92.4 us -> none  [on_device(): lax.psum_scatter(lax.dot_general(columns, gradient, (((1,), (1,)), ((), (...]
    all_gather x1 -> x0, waiting for transfers between devices: 55.4 us -> none  [on_device(): columns = lax.all_gather(gradient, 'row', axis=0, tiled=True)]
    ppermute x0 -> x34, waiting for transfers between devices: none -> 54.1 us  [send(): lax.ppermute(value, AXES, [(source, linear(*to)) for source, to in pairs...]
    ppermute x0 -> x34, starting transfers between devices: none -> 47.8 us  [send(): lax.ppermute(value, AXES, [(source, linear(*to)) for source, to in pairs...]
    pallas_call x0 -> x18, Pallas kernels: none -> 35.1 us  [call(): pl.pallas_call(body, out_shape=outs, in_specs=list(specs or [VMEM] * n) +...]
    dot_general x2 -> x0, matrix products: 31.6 us -> none  [the longest x1 16.1 us: on_device(): lax.dot_general(columns, gradient, (((1,), (1,)), ((), ())), preferred_el...]
    add x1 -> x0, other arithmetic: 2.93 us -> none  [on_device(): stat_new = 0.9 * stat_old + 0.1 * tile]
    concatenate x0 -> x2, other arithmetic: none -> 2.08 us  [the longest x1 1.04 us: onward(): back = jnp.concatenate([parts[1][:, :Q], parts[2][:, Q:]], 1)]
  transfers between devices with their start and end apart: 2 -> 34, of which waited for: 2 -> 17; matrix products, arithmetic and copies ran while one was open for 9% -> 2% of each run, Pallas kernels for 0% -> 22%
where the time goes in v2:
time: 147 us
  waiting for transfers between devices  54.1 us (37%)
  starting transfers between devices  47.8 us (33%)
  Pallas kernels  35.1 us (24%)
  local copies, waits for them, and re-layouts  6.79 us (5%)
  other arithmetic  2.08 us (1%)
    ppermute x34, waiting for transfers between devices, send(): lax.ppermute(value, AXES, [(source, linear(*to)) for source, to in pairs...  54.1 us
    ppermute x34, starting transfers between devices, send(): lax.ppermute(value, AXES, [(source, linear(*to)) for source, to in pairs...  47.8 us
    pallas_call x18, Pallas kernels, call(): pl.pallas_call(body, out_shape=outs, in_specs=list(specs or [VMEM] * n) +...  35.1 us
    unnamed x18, local copies, waits for them, and re-layouts  6.48 us
  transfers between devices with their start and end apart: 34, of which 17 were waited for; matrix products, arithmetic and copies ran while one was open for 2% of the time, Pallas kernels for 22%

profile of v2, /device:TPU:1, one launch (start us, length us, event | category | flops | bytes accessed | tf_op | source)
XLA Modules:
  0.0 146.8 jit_solution(2045262754952695748)
XLA Ops:
  2.1 3.9 %collective-permute-start.4 = (bf16[1024,512]{1,0:T(8,128)(2,1)}, bf16[1024,512]{1,0:T(8,128)(2,1)S(1)}, u32[]{:S(2)}, u32[]{:S(2)}) collective-permute-start(bf16[1024,512]{1,0:T(8,128)(2,1)} %refs_0_.9), channel_id=1, source_target_pairs={{0,96},{1,97},{2,98},{3,99},{4,100},{5,101},{6,102},{7,103},{8,104... | collective-permute-start | bytes 3145736 | tf_op jit(solution)/shard_map/ppermute | solution.py:48
  7.3 2.7 %shard_map.50 = (bf16[4,192,512]{2,1,0:T(8,128)(2,1)S(1)}, bf16[4,192,512]{2,1,0:T(8,128)(2,1)S(1)}, bf16[4,192,512]{2,1,0:T(8,128)(2,1)S(1)}, bf16[4,192,512]{2,1,0:T(8,128)(2,1)S(1)}) custom-call(bf16[1024,512]{1,0:T(8,128)(2,1)S(1)} %copy-done, bf16[1024,512]{1,0:T(8,128)(2,1)S(1)} %collective-permute-done.refs_1_.refs_3_.refs_2_, ...), custom_call_target="tpu_custom_call" | custom-call | flops 1 | bytes 1 | tf_op jit(solution)/shard_map/pallas_call | solution.py:69
  14.5 5.3 %shard_map.51.refs_2_.refs_5_ = f32[1024,512]{1,0:T(8,128)} custom-call(bf16[1024,8192]{1,0:T(8,128)(2,1)} %refs_0_.11, bf16[1024,512]{1,0:T(8,128)(2,1)S(1)} %copy-done.1, bf16[1024,512]{1,0:T(8,128)(2,1)S(1)} %collective-permute-done.refs_1_.refs_3_.refs_2_, bf16[4,192,512]{2,1,0:T(8,128)(2,1)S(1)} %get-tuple-element.36.refs_3_), custom_call_target="tpu_custom_call" | custom-call | flops 1 | bytes 1 | tf_op jit(solution)/shard_map/pallas_call | solution.py:69
  19.8 9.0 %collective-permute-done.4.refs_0_.refs_2_.refs_1_ = bf16[1024,512]{1,0:T(8,128)(2,1)S(1)} collective-permute-done((bf16[1024,512]{1,0:T(8,128)(2,1)}, bf16[1024,512]{1,0:T(8,128)(2,1)S(1)}, u32[]{:S(2)}, u32[]{:S(2)}) %collective-permute-start.4) | collective-permute-done | bytes 1048608 | tf_op jit(solution)/shard_map/ppermute | solution.py:48
  28.8 3.0 %collective-permute-done.5.refs_1_.refs_4_.refs_3_ = bf16[1024,512]{1,0:T(8,128)(2,1)S(1)} collective-permute-done((bf16[1024,512]{1,0:T(8,128)(2,1)}, bf16[1024,512]{1,0:T(8,128)(2,1)S(1)}, u32[]{:S(2)}, u32[]{:S(2)}) %collective-permute-start.5) | collective-permute-done | bytes 1048608 | tf_op jit(solution)/shard_map/ppermute | solution.py:48
  35.0 2.9 %collective-permute-start.12 = (bf16[1024,512]{1,0:T(8,128)(2,1)S(1)}, bf16[1024,512]{1,0:T(8,128)(2,1)S(1)}, u32[]{:S(2)}, u32[]{:S(2)}) collective-permute-start(bf16[1024,512]{1,0:T(8,128)(2,1)S(1)} %get-tuple-element.48), channel_id=1, source_target_pairs={{0,32},{1,33},{2,34},{3,35},{4,36},{5,37},{6,38},{7,39},{8,40},{9,... | collective-permute-start | bytes 3145736 | tf_op jit(solution)/shard_map/ppermute | solution.py:48
  41.7 4.2 %shard_map.54 = (bf16[4,256,512]{2,1,0:T(8,128)(2,1)S(1)}, bf16[4,256,512]{2,1,0:T(8,128)(2,1)S(1)}, bf16[4,256,512]{2,1,0:T(8,128)(2,1)S(1)}, bf16[4,256,512]{2,1,0:T(8,128)(2,1)S(1)}) custom-call(bf16[1024,512]{1,0:T(8,128)(2,1)S(1)} %copy-done.1, bf16[1024,512]{1,0:T(8,128)(2,1)S(1)} %collective-permute-done.refs_1_.refs_3_.refs_2_, ...), custom_call_target="tpu_custom_call" | custom-call | flops 1 | bytes 1 | tf_op jit(solution)/shard_map/pallas_call | solution.py:69
  47.2 2.4 %collective-permute-done.12.refs_0_ = bf16[1024,512]{1,0:T(8,128)(2,1)S(1)} collective-permute-done((bf16[1024,512]{1,0:T(8,128)(2,1)S(1)}, bf16[1024,512]{1,0:T(8,128)(2,1)S(1)}, u32[]{:S(2)}, u32[]{:S(2)}) %collective-permute-start.12) | collective-permute-done | bytes 1048608 | tf_op jit(solution)/shard_map/ppermute | solution.py:48
  52.6 2.7 %collective-permute-start.11 = (bf16[4,256,512]{2,1,0:T(8,128)(2,1)}, bf16[4,256,512]{2,1,0:T(8,128)(2,1)S(1)}, u32[]{:S(2)}, u32[]{:S(2)}) collective-permute-start(bf16[4,256,512]{2,1,0:T(8,128)(2,1)} %pad_maximum_fusion.1), channel_id=1, source_target_pairs={{0,12},{1,13},{2,14},{3,15},{4,0},{5,1},{6,2},{7,3},{8,4},{9,5},{1... | collective-permute-start | bytes 3145736 | tf_op jit(solution)/shard_map/ppermute | solution.py:48
  59.2 10.2 %shard_map.58.refs_4_.refs_3_ = f32[1024,512]{1,0:T(8,128)} custom-call(bf16[1024,8192]{1,0:T(8,128)(2,1)} %refs_0_.11, bf16[1024,512]{1,0:T(8,128)(2,1)S(1)} %collective-permute-done.4.refs_0_.refs_2_.refs_1_, bf16[1024,512]{1,0:T(8,128)(2,1)S(1)} %get-tuple-element.71.refs_3_.refs_2_, bf16[1024,512]{1,0:T(8,128)(2,1)S(1)} %collective-permute-done.5.refs_1_.refs_4_.refs_3_, ...), custom_call_target="tpu_custom_call" | custom-call | flops 1 | bytes 1 | tf_op jit(solution)/shard_map/pallas_call | solution.py:69
  69.5 2.2 %collective-permute-done.10.refs_0_ = bf16[4,256,512]{2,1,0:T(8,128)(2,1)S(1)} collective-permute-done((bf16[4,256,512]{2,1,0:T(8,128)(2,1)}, bf16[4,256,512]{2,1,0:T(8,128)(2,1)S(1)}, u32[]{:S(2)}, u32[]{:S(2)}) %collective-permute-start.10) | collective-permute-done | bytes 1048608 | tf_op jit(solution)/shard_map/ppermute | solution.py:48
  73.6 2.7 %collective-permute-start.15 = (bf16[4,128,512]{2,1,0:T(8,128)(2,1)S(1)}, bf16[4,128,512]{2,1,0:T(8,128)(2,1)S(1)}, u32[]{:S(2)}, u32[]{:S(2)}) collective-permute-start(bf16[4,128,512]{2,1,0:T(8,128)(2,1)S(1)} %get-tuple-element.51), channel_id=1, source_target_pairs={{0,12},{1,13},{2,14},{3,15},{4,0},{5,1},{6,2},{7,3},{8,4},{9,5},{1... | collective-permute-start | bytes 1572872 | tf_op jit(solution)/shard_map/ppermute | solution.py:48
  76.3 2.7 %collective-permute-start.20 = (bf16[4,128,512]{2,1,0:T(8,128)(2,1)S(1)}, bf16[4,128,512]{2,1,0:T(8,128)(2,1)S(1)}, u32[]{:S(2)}, u32[]{:S(2)}) collective-permute-start(bf16[4,128,512]{2,1,0:T(8,128)(2,1)S(1)} %copy-done.8), channel_id=1, source_target_pairs={{0,12},{1,13},{2,14},{3,15},{4,0},{5,1},{6,2},{7,3},{8,4},{9,5},{1... | collective-permute-start | bytes 1572872 | tf_op jit(solution)/shard_map/ppermute | solution.py:48
  79.0 4.2 %collective-permute-done.14.refs_2_ = bf16[4,128,512]{2,1,0:T(8,128)(2,1)S(1)} collective-permute-done((bf16[4,128,512]{2,1,0:T(8,128)(2,1)S(1)}, bf16[4,128,512]{2,1,0:T(8,128)(2,1)S(1)}, u32[]{:S(2)}, u32[]{:S(2)}) %collective-permute-start.14) | collective-permute-done | bytes 524320 | tf_op jit(solution)/shard_map/ppermute | solution.py:48
  85.1 2.3 %collective-permute-start.23 = (bf16[64,512]{1,0:T(8,128)(2,1)S(1)}, bf16[64,512]{1,0:T(8,128)(2,1)S(1)}, u32[]{:S(2)}, u32[]{:S(2)}) collective-permute-start(bf16[64,512]{1,0:T(8,128)(2,1)S(1)} %slice.33), channel_id=1, source_target_pairs={{16,0},{17,1},{18,2},{19,3},{20,4},{21,5},{22,6},{23,7},{24,8},{25... | collective-permute-start | bytes 196616 | tf_op jit(solution)/shard_map/ppermute | solution.py:48
  87.4 6.7 %shard_map.60.refs_5_ = bf16[1024,512]{1,0:T(8,128)(2,1)} custom-call(bf16[1024,8192]{1,0:T(8,128)(2,1)} %refs_0_.11, bf16[1024,512]{1,0:T(8,128)(2,1)S(1)} %shard_map.56.refs_2_.refs_1_, bf16[1024,512]{1,0:T(8,128)(2,1)S(1)} %collective-permute-done.13.refs_3_.refs_2_, f32[1024,512]{1,0:T(8,128)} %shard_map.58.refs_4_.refs_3_, ...), custom_call_target="tpu_custom_call" | custom-call | flops 1 | bytes 1 | tf_op jit(solution)/shard_map/pallas_call | solution.py:69
  95.8 2.7 %collective-permute-start.17 = (bf16[256,512]{1,0:T(8,128)(2,1)S(1)}, bf16[256,512]{1,0:T(8,128)(2,1)S(1)}, u32[]{:S(2)}, u32[]{:S(2)}) collective-permute-start(bf16[256,512]{1,0:T(8,128)(2,1)S(1)} %get-tuple-element.54), channel_id=1, source_target_pairs={{0,3},{1,0},{2,1},{3,2},{4,7},{5,4},{6,5},{7,6},{8,11},{9,8},{10,9... | collective-permute-start | bytes 786440 | tf_op jit(solution)/shard_map/ppermute | solution.py:48
  106.3 4.0 %collective-permute-start.27 = (bf16[128,512]{1,0:T(8,128)(2,1)S(1)}, bf16[128,512]{1,0:T(8,128)(2,1)S(1)}, u32[]{:S(2)}, u32[]{:S(2)}) collective-permute-start(bf16[128,512]{1,0:T(8,128)(2,1)S(1)} %get-tuple-element.75), channel_id=1, source_target_pairs={{0,96},{1,113},{2,115},{3,112},{4,100},{5,117},{6,119},{7,116},{8,... | collective-permute-start | bytes 393224 | tf_op jit(solution)/shard_map/ppermute | solution.py:48
  111.0 3.5 %collective-permute-done.27.refs_4_ = bf16[128,512]{1,0:T(8,128)(2,1)S(1)} collective-permute-done((bf16[128,512]{1,0:T(8,128)(2,1)S(1)}, bf16[128,512]{1,0:T(8,128)(2,1)S(1)}, u32[]{:S(2)}, u32[]{:S(2)}) %collective-permute-start.27) | collective-permute-done | bytes 131104 | tf_op jit(solution)/shard_map/ppermute | solution.py:48
  114.4 4.0 %collective-permute-done.28.refs_5_.refs_6_ = bf16[128,512]{1,0:T(8,128)(2,1)S(1)} collective-permute-done((bf16[128,512]{1,0:T(8,128)(2,1)S(1)}, bf16[128,512]{1,0:T(8,128)(2,1)S(1)}, u32[]{:S(2)}, u32[]{:S(2)}) %collective-permute-start.28) | collective-permute-done | bytes 131104 | tf_op jit(solution)/shard_map/ppermute | solution.py:48
  118.6 8.3 %collective-permute-done.29.refs_5_ = bf16[128,512]{1,0:T(8,128)(2,1)S(1)} collective-permute-done((bf16[128,512]{1,0:T(8,128)(2,1)S(1)}, bf16[128,512]{1,0:T(8,128)(2,1)S(1)}, u32[]{:S(2)}, u32[]{:S(2)}) %collective-permute-start.29) | collective-permute-done | bytes 131104 | tf_op jit(solution)/shard_map/ppermute | solution.py:48
  127.2 2.8 %collective-permute-start.31 = (bf16[256,512]{1,0:T(8,128)(2,1)S(1)}, bf16[256,512]{1,0:T(8,128)(2,1)S(1)}, u32[]{:S(2)}, u32[]{:S(2)}) collective-permute-start(bf16[256,512]{1,0:T(8,128)(2,1)S(1)} %get-tuple-element.66), channel_id=1, source_target_pairs={{0,8},{1,9},{2,10},{3,11},{4,12},{5,13},{6,14},{7,15},{8,0},{9,1},... | collective-permute-start | bytes 786440 | tf_op jit(solution)/shard_map/ppermute | solution.py:48
  129.9 4.2 %collective-permute-done.30.refs_1_ = bf16[256,512]{1,0:T(8,128)(2,1)S(1)} collective-permute-done((bf16[256,512]{1,0:T(8,128)(2,1)S(1)}, bf16[256,512]{1,0:T(8,128)(2,1)S(1)}, u32[]{:S(2)}, u32[]{:S(2)}) %collective-permute-start.30) | collective-permute-done | bytes 262176 | tf_op jit(solution)/shard_map/ppermute | solution.py:48
  134.1 5.7 %collective-permute-done.31.refs_2_ = bf16[256,512]{1,0:T(8,128)(2,1)S(1)} collective-permute-done((bf16[256,512]{1,0:T(8,128)(2,1)S(1)}, bf16[256,512]{1,0:T(8,128)(2,1)S(1)}, u32[]{:S(2)}, u32[]{:S(2)}) %collective-permute-start.31) | collective-permute-done | bytes 262176 | tf_op jit(solution)/shard_map/ppermute | solution.py:48
  (89 shorter events, 43.6 us)
Async XLA Ops:
  2.1 26.7 %collective-permute-start.4 = (bf16[1024,512]{1,0:T(8,128)(2,1)}, bf16[1024,512]{1,0:T(8,128)(2,1)S(1)}, u32[]{:S(2)}, u32[]{:S(2)}) collective-permute-start(bf16[1024,512]{1,0:T(8,128)(2,1)} %refs_0_.9), channel_id=1, source_target_pairs={{0,96},{1,97},{2,98},{3,99},{4,100},{5,101},{6,102},{7,103},{8,104... | collective-permute-start | bytes 3145736 | tf_op jit(solution)/shard_map/ppermute | solution.py:48
  6.0 25.8 %collective-permute-start.5 = (bf16[1024,512]{1,0:T(8,128)(2,1)}, bf16[1024,512]{1,0:T(8,128)(2,1)S(1)}, u32[]{:S(2)}, u32[]{:S(2)}) collective-permute-start(bf16[1024,512]{1,0:T(8,128)(2,1)} %refs_0_.9), channel_id=1, source_target_pairs={{0,32},{1,33},{2,34},{3,35},{4,36},{5,37},{6,38},{7,39},{8,40},{9,... | collective-permute-start | bytes 3145736 | tf_op jit(solution)/shard_map/ppermute | solution.py:48
  10.0 21.8 %collective-permute-start.1 = (bf16[4,192,512]{2,1,0:T(8,128)(2,1)S(1)}, bf16[4,192,512]{2,1,0:T(8,128)(2,1)S(1)}, u32[]{:S(2)}, u32[]{:S(2)}) collective-permute-start(bf16[4,192,512]{2,1,0:T(8,128)(2,1)S(1)} %get-tuple-element.36.refs_3_), channel_id=1, source_target_pairs={{0,4},{1,5},{2,6},{3,7},{4,8},{5,9},{6,10},{7,11},{8,12},{9,13},{1... | collective-permute-start | bytes 2359304 | tf_op jit(solution)/shard_map/ppermute | solution.py:48
  11.4 20.4 %collective-permute-start.2 = (bf16[4,192,512]{2,1,0:T(8,128)(2,1)S(1)}, bf16[4,192,512]{2,1,0:T(8,128)(2,1)S(1)}, u32[]{:S(2)}, u32[]{:S(2)}) collective-permute-start(bf16[4,192,512]{2,1,0:T(8,128)(2,1)S(1)} %get-tuple-element.37), channel_id=1, source_target_pairs={{0,12},{1,13},{2,14},{3,15},{4,0},{5,1},{6,2},{7,3},{8,4},{9,5},{1... | collective-permute-start | bytes 2359304 | tf_op jit(solution)/shard_map/ppermute | solution.py:48
  12.9 19.2 %collective-permute-start.3 = (bf16[4,192,512]{2,1,0:T(8,128)(2,1)S(1)}, bf16[4,192,512]{2,1,0:T(8,128)(2,1)S(1)}, u32[]{:S(2)}, u32[]{:S(2)}) collective-permute-start(bf16[4,192,512]{2,1,0:T(8,128)(2,1)S(1)} %get-tuple-element.38), channel_id=1, source_target_pairs={{0,8},{1,9},{2,10},{3,11},{4,12},{5,13},{6,14},{7,15},{8,0},{9,1},... | collective-permute-start | bytes 2359304 | tf_op jit(solution)/shard_map/ppermute | solution.py:48
  35.0 14.7 %collective-permute-start.12 = (bf16[1024,512]{1,0:T(8,128)(2,1)S(1)}, bf16[1024,512]{1,0:T(8,128)(2,1)S(1)}, u32[]{:S(2)}, u32[]{:S(2)}) collective-permute-start(bf16[1024,512]{1,0:T(8,128)(2,1)S(1)} %get-tuple-element.48), channel_id=1, source_target_pairs={{0,32},{1,33},{2,34},{3,35},{4,36},{5,37},{6,38},{7,39},{8,40},{9,... | collective-permute-start | bytes 3145736 | tf_op jit(solution)/shard_map/ppermute | solution.py:48
  52.6 16.9 %collective-permute-start.11 = (bf16[4,256,512]{2,1,0:T(8,128)(2,1)}, bf16[4,256,512]{2,1,0:T(8,128)(2,1)S(1)}, u32[]{:S(2)}, u32[]{:S(2)}) collective-permute-start(bf16[4,256,512]{2,1,0:T(8,128)(2,1)} %pad_maximum_fusion.1), channel_id=1, source_target_pairs={{0,12},{1,13},{2,14},{3,15},{4,0},{5,1},{6,2},{7,3},{8,4},{9,5},{1... | collective-permute-start | bytes 3145736 | tf_op jit(solution)/shard_map/ppermute | solution.py:48
  56.3 15.4 %collective-permute-start.10 = (bf16[4,256,512]{2,1,0:T(8,128)(2,1)}, bf16[4,256,512]{2,1,0:T(8,128)(2,1)S(1)}, u32[]{:S(2)}, u32[]{:S(2)}) collective-permute-start(bf16[4,256,512]{2,1,0:T(8,128)(2,1)} %pad_maximum_fusion), channel_id=1, source_target_pairs={{0,4},{1,5},{2,6},{3,7},{4,8},{5,9},{6,10},{7,11},{8,12},{9,13},{1... | collective-permute-start | bytes 3145736 | tf_op jit(solution)/shard_map/ppermute | solution.py:48
  73.5 9.6 %collective-permute-start.14 = (bf16[4,128,512]{2,1,0:T(8,128)(2,1)S(1)}, bf16[4,128,512]{2,1,0:T(8,128)(2,1)S(1)}, u32[]{:S(2)}, u32[]{:S(2)}) collective-permute-start(bf16[4,128,512]{2,1,0:T(8,128)(2,1)S(1)} %get-tuple-element.50), channel_id=1, source_target_pairs={{0,4},{1,5},{2,6},{3,7},{4,8},{5,9},{6,10},{7,11},{8,12},{9,13},{1... | collective-permute-start | bytes 1572872 | tf_op jit(solution)/shard_map/ppermute | solution.py:48
  73.6 11.5 %collective-permute-start.15 = (bf16[4,128,512]{2,1,0:T(8,128)(2,1)S(1)}, bf16[4,128,512]{2,1,0:T(8,128)(2,1)S(1)}, u32[]{:S(2)}, u32[]{:S(2)}) collective-permute-start(bf16[4,128,512]{2,1,0:T(8,128)(2,1)S(1)} %get-tuple-element.51), channel_id=1, source_target_pairs={{0,12},{1,13},{2,14},{3,15},{4,0},{5,1},{6,2},{7,3},{8,4},{9,5},{1... | collective-permute-start | bytes 1572872 | tf_op jit(solution)/shard_map/ppermute | solution.py:48
  76.3 22.2 %collective-permute-start.19 = (bf16[4,128,512]{2,1,0:T(8,128)(2,1)S(1)}, bf16[4,128,512]{2,1,0:T(8,128)(2,1)S(1)}, u32[]{:S(2)}, u32[]{:S(2)}) collective-permute-start(bf16[4,128,512]{2,1,0:T(8,128)(2,1)S(1)} %get-tuple-element.49.refs_6_.refs_4_), channel_id=1, source_target_pairs={{0,4},{1,5},{2,6},{3,7},{4,8},{5,9},{6,10},{7,11},{8,12},{9,13},{1... | collective-permute-start | bytes 1572872 | tf_op jit(solution)/shard_map/ppermute | solution.py:48
  76.3 23.1 %collective-permute-start.20 = (bf16[4,128,512]{2,1,0:T(8,128)(2,1)S(1)}, bf16[4,128,512]{2,1,0:T(8,128)(2,1)S(1)}, u32[]{:S(2)}, u32[]{:S(2)}) collective-permute-start(bf16[4,128,512]{2,1,0:T(8,128)(2,1)S(1)} %copy-done.8), channel_id=1, source_target_pairs={{0,12},{1,13},{2,14},{3,15},{4,0},{5,1},{6,2},{7,3},{8,4},{9,5},{1... | collective-permute-start | bytes 1572872 | tf_op jit(solution)/shard_map/ppermute | solution.py:48
  79.0 20.4 %collective-permute-start.21 = (bf16[4,128,512]{2,1,0:T(8,128)(2,1)S(1)}, bf16[4,128,512]{2,1,0:T(8,128)(2,1)S(1)}, u32[]{:S(2)}, u32[]{:S(2)}) collective-permute-start(bf16[4,128,512]{2,1,0:T(8,128)(2,1)S(1)} %get-tuple-element.58), channel_id=1, source_target_pairs={{0,8},{1,9},{2,10},{3,11},{4,12},{5,13},{6,14},{7,15},{8,0},{9,1},... | collective-permute-start | bytes 1572872 | tf_op jit(solution)/shard_map/ppermute | solution.py:48
  83.2 12.7 %collective-permute-start.22 = (bf16[128,512]{1,0:T(8,128)(2,1)S(1)}, bf16[128,512]{1,0:T(8,128)(2,1)S(1)}, u32[]{:S(2)}, u32[]{:S(2)}) collective-permute-start(bf16[128,512]{1,0:T(8,128)(2,1)S(1)} %slice.32), channel_id=1, source_target_pairs={{2,19},{3,16},{6,23},{7,20},{10,27},{11,24},{14,31},{15,28},{16,17... | collective-permute-start | bytes 393224 | tf_op jit(solution)/shard_map/ppermute | solution.py:48
  85.1 10.6 %collective-permute-start.23 = (bf16[64,512]{1,0:T(8,128)(2,1)S(1)}, bf16[64,512]{1,0:T(8,128)(2,1)S(1)}, u32[]{:S(2)}, u32[]{:S(2)}) collective-permute-start(bf16[64,512]{1,0:T(8,128)(2,1)S(1)} %slice.33), channel_id=1, source_target_pairs={{16,0},{17,1},{18,2},{19,3},{20,4},{21,5},{22,6},{23,7},{24,8},{25... | collective-permute-start | bytes 196616 | tf_op jit(solution)/shard_map/ppermute | solution.py:48
  95.8 8.8 %collective-permute-start.17 = (bf16[256,512]{1,0:T(8,128)(2,1)S(1)}, bf16[256,512]{1,0:T(8,128)(2,1)S(1)}, u32[]{:S(2)}, u32[]{:S(2)}) collective-permute-start(bf16[256,512]{1,0:T(8,128)(2,1)S(1)} %get-tuple-element.54), channel_id=1, source_target_pairs={{0,3},{1,0},{2,1},{3,2},{4,7},{5,4},{6,5},{7,6},{8,11},{9,8},{10,9... | collective-permute-start | bytes 786440 | tf_op jit(solution)/shard_map/ppermute | solution.py:48
  99.6 11.3 %collective-permute-start.24 = (bf16[128,512]{1,0:T(8,128)(2,1)S(1)}, bf16[128,512]{1,0:T(8,128)(2,1)S(1)}, u32[]{:S(2)}, u32[]{:S(2)}) collective-permute-start(bf16[128,512]{1,0:T(8,128)(2,1)S(1)} %get-tuple-element.60.refs_4_), channel_id=1, source_target_pairs={{0,1},{1,2},{2,3},{3,0},{4,5},{5,6},{6,7},{7,4},{8,9},{9,10},{10,1... | collective-permute-start | bytes 393224 | tf_op jit(solution)/shard_map/ppermute | solution.py:48
  100.5 10.5 %collective-permute-start.25 = (bf16[128,512]{1,0:T(8,128)(2,1)S(1)}, bf16[128,512]{1,0:T(8,128)(2,1)S(1)}, u32[]{:S(2)}, u32[]{:S(2)}) collective-permute-start(bf16[128,512]{1,0:T(8,128)(2,1)S(1)} %get-tuple-element.61), channel_id=1, source_target_pairs={{0,3},{1,0},{2,1},{3,2},{4,7},{5,4},{6,5},{7,6},{8,11},{9,8},{10,9... | collective-permute-start | bytes 393224 | tf_op jit(solution)/shard_map/ppermute | solution.py:48
  102.5 8.4 %collective-permute-start.26 = (bf16[128,512]{1,0:T(8,128)(2,1)S(1)}, bf16[128,512]{1,0:T(8,128)(2,1)S(1)}, u32[]{:S(2)}, u32[]{:S(2)}) collective-permute-start(bf16[128,512]{1,0:T(8,128)(2,1)S(1)} %get-tuple-element.62), channel_id=1, source_target_pairs={{0,2},{1,3},{2,0},{3,1},{4,6},{5,7},{6,4},{7,5},{8,10},{9,11},{10,... | collective-permute-start | bytes 393224 | tf_op jit(solution)/shard_map/ppermute | solution.py:48
  106.3 8.1 %collective-permute-start.27 = (bf16[128,512]{1,0:T(8,128)(2,1)S(1)}, bf16[128,512]{1,0:T(8,128)(2,1)S(1)}, u32[]{:S(2)}, u32[]{:S(2)}) collective-permute-start(bf16[128,512]{1,0:T(8,128)(2,1)S(1)} %get-tuple-element.75), channel_id=1, source_target_pairs={{0,96},{1,113},{2,115},{3,112},{4,100},{5,117},{6,119},{7,116},{8,... | collective-permute-start | bytes 393224 | tf_op jit(solution)/shard_map/ppermute | solution.py:48
  110.3 8.1 %collective-permute-start.28 = (bf16[128,512]{1,0:T(8,128)(2,1)S(1)}, bf16[128,512]{1,0:T(8,128)(2,1)S(1)}, u32[]{:S(2)}, u32[]{:S(2)}) collective-permute-start(bf16[128,512]{1,0:T(8,128)(2,1)S(1)} %get-tuple-element.74), channel_id=1, source_target_pairs={{0,32},{1,49},{2,51},{3,48},{4,36},{5,53},{6,55},{7,52},{8,40},{9,... | collective-permute-start | bytes 393224 | tf_op jit(solution)/shard_map/ppermute | solution.py:48
  118.5 8.4 %collective-permute-start.29 = (bf16[128,512]{1,0:T(8,128)(2,1)S(1)}, bf16[128,512]{1,0:T(8,128)(2,1)S(1)}, u32[]{:S(2)}, u32[]{:S(2)}) collective-permute-start(bf16[128,512]{1,0:T(8,128)(2,1)S(1)} %shard_map.64.refs_2_), channel_id=1, source_target_pairs={{0,64},{1,81},{2,83},{3,80},{4,68},{5,85},{6,87},{7,84},{8,72},{9,... | collective-permute-start | bytes 393224 | tf_op jit(solution)/shard_map/ppermute | solution.py:48
  127.2 12.7 %collective-permute-start.31 = (bf16[256,512]{1,0:T(8,128)(2,1)S(1)}, bf16[256,512]{1,0:T(8,128)(2,1)S(1)}, u32[]{:S(2)}, u32[]{:S(2)}) collective-permute-start(bf16[256,512]{1,0:T(8,128)(2,1)S(1)} %get-tuple-element.66), channel_id=1, source_target_pairs={{0,8},{1,9},{2,10},{3,11},{4,12},{5,13},{6,14},{7,15},{8,0},{9,1},... | collective-permute-start | bytes 786440 | tf_op jit(solution)/shard_map/ppermute | solution.py:48
  129.9 11.5 %collective-permute-start.32 = (bf16[256,512]{1,0:T(8,128)(2,1)S(1)}, bf16[256,512]{1,0:T(8,128)(2,1)S(1)}, u32[]{:S(2)}, u32[]{:S(2)}) collective-permute-start(bf16[256,512]{1,0:T(8,128)(2,1)S(1)} %get-tuple-element.67), channel_id=1, source_target_pairs={{0,12},{1,13},{2,14},{3,15},{4,0},{5,1},{6,2},{7,3},{8,4},{9,5},{1... | collective-permute-start | bytes 786440 | tf_op jit(solution)/shard_map/ppermute | solution.py:48
  (19 other events, 138.4 us)

commit v3 on v2

--- a/solution.py
+++ b/solution.py
@@ -81,14 +81,14 @@
     return jax.ShapeDtypeStruct(shape, dtype)
 
 
-def shares(mine, theirs, others, turns, diagonal, after=()):
+def shares(mine, theirs, others, turns, diagonal, places, after=()):
     rows, lat = mine.shape
     H = rows // 2
     Q = H // N
     tall = Q + (Q // 2 if diagonal else 0)
 
     def kernel(mine_ref, theirs_ref, *refs):
-        out_refs = refs[-N:]
+        out_refs = refs[2 * len(turns) :]
         z, k, x, y = coordinates()
 
         def rows_of(block, part, parts):
@@ -112,21 +112,26 @@
                 result = lax.dot_general(
                     jnp.concatenate(left, 0), right, (((1,), (1,)), ((), ())), preferred_element_type=F32
                 ).astype(BF16)
-                here = slice(t * tall, (t + 1) * tall)
-
                 @pl.when(k == 0)
-                def _(result=result, i=i, here=here):
+                def _(result=result, i=i, t=t):
                     for m in range(N):
-                        out_refs[m][i, here, :] = result[m * tall : (m + 1) * tall]
+                        for out, to, start, size in places[m][t]:
+                            rows_sent = slice(m * tall + start, m * tall + start + size)
+                            out_refs[out][i, to : to + size, :] = result[rows_sent]
 
                 @pl.when(k == 1)
-                def _(result=result, i=i, here=here):
+                def _(result=result, i=i, t=t):
                     for m in range(N):
-                        out_refs[i][m, here, :] = result[m * tall : (m + 1) * tall]
-
-    n = len(turns)
+                        for out, to, start, size in places[i][t]:
+                            rows_sent = slice(m * tall + start, m * tall + start + size)
+                            out_refs[out][m, to : to + size, :] = result[rows_sent]
+
     flat = [a for pair in others for a in pair]
-    return call(kernel, [array(N, n * tall, H)] * N, [mine, theirs, *flat], after)
+    heights = {}
+    for spots in places:
+        for out, to, _, size in (piece for pieces in spots for piece in pieces):
+            heights[out] = max(heights.get(out, 0), to + size)
+    return call(kernel, [array(N, heights[out], H) for out in sorted(heights)], [mine, theirs, *flat], after)
 
 
 def multiply(inv_root, tiles, blocks, start, dtype, after=()):
@@ -136,7 +141,8 @@
 
     def kernel(root_ref, *refs):
         tile_refs, refs = refs[: len(tiles)], refs[len(tiles) :]
-        out_ref, held, sums, sems = refs[-4:]
+        out_ref, token_ref, held, sums, sems = refs[-5:]
+        token_ref[...] = jnp.zeros_like(token_ref)
         z, k, _, _ = coordinates()
 
         def copy(i):
@@ -165,13 +171,13 @@
     more = [] if start is None else [start]
     return call(
         kernel,
-        [array(height, lat, dtype=dtype)],
+        [array(height, lat, dtype=dtype), array(8, 128, dtype=F32)],
         [inv_root, *tiles, *more],
         after,
         vmem=50,
         specs=[ANY] + [VMEM] * (len(tiles) + len(more)),
         scratch=[pltpu.VMEM((len(tiles), height, rows), BF16), pltpu.VMEM((height, lat), F32), pltpu.SemaphoreType.DMA((len(tiles),))],
-    )[0]
+    )
 
 
 def neighbours(above, below, after):
@@ -215,36 +221,39 @@
     return lambda z, core, x, y: (z, core, x + n, y) if core == k else (z, core, x, y + n)
 
 
-def onward(parts):
-    Q = parts[0].shape[1] // 2
-    ahead = jnp.concatenate([parts[2][:, :Q], parts[0][:, Q:]], 1)
-    back = jnp.concatenate([parts[1][:, :Q], parts[2][:, Q:]], 1)
-    return send(ahead, step(0, 1)), send(back, step(0, -1))
-
-
-def second_step(came, parts, after):
-    Q = parts[0].shape[1] // 2
-
-    def kernel(ahead_ref, back_ref, first_ref, second_ref, to_ref, fro_ref):
-        to_ref[...] = (first_ref[:, :Q].astype(F32) + ahead_ref[:, :Q].astype(F32)).astype(BF16)
-        fro_ref[...] = (second_ref[:, Q:].astype(F32) + back_ref[:, Q:].astype(F32)).astype(BF16)
-
-    shape = (N, Q, parts[0].shape[2])
-    to, fro = call(kernel, [array(*shape)] * 2, [*came, parts[0], parts[1]], after)
+def second_step(came, first, second, far_came, far_first, far_second, after):
+    Q, h = first.shape[1], far_first.shape[1]
+
+    def kernel(ahead_ref, back_ref, first_ref, second_ref, ahead2_ref, back2_ref, first2_ref, second2_ref, to_ref, fro_ref):
+        to_ref[:, :Q] = (first_ref[...].astype(F32) + ahead_ref[:, :Q].astype(F32)).astype(BF16)
+        fro_ref[:, :Q] = (second_ref[...].astype(F32) + back_ref[:, Q:].astype(F32)).astype(BF16)
+        to_ref[:, Q:] = (first2_ref[...].astype(F32) + ahead2_ref[:, :h].astype(F32)).astype(BF16)
+        fro_ref[:, Q:] = (second2_ref[...].astype(F32) + back2_ref[:, h:].astype(F32)).astype(BF16)
+
+    shape = array(first.shape[0], Q + h, first.shape[2])
+    to, fro = call(kernel, [shape] * 2, [*came, first, second, *far_came, far_first, far_second], after)
     return send(to, step(0, 1)), send(fro, step(0, -1))
 
 
-def last_step(came, came_again, own, after):
-    Q = own.shape[1] // 2
-
-    def kernel(ahead_ref, back_ref, to_ref, fro_ref, own_ref, *out_refs):
+def last_step(came, own, far_came, far_own, came_again, after):
+    Q = far_own.shape[1]
+    h = Q // 2
+
+    def kernel(ahead_ref, back_ref, own_ref, ahead2_ref, back2_ref, own2_ref, to_ref, fro_ref, *out_refs):
+        def put(ref, at, *terms):
+            value = terms[0].astype(F32)
+            for term in terms[1:]:
+                value = value + term.astype(F32)
+            ref[at : at + terms[0].shape[0], :] = value.astype(BF16)
+
         for r, ref in enumerate(out_refs):
-            one = own_ref[r, :Q].astype(F32) + back_ref[r, :Q].astype(F32) + to_ref[r].astype(F32)
-            two = own_ref[r, Q:].astype(F32) + ahead_ref[r, Q:].astype(F32) + fro_ref[r].astype(F32)
-            ref[:Q, :] = one.astype(BF16)
-            ref[Q:, :] = two.astype(BF16)
-
-    return call(kernel, [array(*own.shape[1:])] * N, [*came, *came_again, own], after)
+            put(ref, 0, own_ref[r, :Q], back_ref[r, :Q], to_ref[r, :Q])
+            put(ref, Q, own_ref[r, Q:], ahead_ref[r, Q:], fro_ref[r, :Q])
+            put(ref, 2 * Q, own2_ref[r, :h], back2_ref[r, :h], to_ref[r, Q:])
+            put(ref, 2 * Q + h, own2_ref[r, h:], ahead2_ref[r, h:], fro_ref[r, Q:])
+
+    outs = [array(3 * Q, own.shape[2])] * N
+    return call(kernel, outs, [*came, own, *far_came, far_own, *came_again], after)
 
 
 def mirror(turn):
@@ -287,7 +296,7 @@
     return call(kernel, [array(2 * Q, H)] * N, [near, middle, last, *mirrored, other_half])
 
 
-def gathered(got):
+def gathered(got, after):
     Q, H = got[0].shape[0] // 2, got[0].shape[1]
 
     def kernel(*refs):
@@ -300,7 +309,7 @@
         stays = (row_of(z, k, x, y) >> 1) == k
         wanted_ref[...] = jnp.where(stays, both_ref[1], both_ref[0])
 
-    return call(kernel, [array(2, H, H), array(H, H)], got)
+    return call(kernel, [array(2, H, H), array(H, H)], got, after)
 
 
 def finish(both, arrived, stat_old):
@@ -355,45 +364,68 @@
     above = send(gradient, up(-1))
     below = send(gradient, up(1))
 
-    near = shares(gradient, partner, [(gradient, partner)], (0,), True)
+    tall = Q + Q // 2
+    straight = [[[(r, 0, 0, tall)]] for r in range(N)]
+    h = Q // 2
+    halved = [
+        [[(2, 0, 0, h), (0, h, h, h)]],
+        [[(1, 0, 0, h), (3, 0, h, h)]],
+        [[(0, 0, 0, h), (1, h, h, h)]],
+        [[(4, 0, 0, Q)]],
+    ]
+    by_plane = [
+        [[(2, 0, 0, Q)], [(0, Q, 0, Q)]],
+        [[(1, 0, 0, Q)], [(3, 0, 0, Q)]],
+        [[(0, 0, 0, Q)], [(1, Q, 0, Q)]],
+        [[(4, 0, 0, Q)], [(4, Q, 0, Q)]],
+    ]
+    near = shares(gradient, partner, [(gradient, partner)], (0,), True, straight)
     near_came = scatter(near, 0)
-    product = multiply(inv_root, [gradient, partner], [(0, 0), (0, 1)], None, F32, [near[0]])
-
-    far, both = neighbours(above, below, [product, *near_came])
+    product, token = multiply(inv_root, [gradient, partner], [(0, 0), (0, 1)], None, F32, [near[0]])
+
+    far, both = neighbours(above, below, [token, *near_came])
     far = send(far, lambda z, k, x, y: (z + 1 - 2 * k, k, x, y))
     above_partner, below_partner = other_core(both)
     near = total(near_came, near[3], [both])
     near_came = scatter(near, 1)
 
-    middle = shares(gradient, partner, [(above, above_partner), (below, below_partner)], (1, 3), False, [near[0]])
-    middle_came = onward(middle)
-    (near,) = total(near_came, near[3], [middle[0]])
-    mirrored = [send(near[:Q], mirror(0)), None, None, None]
+    ahead, back, first, second, own = shares(
+        gradient,
+        partner,
+        [(above, above_partner), (below, below_partner)],
+        (1, 3),
+        False,
+        by_plane,
+        [near[0]],
+    )
+    came = send(ahead, step(0, 1)), send(back, step(0, -1))
+    (near,) = total(near_came, near[3], [ahead])
+
     other_half = send(near[Q:], lambda z, k, x, y: (z, 0, x, y) if k == 1 else None)
-
     far = hold(far, [near])
     far_partner = other_core(far)
-    last = shares(gradient, partner, [(far, far_partner)], (2,), False)
-    last_came = scatter(last, 0)
-    product = multiply(
-        inv_root, [above, above_partner, below, below_partner], [(1, 0), (1, 1), (3, 0), (3, 1)], product, F32, [last[0]]
+    ahead, back, far_first, far_second, far_own = shares(
+        gradient, partner, [(far, far_partner)], (2,), False, halved, [ahead]
     )
-    middle_again = second_step(middle_came, middle, [product])
-    product = multiply(inv_root, [far, far_partner], [(2, 0), (2, 1)], product, BF16, [last[0]])
-
-    middle = last_step(middle_came, middle_again, middle[3], [product])
-    middle_came = scatter(middle, 1)
-    last = total(last_came, last[3], [middle[0], mirrored[0], other_half])
-    last_came = scatter(last, 1)
-    (middle,) = total(middle_came, middle[3], [last[0]])
-    mirrored[3] = send(middle[:Q], mirror(1))
-    mirrored[1] = send(middle[Q:], mirror(3))
-    (last,) = total(last_came, last[3], [mirrored[1], mirrored[3]])
-    mirrored[2] = send(last, mirror(2))
-
-    out = messages(near, middle, last, mirrored, other_half)
+    far_came = send(ahead, step(0, 1)), send(back, step(0, -1))
+    product, token = multiply(inv_root, [far, far_partner], [(2, 0), (2, 1)], product, F32, [ahead, other_half])
+    came_again = second_step(came, first, second, far_came, far_first, far_second, [token])
+    mirrored = [send(near[:Q], mirror(0))]
+    product, token = multiply(
+        inv_root, [above, above_partner], [(1, 0), (1, 1)], product, F32, [*came, *far_came, token]
+    )
+    rest = last_step(came, own, far_came, far_own, came_again, [token, mirrored[0]])
+    (rest,) = total(scatter(rest, 1), rest[3])
+
+    mirrored += [
+        send(rest[Q : 2 * Q], mirror(3)),
+        send(rest[2 * Q :], mirror(2)),
+        send(rest[:Q], mirror(1)),
+    ]
+    out = messages(near, rest[: 2 * Q], rest[2 * Q :], mirrored, other_half)
     got = [out[0]] + [send(out[d], lambda z, k, x, y, d=d: (z, k, x + d, y)) for d in range(1, N)]
-    both, wanted = gathered(got)
+    product, token = multiply(inv_root, [below, below_partner], [(3, 0), (3, 1)], product, BF16, [out[0]])
+    both, wanted = gathered(got, [token])
     return finish(both, other_core(wanted), stat_old), product
 
 

time: 147 us -> 135 us (0.918)
  waiting for transfers between devices: 54.1 us -> 38.2 us
  Pallas kernels: 35.1 us -> 42 us
  local copies, waits for them, and re-layouts: 6.79 us -> 4.47 us
  other arithmetic: 2.08 us -> 0 us
  starting transfers between devices: 47.8 us -> 49.6 us
    ppermute x34 -> x30, waiting for transfers between devices: 54.1 us -> 38.2 us  [send(): lax.ppermute(value, AXES, [(source, linear(*to)) for source, to in pairs...]
    pallas_call x18 -> x17, Pallas kernels: 35.1 us -> 42 us  [call(): pl.pallas_call(body, out_shape=outs, in_specs=list(specs or [VMEM] * n) +...]
    unnamed x18 -> x26, local copies, waits for them, and re-layouts: 6.48 us -> 4.27 us
    concatenate x2 -> x0, other arithmetic: 2.08 us -> none  [the longest x1 1.04 us: onward(): back = jnp.concatenate([parts[1][:, :Q], parts[2][:, Q:]], 1)]
    ppermute x34 -> x30, starting transfers between devices: 47.8 us -> 49.6 us  [send(): lax.ppermute(value, AXES, [(source, linear(*to)) for source, to in pairs...]
  transfers between devices with their start and end apart: 34 -> 30, of which waited for: 17 -> 16; matrix products, arithmetic and copies ran while one was open for 2% -> 0% of each run, Pallas kernels for 22% -> 28%
where the time goes in v3:
time: 135 us
  starting transfers between devices  49.6 us (37%)
  Pallas kernels  42 us (31%)
  waiting for transfers between devices  38.2 us (28%)
  local copies, waits for them, and re-layouts  4.47 us (3%)
    ppermute x30, starting transfers between devices, send(): lax.ppermute(value, AXES, [(source, linear(*to)) for source, to in pairs...  49.6 us
    pallas_call x17, Pallas kernels, call(): pl.pallas_call(body, out_shape=outs, in_specs=list(specs or [VMEM] * n) +...  42 us
    ppermute x30, waiting for transfers between devices, send(): lax.ppermute(value, AXES, [(source, linear(*to)) for source, to in pairs...  38.2 us
    unnamed x26, local copies, waits for them, and re-layouts  4.27 us
  transfers between devices with their start and end apart: 30, of which 16 were waited for; matrix products, arithmetic and copies ran while one was open for 0% of the time, Pallas kernels for 28%

profile of v3, /device:TPU:1, one launch (start us, length us, event | category | flops | bytes accessed | tf_op | source)
XLA Modules:
  0.0 135.2 jit_solution(11836177218466245250)
XLA Ops:
  2.1 3.9 %collective-permute-start.4 = (bf16[1024,512]{1,0:T(8,128)(2,1)}, bf16[1024,512]{1,0:T(8,128)(2,1)S(1)}, u32[]{:S(2)}, u32[]{:S(2)}) collective-permute-start(bf16[1024,512]{1,0:T(8,128)(2,1)} %refs_0_.10), channel_id=1, source_target_pairs={{0,96},{1,97},{2,98},{3,99},{4,100},{5,101},{6,102},{7,103},{8,104... | collective-permute-start | bytes 3145736 | tf_op jit(solution)/shard_map/ppermute | solution.py:48
  7.3 2.8 %shard_map.50 = (bf16[4,192,512]{2,1,0:T(8,128)(2,1)S(1)}, bf16[4,192,512]{2,1,0:T(8,128)(2,1)S(1)}, bf16[4,192,512]{2,1,0:T(8,128)(2,1)S(1)}, bf16[4,192,512]{2,1,0:T(8,128)(2,1)S(1)}) custom-call(bf16[1024,512]{1,0:T(8,128)(2,1)S(1)} %copy-done, bf16[1024,512]{1,0:T(8,128)(2,1)S(1)} %collective-permute-done.refs_1_.refs_3_.refs_2_, ...), custom_call_target="tpu_custom_call" | custom-call | flops 1 | bytes 1 | tf_op jit(solution)/shard_map/pallas_call | solution.py:69
  14.5 5.3 %shard_map.51 = (f32[1024,512]{1,0:T(8,128)}, f32[8,128]{1,0:T(8,128)S(1)}) custom-call(bf16[1024,8192]{1,0:T(8,128)(2,1)} %refs_0_.13, bf16[1024,512]{1,0:T(8,128)(2,1)S(1)} %copy-done.1, bf16[1024,512]{1,0:T(8,128)(2,1)S(1)} %collective-permute-done.refs_1_.refs_3_.refs_2_, bf16[4,192,512]{2,1,0:T(8,128)(2,1)S(1)} %get-tuple-element.42.refs_3_), custom_call_target="tpu_custom_call" | custom-call | flops 1 | bytes 1 | tf_op jit(solution)/shard_map/pallas_call | solution.py:69
  19.8 9.0 %collective-permute-done.4.refs_0_.refs_2_.refs_1_ = bf16[1024,512]{1,0:T(8,128)(2,1)S(1)} collective-permute-done((bf16[1024,512]{1,0:T(8,128)(2,1)}, bf16[1024,512]{1,0:T(8,128)(2,1)S(1)}, u32[]{:S(2)}, u32[]{:S(2)}) %collective-permute-start.4) | collective-permute-done | bytes 1048608 | tf_op jit(solution)/shard_map/ppermute | solution.py:48
  28.8 3.0 %collective-permute-done.5.refs_1_.refs_4_ = bf16[1024,512]{1,0:T(8,128)(2,1)S(1)} collective-permute-done((bf16[1024,512]{1,0:T(8,128)(2,1)}, bf16[1024,512]{1,0:T(8,128)(2,1)S(1)}, u32[]{:S(2)}, u32[]{:S(2)}) %collective-permute-start.5) | collective-permute-done | bytes 1048608 | tf_op jit(solution)/shard_map/ppermute | solution.py:48
  33.4 2.9 %collective-permute-start.12 = (bf16[1024,512]{1,0:T(8,128)(2,1)S(1)}, bf16[1024,512]{1,0:T(8,128)(2,1)S(1)}, u32[]{:S(2)}, u32[]{:S(2)}) collective-permute-start(bf16[1024,512]{1,0:T(8,128)(2,1)S(1)} %get-tuple-element.55), channel_id=1, source_target_pairs={{0,32},{1,33},{2,34},{3,35},{4,36},{5,37},{6,38},{7,39},{8,40},{9,... | collective-permute-start | bytes 3145736 | tf_op jit(solution)/shard_map/ppermute | solution.py:48
  40.1 5.2 %shard_map.54 = (bf16[4,256,512]{2,1,0:T(8,128)(2,1)S(1)}, bf16[4,256,512]{2,1,0:T(8,128)(2,1)}, bf16[4,128,512]{2,1,0:T(8,128)(2,1)S(1)}, bf16[4,128,512]{2,1,0:T(8,128)(2,1)S(1)}, bf16[4,256,512]{2,1,0:T(8,128)(2,1)S(1)}) custom-call(bf16[1024,512]{1,0:T(8,128)(2,1)S(1)} %copy-done.1, bf16[1024,512]{1,0:T(8,128)(2,1)S(1)} %collective-permute-done.refs_1_.refs_3_.refs_2_, ...), custom_call_target="tpu_custom_call" | custom-call | flops 1 | bytes 1 | tf_op jit(solution)/shard_map/pallas_call | solution.py:69
  46.3 1.8 %collective-permute-done.12.refs_0_ = bf16[1024,512]{1,0:T(8,128)(2,1)S(1)} collective-permute-done((bf16[1024,512]{1,0:T(8,128)(2,1)S(1)}, bf16[1024,512]{1,0:T(8,128)(2,1)S(1)}, u32[]{:S(2)}, u32[]{:S(2)}) %collective-permute-start.12) | collective-permute-done | bytes 1048608 | tf_op jit(solution)/shard_map/ppermute | solution.py:48
  52.6 3.1 %shard_map.57 = (bf16[4,128,512]{2,1,0:T(8,128)(2,1)}, bf16[4,128,512]{2,1,0:T(8,128)(2,1)}, bf16[4,64,512]{2,1,0:T(8,128)(2,1)S(1)}, bf16[4,64,512]{2,1,0:T(8,128)(2,1)S(1)}, bf16[4,128,512]{2,1,0:T(8,128)(2,1)S(1)}) custom-call(bf16[1024,512]{1,0:T(8,128)(2,1)S(1)} %copy-done.1, bf16[1024,512]{1,0:T(8,128)(2,1)S(1)} %collective-permute-done.refs_1_.refs_3_.refs_2_, ...), custom_call_target="tpu_custom_call" | custom-call | flops 1 | bytes 1 | tf_op jit(solution)/shard_map/pallas_call | solution.py:69
  57.9 1.8 %collective-permute-start.15 = (bf16[4,128,512]{2,1,0:T(8,128)(2,1)}, bf16[4,128,512]{2,1,0:T(8,128)(2,1)S(1)}, u32[]{:S(2)}, u32[]{:S(2)}) collective-permute-start(bf16[4,128,512]{2,1,0:T(8,128)(2,1)} %get-tuple-element.57), channel_id=1, source_target_pairs={{0,12},{1,13},{2,14},{3,15},{4,0},{5,1},{6,2},{7,3},{8,4},{9,5},{1... | collective-permute-start | bytes 1572872 | tf_op jit(solution)/shard_map/ppermute | solution.py:48
  59.8 3.0 %collective-permute-start.16 = (bf16[64,512]{1,0:T(8,128)(2,1)S(1)}, bf16[64,512]{1,0:T(8,128)(2,1)S(1)}, u32[]{:S(2)}, u32[]{:S(2)}) collective-permute-start(bf16[64,512]{1,0:T(8,128)(2,1)S(1)} %slice.25), channel_id=1, source_target_pairs={{16,0},{17,1},{18,2},{19,3},{20,4},{21,5},{22,6},{23,7},{24,8},{25... | collective-permute-start | bytes 196616 | tf_op jit(solution)/shard_map/ppermute | solution.py:48
  63.7 7.2 %shard_map.58 = (f32[1024,512]{1,0:T(8,128)}, f32[8,128]{1,0:T(8,128)S(1)}) custom-call(bf16[1024,8192]{1,0:T(8,128)(2,1)} %refs_0_.13, bf16[1024,512]{1,0:T(8,128)(2,1)S(1)} %shard_map.56.refs_2_.refs_1_, bf16[1024,512]{1,0:T(8,128)(2,1)S(1)} %collective-permute-done.13.refs_3_.refs_2_, f32[1024,512]{1,0:T(8,128)} %get-tuple-element.63.refs_3_, ...), custom_call_target="tpu_custom_call" | custom-call | flops 1 | bytes 1 | tf_op jit(solution)/shard_map/pallas_call | solution.py:69
  75.1 1.9 %collective-permute-start.19 = (bf16[128,512]{1,0:T(8,128)(2,1)S(1)}, bf16[128,512]{1,0:T(8,128)(2,1)S(1)}, u32[]{:S(2)}, u32[]{:S(2)}) collective-permute-start(bf16[128,512]{1,0:T(8,128)(2,1)S(1)} %slice.26), channel_id=1, source_target_pairs={{2,19},{3,16},{6,23},{7,20},{10,27},{11,24},{14,31},{15,28},{16,17... | collective-permute-start | bytes 393224 | tf_op jit(solution)/shard_map/ppermute | solution.py:48
  77.0 7.3 %shard_map.60 = (f32[1024,512]{1,0:T(8,128)}, f32[8,128]{1,0:T(8,128)S(1)}) custom-call(bf16[1024,8192]{1,0:T(8,128)(2,1)} %refs_0_.13, bf16[1024,512]{1,0:T(8,128)(2,1)S(1)} %collective-permute-done.4.refs_0_.refs_2_.refs_1_, bf16[1024,512]{1,0:T(8,128)(2,1)S(1)} %get-tuple-element.83.refs_3_.refs_2_, f32[1024,512]{1,0:T(8,128)} %get-tuple-element.67.refs_3_, ...), custom_call_target="tpu_custom_call" | custom-call | flops 1 | bytes 1 | tf_op jit(solution)/shard_map/pallas_call | solution.py:69
  86.7 2.5 %collective-permute-start.21 = (bf16[384,512]{1,0:T(8,128)(2,1)S(1)}, bf16[384,512]{1,0:T(8,128)(2,1)S(1)}, u32[]{:S(2)}, u32[]{:S(2)}) collective-permute-start(bf16[384,512]{1,0:T(8,128)(2,1)S(1)} %get-tuple-element.70), channel_id=1, source_target_pairs={{0,3},{1,0},{2,1},{3,2},{4,7},{5,4},{6,5},{7,6},{8,11},{9,8},{10,9... | collective-permute-start | bytes 1179656 | tf_op jit(solution)/shard_map/ppermute | solution.py:48
  89.7 5.0 %collective-permute-done.20.refs_0_ = bf16[384,512]{1,0:T(8,128)(2,1)S(1)} collective-permute-done((bf16[384,512]{1,0:T(8,128)(2,1)S(1)}, bf16[384,512]{1,0:T(8,128)(2,1)S(1)}, u32[]{:S(2)}, u32[]{:S(2)}) %collective-permute-start.20) | collective-permute-done | bytes 393248 | tf_op jit(solution)/shard_map/ppermute | solution.py:48
  94.6 3.5 %collective-permute-done.21.refs_1_ = bf16[384,512]{1,0:T(8,128)(2,1)S(1)} collective-permute-done((bf16[384,512]{1,0:T(8,128)(2,1)S(1)}, bf16[384,512]{1,0:T(8,128)(2,1)S(1)}, u32[]{:S(2)}, u32[]{:S(2)}) %collective-permute-start.21) | collective-permute-done | bytes 393248 | tf_op jit(solution)/shard_map/ppermute | solution.py:48
  99.3 4.8 %collective-permute-start.23 = (bf16[128,512]{1,0:T(8,128)(2,1)S(1)}, bf16[128,512]{1,0:T(8,128)(2,1)S(1)}, u32[]{:S(2)}, u32[]{:S(2)}) collective-permute-start(bf16[128,512]{1,0:T(8,128)(2,1)S(1)} %get-tuple-element.85), channel_id=1, source_target_pairs={{0,96},{1,113},{2,115},{3,112},{4,100},{5,117},{6,119},{7,116},{8,... | collective-permute-start | bytes 393224 | tf_op jit(solution)/shard_map/ppermute | solution.py:48
  104.7 2.1 %collective-permute-done.23.refs_4_ = bf16[128,512]{1,0:T(8,128)(2,1)S(1)} collective-permute-done((bf16[128,512]{1,0:T(8,128)(2,1)S(1)}, bf16[128,512]{1,0:T(8,128)(2,1)S(1)}, u32[]{:S(2)}, u32[]{:S(2)}) %collective-permute-start.23) | collective-permute-done | bytes 131104 | tf_op jit(solution)/shard_map/ppermute | solution.py:48
  106.8 6.3 %collective-permute-done.24.refs_5_ = bf16[128,512]{1,0:T(8,128)(2,1)S(1)} collective-permute-done((bf16[128,512]{1,0:T(8,128)(2,1)S(1)}, bf16[128,512]{1,0:T(8,128)(2,1)S(1)}, u32[]{:S(2)}, u32[]{:S(2)}) %collective-permute-start.24) | collective-permute-done | bytes 131104 | tf_op jit(solution)/shard_map/ppermute | solution.py:48
  115.4 3.6 %collective-permute-start.27 = (bf16[256,512]{1,0:T(8,128)(2,1)S(1)}, bf16[256,512]{1,0:T(8,128)(2,1)S(1)}, u32[]{:S(2)}, u32[]{:S(2)}) collective-permute-start(bf16[256,512]{1,0:T(8,128)(2,1)S(1)} %get-tuple-element.75), channel_id=1, source_target_pairs={{0,8},{1,9},{2,10},{3,11},{4,12},{5,13},{6,14},{7,15},{8,0},{9,1},... | collective-permute-start | bytes 786440 | tf_op jit(solution)/shard_map/ppermute | solution.py:48
  119.1 1.8 %collective-permute-start.28 = (bf16[256,512]{1,0:T(8,128)(2,1)S(1)}, bf16[256,512]{1,0:T(8,128)(2,1)S(1)}, u32[]{:S(2)}, u32[]{:S(2)}) collective-permute-start(bf16[256,512]{1,0:T(8,128)(2,1)S(1)} %get-tuple-element.76), channel_id=1, source_target_pairs={{0,12},{1,13},{2,14},{3,15},{4,0},{5,1},{6,2},{7,3},{8,4},{9,5},{1... | collective-permute-start | bytes 786440 | tf_op jit(solution)/shard_map/ppermute | solution.py:48
  120.8 7.0 %shard_map.64 = (bf16[1024,512]{1,0:T(8,128)(2,1)}, f32[8,128]{1,0:T(8,128)S(1)}) custom-call(bf16[1024,8192]{1,0:T(8,128)(2,1)} %refs_0_.13, bf16[1024,512]{1,0:T(8,128)(2,1)S(1)} %collective-permute-done.5.refs_1_.refs_4_, bf16[1024,512]{1,0:T(8,128)(2,1)S(1)} %get-tuple-element.82.refs_5_.refs_2_, f32[1024,512]{1,0:T(8,128)} %get-tuple-element.77.refs_3_, ...), custom_call_target="tpu_custom_call" | custom-call | flops 1 | bytes 1 | tf_op jit(solution)/shard_map/pallas_call | solution.py:69
  129.0 2.9 %collective-permute-start.29 = (bf16[512,512]{1,0:T(8,128)(2,1)S(1)}, bf16[512,512]{1,0:T(8,128)(2,1)S(1)}, u32[]{:S(2)}, u32[]{:S(2)}) collective-permute-start(bf16[512,512]{1,0:T(8,128)(2,1)S(1)} %get-tuple-element.80), channel_id=1, source_target_pairs={{0,16},{1,17},{2,18},{3,19},{4,20},{5,21},{6,22},{7,23},{8,24},{9,... | collective-permute-start | bytes 1572872 | tf_op jit(solution)/shard_map/ppermute | solution.py:48
  (84 shorter events, 36.6 us)
Async XLA Ops:
  2.1 26.7 %collective-permute-start.4 = (bf16[1024,512]{1,0:T(8,128)(2,1)}, bf16[1024,512]{1,0:T(8,128)(2,1)S(1)}, u32[]{:S(2)}, u32[]{:S(2)}) collective-permute-start(bf16[1024,512]{1,0:T(8,128)(2,1)} %refs_0_.10), channel_id=1, source_target_pairs={{0,96},{1,97},{2,98},{3,99},{4,100},{5,101},{6,102},{7,103},{8,104... | collective-permute-start | bytes 3145736 | tf_op jit(solution)/shard_map/ppermute | solution.py:48
  6.0 25.8 %collective-permute-start.5 = (bf16[1024,512]{1,0:T(8,128)(2,1)}, bf16[1024,512]{1,0:T(8,128)(2,1)S(1)}, u32[]{:S(2)}, u32[]{:S(2)}) collective-permute-start(bf16[1024,512]{1,0:T(8,128)(2,1)} %refs_0_.10), channel_id=1, source_target_pairs={{0,32},{1,33},{2,34},{3,35},{4,36},{5,37},{6,38},{7,39},{8,40},{9,... | collective-permute-start | bytes 3145736 | tf_op jit(solution)/shard_map/ppermute | solution.py:48
  10.1 21.7 %collective-permute-start.1 = (bf16[4,192,512]{2,1,0:T(8,128)(2,1)S(1)}, bf16[4,192,512]{2,1,0:T(8,128)(2,1)S(1)}, u32[]{:S(2)}, u32[]{:S(2)}) collective-permute-start(bf16[4,192,512]{2,1,0:T(8,128)(2,1)S(1)} %get-tuple-element.42.refs_3_), channel_id=1, source_target_pairs={{0,4},{1,5},{2,6},{3,7},{4,8},{5,9},{6,10},{7,11},{8,12},{9,13},{1... | collective-permute-start | bytes 2359304 | tf_op jit(solution)/shard_map/ppermute | solution.py:48
  11.4 20.4 %collective-permute-start.2 = (bf16[4,192,512]{2,1,0:T(8,128)(2,1)S(1)}, bf16[4,192,512]{2,1,0:T(8,128)(2,1)S(1)}, u32[]{:S(2)}, u32[]{:S(2)}) collective-permute-start(bf16[4,192,512]{2,1,0:T(8,128)(2,1)S(1)} %get-tuple-element.43), channel_id=1, source_target_pairs={{0,12},{1,13},{2,14},{3,15},{4,0},{5,1},{6,2},{7,3},{8,4},{9,5},{1... | collective-permute-start | bytes 2359304 | tf_op jit(solution)/shard_map/ppermute | solution.py:48
  12.9 19.2 %collective-permute-start.3 = (bf16[4,192,512]{2,1,0:T(8,128)(2,1)S(1)}, bf16[4,192,512]{2,1,0:T(8,128)(2,1)S(1)}, u32[]{:S(2)}, u32[]{:S(2)}) collective-permute-start(bf16[4,192,512]{2,1,0:T(8,128)(2,1)S(1)} %get-tuple-element.44), channel_id=1, source_target_pairs={{0,8},{1,9},{2,10},{3,11},{4,12},{5,13},{6,14},{7,15},{8,0},{9,1},... | collective-permute-start | bytes 2359304 | tf_op jit(solution)/shard_map/ppermute | solution.py:48
  32.4 7.6 %collective-permute-start.9 = (bf16[2,1024,512]{2,1,0:T(8,128)(2,1)S(1)}, bf16[2,1024,512]{2,1,0:T(8,128)(2,1)S(1)}, u32[]{:S(2)}, u32[]{:S(2)}) collective-permute-start(bf16[2,1024,512]{2,1,0:T(8,128)(2,1)S(1)} %get-tuple-element.47.refs_4_), channel_id=1, source_target_pairs={{0,16},{1,17},{2,18},{3,19},{4,20},{5,21},{6,22},{7,23},{8,24},{9,... | collective-permute-start | bytes 6291464 | tf_op jit(solution)/shard_map/ppermute | solution.py:48
  33.4 14.7 %collective-permute-start.12 = (bf16[1024,512]{1,0:T(8,128)(2,1)S(1)}, bf16[1024,512]{1,0:T(8,128)(2,1)S(1)}, u32[]{:S(2)}, u32[]{:S(2)}) collective-permute-start(bf16[1024,512]{1,0:T(8,128)(2,1)S(1)} %get-tuple-element.55), channel_id=1, source_target_pairs={{0,32},{1,33},{2,34},{3,35},{4,36},{5,37},{6,38},{7,39},{8,40},{9,... | collective-permute-start | bytes 3145736 | tf_op jit(solution)/shard_map/ppermute | solution.py:48
  36.7 8.6 %collective-permute-start.6 = (bf16[192,512]{1,0:T(8,128)(2,1)S(1)}, bf16[192,512]{1,0:T(8,128)(2,1)S(1)}, u32[]{:S(2)}, u32[]{:S(2)}) collective-permute-start(bf16[192,512]{1,0:T(8,128)(2,1)S(1)} %get-tuple-element.48.refs_6_), channel_id=1, source_target_pairs={{0,1},{1,2},{2,3},{3,0},{4,5},{5,6},{6,7},{7,4},{8,9},{9,10},{10,1... | collective-permute-start | bytes 589832 | tf_op jit(solution)/shard_map/ppermute | solution.py:48
  49.8 21.1 %collective-permute-start.10 = (bf16[4,256,512]{2,1,0:T(8,128)(2,1)S(1)}, bf16[4,256,512]{2,1,0:T(8,128)(2,1)S(1)}, u32[]{:S(2)}, u32[]{:S(2)}) collective-permute-start(bf16[4,256,512]{2,1,0:T(8,128)(2,1)S(1)} %get-tuple-element.52.refs_4_), channel_id=1, source_target_pairs={{0,4},{1,5},{2,6},{3,7},{4,8},{5,9},{6,10},{7,11},{8,12},{9,13},{1... | collective-permute-start | bytes 3145736 | tf_op jit(solution)/shard_map/ppermute | solution.py:48
  51.2 19.8 %collective-permute-start.11 = (bf16[4,256,512]{2,1,0:T(8,128)(2,1)}, bf16[4,256,512]{2,1,0:T(8,128)(2,1)S(1)}, u32[]{:S(2)}, u32[]{:S(2)}) collective-permute-start(bf16[4,256,512]{2,1,0:T(8,128)(2,1)} %get-tuple-element.53), channel_id=1, source_target_pairs={{0,12},{1,13},{2,14},{3,15},{4,0},{5,1},{6,2},{7,3},{8,4},{9,5},{1... | collective-permute-start | bytes 3145736 | tf_op jit(solution)/shard_map/ppermute | solution.py:48
  57.1 13.9 %collective-permute-start.14 = (bf16[4,128,512]{2,1,0:T(8,128)(2,1)}, bf16[4,128,512]{2,1,0:T(8,128)(2,1)S(1)}, u32[]{:S(2)}, u32[]{:S(2)}) collective-permute-start(bf16[4,128,512]{2,1,0:T(8,128)(2,1)} %get-tuple-element.56.refs_4_), channel_id=1, source_target_pairs={{0,4},{1,5},{2,6},{3,7},{4,8},{5,9},{6,10},{7,11},{8,12},{9,13},{1... | collective-permute-start | bytes 1572872 | tf_op jit(solution)/shard_map/ppermute | solution.py:48
  57.9 13.1 %collective-permute-start.15 = (bf16[4,128,512]{2,1,0:T(8,128)(2,1)}, bf16[4,128,512]{2,1,0:T(8,128)(2,1)S(1)}, u32[]{:S(2)}, u32[]{:S(2)}) collective-permute-start(bf16[4,128,512]{2,1,0:T(8,128)(2,1)} %get-tuple-element.57), channel_id=1, source_target_pairs={{0,12},{1,13},{2,14},{3,15},{4,0},{5,1},{6,2},{7,3},{8,4},{9,5},{1... | collective-permute-start | bytes 1572872 | tf_op jit(solution)/shard_map/ppermute | solution.py:48
  72.3 13.5 %collective-permute-start.17 = (bf16[4,192,512]{2,1,0:T(8,128)(2,1)S(1)}, bf16[4,192,512]{2,1,0:T(8,128)(2,1)S(1)}, u32[]{:S(2)}, u32[]{:S(2)}) collective-permute-start(bf16[4,192,512]{2,1,0:T(8,128)(2,1)S(1)} %get-tuple-element.65), channel_id=1, source_target_pairs={{0,4},{1,5},{2,6},{3,7},{4,8},{5,9},{6,10},{7,11},{8,12},{9,13},{1... | collective-permute-start | bytes 2359304 | tf_op jit(solution)/shard_map/ppermute | solution.py:48
  73.6 12.2 %collective-permute-start.18 = (bf16[4,192,512]{2,1,0:T(8,128)(2,1)S(1)}, bf16[4,192,512]{2,1,0:T(8,128)(2,1)S(1)}, u32[]{:S(2)}, u32[]{:S(2)}) collective-permute-start(bf16[4,192,512]{2,1,0:T(8,128)(2,1)S(1)} %get-tuple-element.66), channel_id=1, source_target_pairs={{0,12},{1,13},{2,14},{3,15},{4,0},{5,1},{6,2},{7,3},{8,4},{9,5},{1... | collective-permute-start | bytes 2359304 | tf_op jit(solution)/shard_map/ppermute | solution.py:48
  75.1 9.3 %collective-permute-start.19 = (bf16[128,512]{1,0:T(8,128)(2,1)S(1)}, bf16[128,512]{1,0:T(8,128)(2,1)S(1)}, u32[]{:S(2)}, u32[]{:S(2)}) collective-permute-start(bf16[128,512]{1,0:T(8,128)(2,1)S(1)} %slice.26), channel_id=1, source_target_pairs={{2,19},{3,16},{6,23},{7,20},{10,27},{11,24},{14,31},{15,28},{16,17... | collective-permute-start | bytes 393224 | tf_op jit(solution)/shard_map/ppermute | solution.py:48
  86.4 8.2 %collective-permute-start.20 = (bf16[384,512]{1,0:T(8,128)(2,1)S(1)}, bf16[384,512]{1,0:T(8,128)(2,1)S(1)}, u32[]{:S(2)}, u32[]{:S(2)}) collective-permute-start(bf16[384,512]{1,0:T(8,128)(2,1)S(1)} %get-tuple-element.69), channel_id=1, source_target_pairs={{0,1},{1,2},{2,3},{3,0},{4,5},{5,6},{6,7},{7,4},{8,9},{9,10},{10,1... | collective-permute-start | bytes 1179656 | tf_op jit(solution)/shard_map/ppermute | solution.py:48
  86.7 11.4 %collective-permute-start.21 = (bf16[384,512]{1,0:T(8,128)(2,1)S(1)}, bf16[384,512]{1,0:T(8,128)(2,1)S(1)}, u32[]{:S(2)}, u32[]{:S(2)}) collective-permute-start(bf16[384,512]{1,0:T(8,128)(2,1)S(1)} %get-tuple-element.70), channel_id=1, source_target_pairs={{0,3},{1,0},{2,1},{3,2},{4,7},{5,4},{6,5},{7,6},{8,11},{9,8},{10,9... | collective-permute-start | bytes 1179656 | tf_op jit(solution)/shard_map/ppermute | solution.py:48
  89.2 9.9 %collective-permute-start.22 = (bf16[384,512]{1,0:T(8,128)(2,1)S(1)}, bf16[384,512]{1,0:T(8,128)(2,1)S(1)}, u32[]{:S(2)}, u32[]{:S(2)}) collective-permute-start(bf16[384,512]{1,0:T(8,128)(2,1)S(1)} %get-tuple-element.71), channel_id=1, source_target_pairs={{0,2},{1,3},{2,0},{3,1},{4,6},{5,7},{6,4},{7,5},{8,10},{9,11},{10,... | collective-permute-start | bytes 1179656 | tf_op jit(solution)/shard_map/ppermute | solution.py:48
  99.3 7.5 %collective-permute-start.23 = (bf16[128,512]{1,0:T(8,128)(2,1)S(1)}, bf16[128,512]{1,0:T(8,128)(2,1)S(1)}, u32[]{:S(2)}, u32[]{:S(2)}) collective-permute-start(bf16[128,512]{1,0:T(8,128)(2,1)S(1)} %get-tuple-element.85), channel_id=1, source_target_pairs={{0,96},{1,113},{2,115},{3,112},{4,100},{5,117},{6,119},{7,116},{8,... | collective-permute-start | bytes 393224 | tf_op jit(solution)/shard_map/ppermute | solution.py:48
  104.1 9.0 %collective-permute-start.24 = (bf16[128,512]{1,0:T(8,128)(2,1)S(1)}, bf16[128,512]{1,0:T(8,128)(2,1)S(1)}, u32[]{:S(2)}, u32[]{:S(2)}) collective-permute-start(bf16[128,512]{1,0:T(8,128)(2,1)S(1)} %get-tuple-element.86.refs_2_), channel_id=1, source_target_pairs={{0,64},{1,81},{2,83},{3,80},{4,68},{5,85},{6,87},{7,84},{8,72},{9,... | collective-permute-start | bytes 393224 | tf_op jit(solution)/shard_map/ppermute | solution.py:48
  104.1 10.3 %collective-permute-start.25 = (bf16[128,512]{1,0:T(8,128)(2,1)S(1)}, bf16[128,512]{1,0:T(8,128)(2,1)S(1)}, u32[]{:S(2)}, u32[]{:S(2)}) collective-permute-start(bf16[128,512]{1,0:T(8,128)(2,1)S(1)} %get-tuple-element.84), channel_id=1, source_target_pairs={{0,32},{1,49},{2,51},{3,48},{4,36},{5,53},{6,55},{7,52},{8,40},{9,... | collective-permute-start | bytes 393224 | tf_op jit(solution)/shard_map/ppermute | solution.py:48
  114.6 13.2 %collective-permute-start.26 = (bf16[256,512]{1,0:T(8,128)(2,1)S(1)}, bf16[256,512]{1,0:T(8,128)(2,1)S(1)}, u32[]{:S(2)}, u32[]{:S(2)}) collective-permute-start(bf16[256,512]{1,0:T(8,128)(2,1)S(1)} %get-tuple-element.74), channel_id=1, source_target_pairs={{0,4},{1,5},{2,6},{3,7},{4,8},{5,9},{6,10},{7,11},{8,12},{9,13},{1... | collective-permute-start | bytes 786440 | tf_op jit(solution)/shard_map/ppermute | solution.py:48
  115.4 13.2 %collective-permute-start.27 = (bf16[256,512]{1,0:T(8,128)(2,1)S(1)}, bf16[256,512]{1,0:T(8,128)(2,1)S(1)}, u32[]{:S(2)}, u32[]{:S(2)}) collective-permute-start(bf16[256,512]{1,0:T(8,128)(2,1)S(1)} %get-tuple-element.75), channel_id=1, source_target_pairs={{0,8},{1,9},{2,10},{3,11},{4,12},{5,13},{6,14},{7,15},{8,0},{9,1},... | collective-permute-start | bytes 786440 | tf_op jit(solution)/shard_map/ppermute | solution.py:48
  119.1 9.7 %collective-permute-start.28 = (bf16[256,512]{1,0:T(8,128)(2,1)S(1)}, bf16[256,512]{1,0:T(8,128)(2,1)S(1)}, u32[]{:S(2)}, u32[]{:S(2)}) collective-permute-start(bf16[256,512]{1,0:T(8,128)(2,1)S(1)} %get-tuple-element.76), channel_id=1, source_target_pairs={{0,12},{1,13},{2,14},{3,15},{4,0},{5,1},{6,2},{7,3},{8,4},{9,5},{1... | collective-permute-start | bytes 786440 | tf_op jit(solution)/shard_map/ppermute | solution.py:48
  (19 other events, 98.5 us)

commit v4 on v3

--- a/solution.py
+++ b/solution.py
@@ -96,35 +96,31 @@
             window = pl.ds(start, H // parts)
             return jnp.where((block >> 1) == k, mine_ref[window, :], theirs_ref[window, :])
 
-        for t, turn in enumerate(turns):
-            j = (z + turn) & 3
-            for i, offset in enumerate(OFFSETS):
-                q = (y + offset) & 3
-                p = row_of(z, k, j, q)
-                window = pl.ds(pl.multiple_of((q & 1) * H, H), H)
-                right = jnp.where((q >> 1) == k, refs[2 * t][window, :], refs[2 * t + 1][window, :])
-                left = []
-                for offset in OFFSETS:
-                    c = (x + offset) & 3
-                    left.append(rows_of(p, c, N))
-                    if diagonal:
-                        left.append(rows_of((q + 2) & 3, k * N + c, 2 * N))
-                result = lax.dot_general(
-                    jnp.concatenate(left, 0), right, (((1,), (1,)), ((), ())), preferred_element_type=F32
-                ).astype(BF16)
-                @pl.when(k == 0)
-                def _(result=result, i=i, t=t):
+        def work(core):
+            for t, turn in enumerate(turns):
+                j = (z + turn) & 3
+                for i, offset in enumerate(OFFSETS):
+                    q = (y + offset) & 3
+                    p = row_of(z, k, j, q)
+                    window = pl.ds(pl.multiple_of((q & 1) * H, H), H)
+                    right = jnp.where((q >> 1) == k, refs[2 * t][window, :], refs[2 * t + 1][window, :])
+                    left = []
+                    for offset in OFFSETS:
+                        c = (x + offset) & 3
+                        left.append(rows_of(p, c, N))
+                        if diagonal:
+                            left.append(rows_of((q + 2) & 3, k * N + c, 2 * N))
+                    result = lax.dot_general(
+                        jnp.concatenate(left, 0), right, (((1,), (1,)), ((), ())), preferred_element_type=F32
+                    ).astype(BF16)
                     for m in range(N):
-                        for out, to, start, size in places[m][t]:
+                        part, second = (m, i) if core == 0 else (i, m)
+                        for out, to, start, size in places[part][t]:
                             rows_sent = slice(m * tall + start, m * tall + start + size)
-                            out_refs[out][i, to : to + size, :] = result[rows_sent]
-
-                @pl.when(k == 1)
-                def _(result=result, i=i, t=t):
-                    for m in range(N):
-                        for out, to, start, size in places[i][t]:
-                            rows_sent = slice(m * tall + start, m * tall + start + size)
-                            out_refs[out][m, to : to + size, :] = result[rows_sent]
+                            out_refs[out][second, to : to + size, :] = result[rows_sent]
+
+        for core in range(2):
+            pl.when(k == core)(functools.partial(work, core))
 
     flat = [a for pair in others for a in pair]
     heights = {}
@@ -174,7 +170,7 @@
         [array(height, lat, dtype=dtype), array(8, 128, dtype=F32)],
         [inv_root, *tiles, *more],
         after,
-        vmem=50,
+        vmem=42,
         specs=[ANY] + [VMEM] * (len(tiles) + len(more)),
         scratch=[pltpu.VMEM((len(tiles), height, rows), BF16), pltpu.VMEM((height, lat), F32), pltpu.SemaphoreType.DMA((len(tiles),))],
     )

time: 135 us -> 134 us (level)
  waiting for transfers between devices: 38.2 us -> 53.5 us
  Pallas kernels: 42 us -> 27.4 us
  local copies, waits for them, and re-layouts: 4.47 us -> 1.49 us
    ppermute x30, waiting for transfers between devices: 38.2 us -> 53.5 us  [send(): lax.ppermute(value, AXES, [(source, linear(*to)) for source, to in pairs...]
    pallas_call x17, Pallas kernels: 42 us -> 27.4 us  [call(): pl.pallas_call(body, out_shape=outs, in_specs=list(specs or [VMEM] * n) +...]
    unnamed x26 -> x6, local copies, waits for them, and re-layouts: 4.27 us -> 1.29 us
  transfers between devices with their start and end apart: 30 -> 30, of which waited for: 16 -> 19; matrix products, arithmetic and copies ran while one was open for 0% -> 0% of each run, Pallas kernels for 28% -> 18%
where the time goes in v4:
time: 134 us
  waiting for transfers between devices  53.5 us (40%)
  starting transfers between devices  50.5 us (38%)
  Pallas kernels  27.4 us (20%)
  local copies, waits for them, and re-layouts  1.49 us (1%)
    ppermute x30, waiting for transfers between devices, send(): lax.ppermute(value, AXES, [(source, linear(*to)) for source, to in pairs...  53.5 us
    ppermute x30, starting transfers between devices, send(): lax.ppermute(value, AXES, [(source, linear(*to)) for source, to in pairs...  50.5 us
    pallas_call x17, Pallas kernels, call(): pl.pallas_call(body, out_shape=outs, in_specs=list(specs or [VMEM] * n) +...  27.4 us
  transfers between devices with their start and end apart: 30, of which 19 were waited for; matrix products, arithmetic and copies ran while one was open for 0% of the time, Pallas kernels for 18%

profile of v4, /device:TPU:1, one launch (start us, length us, event | category | flops | bytes accessed | tf_op | source)
XLA Modules:
  0.0 133.6 jit_solution(14977699062681162458)
XLA Ops:
  2.1 3.9 %collective-permute-start.4 = (bf16[1024,512]{1,0:T(8,128)(2,1)}, bf16[1024,512]{1,0:T(8,128)(2,1)S(1)}, u32[]{:S(2)}, u32[]{:S(2)}) collective-permute-start(bf16[1024,512]{1,0:T(8,128)(2,1)} %refs_0_.10), channel_id=1, source_target_pairs={{0,96},{1,97},{2,98},{3,99},{4,100},{5,101},{6,102},{7,103},{8,104... | collective-permute-start | bytes 3145736 | tf_op jit(solution)/shard_map/ppermute | solution.py:48
  7.3 1.9 %shard_map.50 = (bf16[4,192,512]{2,1,0:T(8,128)(2,1)S(1)}, bf16[4,192,512]{2,1,0:T(8,128)(2,1)S(1)}, bf16[4,192,512]{2,1,0:T(8,128)(2,1)S(1)}, bf16[4,192,512]{2,1,0:T(8,128)(2,1)S(1)}) custom-call(bf16[1024,512]{1,0:T(8,128)(2,1)S(1)} %copy-done, bf16[1024,512]{1,0:T(8,128)(2,1)S(1)} %collective-permute-done.refs_1_.refs_3_.refs_2_, ...), custom_call_target="tpu_custom_call" | custom-call | flops 1 | bytes 1 | tf_op jit(solution)/shard_map/pallas_call | solution.py:69
  13.6 4.0 %shard_map.51 = (f32[1024,512]{1,0:T(8,128)S(1)}, f32[8,128]{1,0:T(8,128)S(1)}) custom-call(bf16[1024,8192]{1,0:T(8,128)(2,1)} %refs_0_.13, bf16[1024,512]{1,0:T(8,128)(2,1)S(1)} %copy-done.1, bf16[1024,512]{1,0:T(8,128)(2,1)S(1)} %collective-permute-done.refs_1_.refs_3_.refs_2_, bf16[4,192,512]{2,1,0:T(8,128)(2,1)S(1)} %get-tuple-element.42.refs_3_), custom_call_target="tpu_custom_call" | custom-call | flops 1 | bytes 1 | tf_op jit(solution)/shard_map/pallas_call | solution.py:69
  17.6 11.2 %collective-permute-done.4.refs_0_.refs_2_.refs_1_ = bf16[1024,512]{1,0:T(8,128)(2,1)S(1)} collective-permute-done((bf16[1024,512]{1,0:T(8,128)(2,1)}, bf16[1024,512]{1,0:T(8,128)(2,1)S(1)}, u32[]{:S(2)}, u32[]{:S(2)}) %collective-permute-start.4) | collective-permute-done | bytes 1048608 | tf_op jit(solution)/shard_map/ppermute | solution.py:48
  28.8 3.0 %collective-permute-done.5.refs_1_.refs_4_ = bf16[1024,512]{1,0:T(8,128)(2,1)S(1)} collective-permute-done((bf16[1024,512]{1,0:T(8,128)(2,1)}, bf16[1024,512]{1,0:T(8,128)(2,1)S(1)}, u32[]{:S(2)}, u32[]{:S(2)}) %collective-permute-start.5) | collective-permute-done | bytes 1048608 | tf_op jit(solution)/shard_map/ppermute | solution.py:48
  33.3 2.1 %collective-permute-start.12 = (bf16[1024,512]{1,0:T(8,128)(2,1)S(1)}, bf16[1024,512]{1,0:T(8,128)(2,1)S(1)}, u32[]{:S(2)}, u32[]{:S(2)}) collective-permute-start(bf16[1024,512]{1,0:T(8,128)(2,1)S(1)} %get-tuple-element.55), channel_id=1, source_target_pairs={{0,32},{1,33},{2,34},{3,35},{4,36},{5,37},{6,38},{7,39},{8,40},{9,... | collective-permute-start | bytes 3145736 | tf_op jit(solution)/shard_map/ppermute | solution.py:48
  39.2 2.7 %shard_map.54 = (bf16[4,256,512]{2,1,0:T(8,128)(2,1)S(1)}, bf16[4,256,512]{2,1,0:T(8,128)(2,1)S(1)}, bf16[4,128,512]{2,1,0:T(8,128)(2,1)S(1)}, bf16[4,128,512]{2,1,0:T(8,128)(2,1)S(1)}, bf16[4,256,512]{2,1,0:T(8,128)(2,1)S(1)}) custom-call(bf16[1024,512]{1,0:T(8,128)(2,1)S(1)} %copy-done.1, ...), custom_call_target="tpu_custom_call" | custom-call | flops 1 | bytes 1 | tf_op jit(solution)/shard_map/pallas_call | solution.py:69
  44.7 2.6 %collective-permute-done.12.refs_0_ = bf16[1024,512]{1,0:T(8,128)(2,1)S(1)} collective-permute-done((bf16[1024,512]{1,0:T(8,128)(2,1)S(1)}, bf16[1024,512]{1,0:T(8,128)(2,1)S(1)}, u32[]{:S(2)}, u32[]{:S(2)}) %collective-permute-start.12) | collective-permute-done | bytes 1048608 | tf_op jit(solution)/shard_map/ppermute | solution.py:48
  47.3 2.2 %collective-permute-start.13 = (bf16[1024,512]{1,0:T(8,128)(2,1)S(1)}, bf16[1024,512]{1,0:T(8,128)(2,1)S(1)}, u32[]{:S(2)}, u32[]{:S(2)}) collective-permute-start(bf16[1024,512]{1,0:T(8,128)(2,1)S(1)} %shard_map.56.refs_2_.refs_1_), channel_id=1, source_target_pairs={{0,16},{1,17},{2,18},{3,19},{4,20},{5,21},{6,22},{7,23},{8,24},{9,... | collective-permute-start | bytes 3145736 | tf_op jit(solution)/shard_map/ppermute | solution.py:48
  56.4 3.0 %collective-permute-start.16 = (bf16[64,512]{1,0:T(8,128)(2,1)S(1)}, bf16[64,512]{1,0:T(8,128)(2,1)S(1)}, u32[]{:S(2)}, u32[]{:S(2)}) collective-permute-start(bf16[64,512]{1,0:T(8,128)(2,1)S(1)} %slice.25), channel_id=1, source_target_pairs={{16,0},{17,1},{18,2},{19,3},{20,4},{21,5},{22,6},{23,7},{24,8},{25... | collective-permute-start | bytes 196616 | tf_op jit(solution)/shard_map/ppermute | solution.py:48
  60.3 4.2 %shard_map.58 = (f32[1024,512]{1,0:T(8,128)S(1)}, f32[8,128]{1,0:T(8,128)S(1)}) custom-call(bf16[1024,8192]{1,0:T(8,128)(2,1)} %refs_0_.13, bf16[1024,512]{1,0:T(8,128)(2,1)S(1)} %shard_map.56.refs_2_.refs_1_, bf16[1024,512]{1,0:T(8,128)(2,1)S(1)} %collective-permute-done.13.refs_3_.refs_2_, f32[1024,512]{1,0:T(8,128)S(1)} %get-tuple-element.63.refs_3_, ...), custom_call_target="tpu_custom_call" | custom-call | flops 1 | bytes 1 | tf_op jit(solution)/shard_map/pallas_call | solution.py:69
  64.8 5.6 %collective-permute-done.14.refs_4_.refs_6_.refs_3_ = bf16[4,128,512]{2,1,0:T(8,128)(2,1)S(1)} collective-permute-done((bf16[4,128,512]{2,1,0:T(8,128)(2,1)S(1)}, bf16[4,128,512]{2,1,0:T(8,128)(2,1)S(1)}, u32[]{:S(2)}, u32[]{:S(2)}) %collective-permute-start.14) | collective-permute-done | bytes 524320 | tf_op jit(solution)/shard_map/ppermute | solution.py:48
  73.6 1.9 %collective-permute-start.19 = (bf16[128,512]{1,0:T(8,128)(2,1)S(1)}, bf16[128,512]{1,0:T(8,128)(2,1)S(1)}, u32[]{:S(2)}, u32[]{:S(2)}) collective-permute-start(bf16[128,512]{1,0:T(8,128)(2,1)S(1)} %slice.26), channel_id=1, source_target_pairs={{2,19},{3,16},{6,23},{7,20},{10,27},{11,24},{14,31},{15,28},{16,17... | collective-permute-start | bytes 393224 | tf_op jit(solution)/shard_map/ppermute | solution.py:48
  75.6 4.1 %shard_map.60 = (f32[1024,512]{1,0:T(8,128)S(1)}, f32[8,128]{1,0:T(8,128)S(1)}) custom-call(bf16[1024,8192]{1,0:T(8,128)(2,1)} %refs_0_.13, bf16[1024,512]{1,0:T(8,128)(2,1)S(1)} %collective-permute-done.4.refs_0_.refs_2_.refs_1_, bf16[1024,512]{1,0:T(8,128)(2,1)S(1)} %get-tuple-element.83.refs_3_.refs_2_, f32[1024,512]{1,0:T(8,128)S(1)} %get-tuple-element.67.refs_3_, ...), custom_call_target="tpu_custom_call" | custom-call | flops 1 | bytes 1 | tf_op jit(solution)/shard_map/pallas_call | solution.py:69
  79.7 3.9 %collective-permute-done.19.refs_9_.refs_3_ = bf16[128,512]{1,0:T(8,128)(2,1)S(1)} collective-permute-done((bf16[128,512]{1,0:T(8,128)(2,1)S(1)}, bf16[128,512]{1,0:T(8,128)(2,1)S(1)}, u32[]{:S(2)}, u32[]{:S(2)}) %collective-permute-start.19) | collective-permute-done | bytes 131104 | tf_op jit(solution)/shard_map/ppermute | solution.py:48
  89.2 4.2 %collective-permute-done.20.refs_0_ = bf16[384,512]{1,0:T(8,128)(2,1)S(1)} collective-permute-done((bf16[384,512]{1,0:T(8,128)(2,1)S(1)}, bf16[384,512]{1,0:T(8,128)(2,1)S(1)}, u32[]{:S(2)}, u32[]{:S(2)}) %collective-permute-start.20) | collective-permute-done | bytes 393248 | tf_op jit(solution)/shard_map/ppermute | solution.py:48
  93.4 3.5 %collective-permute-done.21.refs_1_ = bf16[384,512]{1,0:T(8,128)(2,1)S(1)} collective-permute-done((bf16[384,512]{1,0:T(8,128)(2,1)S(1)}, bf16[384,512]{1,0:T(8,128)(2,1)S(1)}, u32[]{:S(2)}, u32[]{:S(2)}) %collective-permute-start.21) | collective-permute-done | bytes 393248 | tf_op jit(solution)/shard_map/ppermute | solution.py:48
  98.8 3.7 %collective-permute-start.23 = (bf16[128,512]{1,0:T(8,128)(2,1)S(1)}, bf16[128,512]{1,0:T(8,128)(2,1)S(1)}, u32[]{:S(2)}, u32[]{:S(2)}) collective-permute-start(bf16[128,512]{1,0:T(8,128)(2,1)S(1)} %get-tuple-element.85), channel_id=1, source_target_pairs={{0,96},{1,113},{2,115},{3,112},{4,100},{5,117},{6,119},{7,116},{8,... | collective-permute-start | bytes 393224 | tf_op jit(solution)/shard_map/ppermute | solution.py:48
  104.3 2.1 %collective-permute-done.23.refs_4_ = bf16[128,512]{1,0:T(8,128)(2,1)S(1)} collective-permute-done((bf16[128,512]{1,0:T(8,128)(2,1)S(1)}, bf16[128,512]{1,0:T(8,128)(2,1)S(1)}, u32[]{:S(2)}, u32[]{:S(2)}) %collective-permute-start.23) | collective-permute-done | bytes 131104 | tf_op jit(solution)/shard_map/ppermute | solution.py:48
  106.3 4.9 %collective-permute-done.24.refs_5_ = bf16[128,512]{1,0:T(8,128)(2,1)S(1)} collective-permute-done((bf16[128,512]{1,0:T(8,128)(2,1)S(1)}, bf16[128,512]{1,0:T(8,128)(2,1)S(1)}, u32[]{:S(2)}, u32[]{:S(2)}) %collective-permute-start.24) | collective-permute-done | bytes 131104 | tf_op jit(solution)/shard_map/ppermute | solution.py:48
  114.0 3.2 %collective-permute-start.27 = (bf16[256,512]{1,0:T(8,128)(2,1)S(1)}, bf16[256,512]{1,0:T(8,128)(2,1)S(1)}, u32[]{:S(2)}, u32[]{:S(2)}) collective-permute-start(bf16[256,512]{1,0:T(8,128)(2,1)S(1)} %get-tuple-element.75), channel_id=1, source_target_pairs={{0,8},{1,9},{2,10},{3,11},{4,12},{5,13},{6,14},{7,15},{8,0},{9,1},... | collective-permute-start | bytes 786440 | tf_op jit(solution)/shard_map/ppermute | solution.py:48
  119.1 5.2 %shard_map.64 = (bf16[1024,512]{1,0:T(8,128)(2,1)}, f32[8,128]{1,0:T(8,128)S(1)}) custom-call(bf16[1024,8192]{1,0:T(8,128)(2,1)} %refs_0_.13, bf16[1024,512]{1,0:T(8,128)(2,1)S(1)} %collective-permute-done.5.refs_1_.refs_4_, bf16[1024,512]{1,0:T(8,128)(2,1)S(1)} %get-tuple-element.82.refs_5_.refs_2_, f32[1024,512]{1,0:T(8,128)S(1)} %get-tuple-element.77.refs_3_, ...), custom_call_target="tpu_custom_call" | custom-call | flops 1 | bytes 1 | tf_op jit(solution)/shard_map/pallas_call | solution.py:69
  124.3 2.7 %collective-permute-done.27.refs_2_ = bf16[256,512]{1,0:T(8,128)(2,1)S(1)} collective-permute-done((bf16[256,512]{1,0:T(8,128)(2,1)S(1)}, bf16[256,512]{1,0:T(8,128)(2,1)S(1)}, u32[]{:S(2)}, u32[]{:S(2)}) %collective-permute-start.27) | collective-permute-done | bytes 262176 | tf_op jit(solution)/shard_map/ppermute | solution.py:48
  127.2 3.2 %collective-permute-start.29 = (bf16[512,512]{1,0:T(8,128)(2,1)S(1)}, bf16[512,512]{1,0:T(8,128)(2,1)S(1)}, u32[]{:S(2)}, u32[]{:S(2)}) collective-permute-start(bf16[512,512]{1,0:T(8,128)(2,1)S(1)} %get-tuple-element.80), channel_id=1, source_target_pairs={{0,16},{1,17},{2,18},{3,19},{4,20},{5,21},{6,22},{7,23},{8,24},{9,... | collective-permute-start | bytes 1572872 | tf_op jit(solution)/shard_map/ppermute | solution.py:48
  (64 shorter events, 43.9 us)
Async XLA Ops:
  2.1 26.7 %collective-permute-start.4 = (bf16[1024,512]{1,0:T(8,128)(2,1)}, bf16[1024,512]{1,0:T(8,128)(2,1)S(1)}, u32[]{:S(2)}, u32[]{:S(2)}) collective-permute-start(bf16[1024,512]{1,0:T(8,128)(2,1)} %refs_0_.10), channel_id=1, source_target_pairs={{0,96},{1,97},{2,98},{3,99},{4,100},{5,101},{6,102},{7,103},{8,104... | collective-permute-start | bytes 3145736 | tf_op jit(solution)/shard_map/ppermute | solution.py:48
  6.0 25.8 %collective-permute-start.5 = (bf16[1024,512]{1,0:T(8,128)(2,1)}, bf16[1024,512]{1,0:T(8,128)(2,1)S(1)}, u32[]{:S(2)}, u32[]{:S(2)}) collective-permute-start(bf16[1024,512]{1,0:T(8,128)(2,1)} %refs_0_.10), channel_id=1, source_target_pairs={{0,32},{1,33},{2,34},{3,35},{4,36},{5,37},{6,38},{7,39},{8,40},{9,... | collective-permute-start | bytes 3145736 | tf_op jit(solution)/shard_map/ppermute | solution.py:48
  9.2 22.6 %collective-permute-start.1 = (bf16[4,192,512]{2,1,0:T(8,128)(2,1)S(1)}, bf16[4,192,512]{2,1,0:T(8,128)(2,1)S(1)}, u32[]{:S(2)}, u32[]{:S(2)}) collective-permute-start(bf16[4,192,512]{2,1,0:T(8,128)(2,1)S(1)} %get-tuple-element.42.refs_3_), channel_id=1, source_target_pairs={{0,4},{1,5},{2,6},{3,7},{4,8},{5,9},{6,10},{7,11},{8,12},{9,13},{1... | collective-permute-start | bytes 2359304 | tf_op jit(solution)/shard_map/ppermute | solution.py:48
  10.5 21.3 %collective-permute-start.2 = (bf16[4,192,512]{2,1,0:T(8,128)(2,1)S(1)}, bf16[4,192,512]{2,1,0:T(8,128)(2,1)S(1)}, u32[]{:S(2)}, u32[]{:S(2)}) collective-permute-start(bf16[4,192,512]{2,1,0:T(8,128)(2,1)S(1)} %get-tuple-element.43), channel_id=1, source_target_pairs={{0,12},{1,13},{2,14},{3,15},{4,0},{5,1},{6,2},{7,3},{8,4},{9,5},{1... | collective-permute-start | bytes 2359304 | tf_op jit(solution)/shard_map/ppermute | solution.py:48
  12.0 19.8 %collective-permute-start.3 = (bf16[4,192,512]{2,1,0:T(8,128)(2,1)S(1)}, bf16[4,192,512]{2,1,0:T(8,128)(2,1)S(1)}, u32[]{:S(2)}, u32[]{:S(2)}) collective-permute-start(bf16[4,192,512]{2,1,0:T(8,128)(2,1)S(1)} %get-tuple-element.44), channel_id=1, source_target_pairs={{0,8},{1,9},{2,10},{3,11},{4,12},{5,13},{6,14},{7,15},{8,0},{9,1},... | collective-permute-start | bytes 2359304 | tf_op jit(solution)/shard_map/ppermute | solution.py:48
  32.1 7.0 %collective-permute-start.9 = (bf16[2,1024,512]{2,1,0:T(8,128)(2,1)S(1)}, bf16[2,1024,512]{2,1,0:T(8,128)(2,1)S(1)}, u32[]{:S(2)}, u32[]{:S(2)}) collective-permute-start(bf16[2,1024,512]{2,1,0:T(8,128)(2,1)S(1)} %get-tuple-element.47.refs_4_), channel_id=1, source_target_pairs={{0,16},{1,17},{2,18},{3,19},{4,20},{5,21},{6,22},{7,23},{8,24},{9,... | collective-permute-start | bytes 6291464 | tf_op jit(solution)/shard_map/ppermute | solution.py:48
  33.3 13.9 %collective-permute-start.12 = (bf16[1024,512]{1,0:T(8,128)(2,1)S(1)}, bf16[1024,512]{1,0:T(8,128)(2,1)S(1)}, u32[]{:S(2)}, u32[]{:S(2)}) collective-permute-start(bf16[1024,512]{1,0:T(8,128)(2,1)S(1)} %get-tuple-element.55), channel_id=1, source_target_pairs={{0,32},{1,33},{2,34},{3,35},{4,36},{5,37},{6,38},{7,39},{8,40},{9,... | collective-permute-start | bytes 3145736 | tf_op jit(solution)/shard_map/ppermute | solution.py:48
  37.0 6.3 %collective-permute-start.7 = (bf16[192,512]{1,0:T(8,128)(2,1)S(1)}, bf16[192,512]{1,0:T(8,128)(2,1)S(1)}, u32[]{:S(2)}, u32[]{:S(2)}) collective-permute-start(bf16[192,512]{1,0:T(8,128)(2,1)S(1)} %get-tuple-element.49), channel_id=1, source_target_pairs={{0,3},{1,0},{2,1},{3,2},{4,7},{5,4},{6,5},{7,6},{8,11},{9,8},{10,9... | collective-permute-start | bytes 589832 | tf_op jit(solution)/shard_map/ppermute | solution.py:48
  49.6 15.2 %collective-permute-start.10 = (bf16[4,256,512]{2,1,0:T(8,128)(2,1)S(1)}, bf16[4,256,512]{2,1,0:T(8,128)(2,1)S(1)}, u32[]{:S(2)}, u32[]{:S(2)}) collective-permute-start(bf16[4,256,512]{2,1,0:T(8,128)(2,1)S(1)} %get-tuple-element.52.refs_4_), channel_id=1, source_target_pairs={{0,4},{1,5},{2,6},{3,7},{4,8},{5,9},{6,10},{7,11},{8,12},{9,13},{1... | collective-permute-start | bytes 3145736 | tf_op jit(solution)/shard_map/ppermute | solution.py:48
  50.9 13.9 %collective-permute-start.11 = (bf16[4,256,512]{2,1,0:T(8,128)(2,1)S(1)}, bf16[4,256,512]{2,1,0:T(8,128)(2,1)S(1)}, u32[]{:S(2)}, u32[]{:S(2)}) collective-permute-start(bf16[4,256,512]{2,1,0:T(8,128)(2,1)S(1)} %get-tuple-element.53), channel_id=1, source_target_pairs={{0,12},{1,13},{2,14},{3,15},{4,0},{5,1},{6,2},{7,3},{8,4},{9,5},{1... | collective-permute-start | bytes 3145736 | tf_op jit(solution)/shard_map/ppermute | solution.py:48
  53.6 16.8 %collective-permute-start.14 = (bf16[4,128,512]{2,1,0:T(8,128)(2,1)S(1)}, bf16[4,128,512]{2,1,0:T(8,128)(2,1)S(1)}, u32[]{:S(2)}, u32[]{:S(2)}) collective-permute-start(bf16[4,128,512]{2,1,0:T(8,128)(2,1)S(1)} %get-tuple-element.56.refs_4_), channel_id=1, source_target_pairs={{0,4},{1,5},{2,6},{3,7},{4,8},{5,9},{6,10},{7,11},{8,12},{9,13},{1... | collective-permute-start | bytes 1572872 | tf_op jit(solution)/shard_map/ppermute | solution.py:48
  54.5 15.9 %collective-permute-start.15 = (bf16[4,128,512]{2,1,0:T(8,128)(2,1)S(1)}, bf16[4,128,512]{2,1,0:T(8,128)(2,1)S(1)}, u32[]{:S(2)}, u32[]{:S(2)}) collective-permute-start(bf16[4,128,512]{2,1,0:T(8,128)(2,1)S(1)} %get-tuple-element.57), channel_id=1, source_target_pairs={{0,12},{1,13},{2,14},{3,15},{4,0},{5,1},{6,2},{7,3},{8,4},{9,5},{1... | collective-permute-start | bytes 1572872 | tf_op jit(solution)/shard_map/ppermute | solution.py:48
  70.8 13.8 %collective-permute-start.17 = (bf16[4,192,512]{2,1,0:T(8,128)(2,1)S(1)}, bf16[4,192,512]{2,1,0:T(8,128)(2,1)S(1)}, u32[]{:S(2)}, u32[]{:S(2)}) collective-permute-start(bf16[4,192,512]{2,1,0:T(8,128)(2,1)S(1)} %get-tuple-element.65), channel_id=1, source_target_pairs={{0,4},{1,5},{2,6},{3,7},{4,8},{5,9},{6,10},{7,11},{8,12},{9,13},{1... | collective-permute-start | bytes 2359304 | tf_op jit(solution)/shard_map/ppermute | solution.py:48
  72.2 12.5 %collective-permute-start.18 = (bf16[4,192,512]{2,1,0:T(8,128)(2,1)S(1)}, bf16[4,192,512]{2,1,0:T(8,128)(2,1)S(1)}, u32[]{:S(2)}, u32[]{:S(2)}) collective-permute-start(bf16[4,192,512]{2,1,0:T(8,128)(2,1)S(1)} %get-tuple-element.66), channel_id=1, source_target_pairs={{0,12},{1,13},{2,14},{3,15},{4,0},{5,1},{6,2},{7,3},{8,4},{9,5},{1... | collective-permute-start | bytes 2359304 | tf_op jit(solution)/shard_map/ppermute | solution.py:48
  73.6 9.9 %collective-permute-start.19 = (bf16[128,512]{1,0:T(8,128)(2,1)S(1)}, bf16[128,512]{1,0:T(8,128)(2,1)S(1)}, u32[]{:S(2)}, u32[]{:S(2)}) collective-permute-start(bf16[128,512]{1,0:T(8,128)(2,1)S(1)} %slice.26), channel_id=1, source_target_pairs={{2,19},{3,16},{6,23},{7,20},{10,27},{11,24},{14,31},{15,28},{16,17... | collective-permute-start | bytes 393224 | tf_op jit(solution)/shard_map/ppermute | solution.py:48
  85.2 8.2 %collective-permute-start.20 = (bf16[384,512]{1,0:T(8,128)(2,1)S(1)}, bf16[384,512]{1,0:T(8,128)(2,1)S(1)}, u32[]{:S(2)}, u32[]{:S(2)}) collective-permute-start(bf16[384,512]{1,0:T(8,128)(2,1)S(1)} %get-tuple-element.69), channel_id=1, source_target_pairs={{0,1},{1,2},{2,3},{3,0},{4,5},{5,6},{6,7},{7,4},{8,9},{9,10},{10,1... | collective-permute-start | bytes 1179656 | tf_op jit(solution)/shard_map/ppermute | solution.py:48
  86.2 10.7 %collective-permute-start.21 = (bf16[384,512]{1,0:T(8,128)(2,1)S(1)}, bf16[384,512]{1,0:T(8,128)(2,1)S(1)}, u32[]{:S(2)}, u32[]{:S(2)}) collective-permute-start(bf16[384,512]{1,0:T(8,128)(2,1)S(1)} %get-tuple-element.70), channel_id=1, source_target_pairs={{0,3},{1,0},{2,1},{3,2},{4,7},{5,4},{6,5},{7,6},{8,11},{9,8},{10,9... | collective-permute-start | bytes 1179656 | tf_op jit(solution)/shard_map/ppermute | solution.py:48
  87.9 10.7 %collective-permute-start.22 = (bf16[384,512]{1,0:T(8,128)(2,1)S(1)}, bf16[384,512]{1,0:T(8,128)(2,1)S(1)}, u32[]{:S(2)}, u32[]{:S(2)}) collective-permute-start(bf16[384,512]{1,0:T(8,128)(2,1)S(1)} %get-tuple-element.71), channel_id=1, source_target_pairs={{0,2},{1,3},{2,0},{3,1},{4,6},{5,7},{6,4},{7,5},{8,10},{9,11},{10,... | collective-permute-start | bytes 1179656 | tf_op jit(solution)/shard_map/ppermute | solution.py:48
  98.8 7.5 %collective-permute-start.23 = (bf16[128,512]{1,0:T(8,128)(2,1)S(1)}, bf16[128,512]{1,0:T(8,128)(2,1)S(1)}, u32[]{:S(2)}, u32[]{:S(2)}) collective-permute-start(bf16[128,512]{1,0:T(8,128)(2,1)S(1)} %get-tuple-element.85), channel_id=1, source_target_pairs={{0,96},{1,113},{2,115},{3,112},{4,100},{5,117},{6,119},{7,116},{8,... | collective-permute-start | bytes 393224 | tf_op jit(solution)/shard_map/ppermute | solution.py:48
  102.6 8.7 %collective-permute-start.24 = (bf16[128,512]{1,0:T(8,128)(2,1)S(1)}, bf16[128,512]{1,0:T(8,128)(2,1)S(1)}, u32[]{:S(2)}, u32[]{:S(2)}) collective-permute-start(bf16[128,512]{1,0:T(8,128)(2,1)S(1)} %get-tuple-element.86.refs_2_), channel_id=1, source_target_pairs={{0,64},{1,81},{2,83},{3,80},{4,68},{5,85},{6,87},{7,84},{8,72},{9,... | collective-permute-start | bytes 393224 | tf_op jit(solution)/shard_map/ppermute | solution.py:48
  103.1 9.8 %collective-permute-start.25 = (bf16[128,512]{1,0:T(8,128)(2,1)S(1)}, bf16[128,512]{1,0:T(8,128)(2,1)S(1)}, u32[]{:S(2)}, u32[]{:S(2)}) collective-permute-start(bf16[128,512]{1,0:T(8,128)(2,1)S(1)} %get-tuple-element.84), channel_id=1, source_target_pairs={{0,32},{1,49},{2,51},{3,48},{4,36},{5,53},{6,55},{7,52},{8,40},{9,... | collective-permute-start | bytes 393224 | tf_op jit(solution)/shard_map/ppermute | solution.py:48
  113.0 11.3 %collective-permute-start.26 = (bf16[256,512]{1,0:T(8,128)(2,1)S(1)}, bf16[256,512]{1,0:T(8,128)(2,1)S(1)}, u32[]{:S(2)}, u32[]{:S(2)}) collective-permute-start(bf16[256,512]{1,0:T(8,128)(2,1)S(1)} %get-tuple-element.74), channel_id=1, source_target_pairs={{0,4},{1,5},{2,6},{3,7},{4,8},{5,9},{6,10},{7,11},{8,12},{9,13},{1... | collective-permute-start | bytes 786440 | tf_op jit(solution)/shard_map/ppermute | solution.py:48
  114.0 13.0 %collective-permute-start.27 = (bf16[256,512]{1,0:T(8,128)(2,1)S(1)}, bf16[256,512]{1,0:T(8,128)(2,1)S(1)}, u32[]{:S(2)}, u32[]{:S(2)}) collective-permute-start(bf16[256,512]{1,0:T(8,128)(2,1)S(1)} %get-tuple-element.75), channel_id=1, source_target_pairs={{0,8},{1,9},{2,10},{3,11},{4,12},{5,13},{6,14},{7,15},{8,0},{9,1},... | collective-permute-start | bytes 786440 | tf_op jit(solution)/shard_map/ppermute | solution.py:48
  117.2 9.8 %collective-permute-start.28 = (bf16[256,512]{1,0:T(8,128)(2,1)S(1)}, bf16[256,512]{1,0:T(8,128)(2,1)S(1)}, u32[]{:S(2)}, u32[]{:S(2)}) collective-permute-start(bf16[256,512]{1,0:T(8,128)(2,1)S(1)} %get-tuple-element.76), channel_id=1, source_target_pairs={{0,12},{1,13},{2,14},{3,15},{4,0},{5,1},{6,2},{7,3},{8,4},{9,5},{1... | collective-permute-start | bytes 786440 | tf_op jit(solution)/shard_map/ppermute | solution.py:48
  (9 other events, 51.5 us)

commit v5 on v4

--- a/solution.py
+++ b/solution.py
@@ -176,14 +176,20 @@
     )
 
 
-def neighbours(above, below, after):
-    def kernel(above_ref, below_ref, far_ref, both_ref):
+def onward(above, below, after):
+    def kernel(above_ref, below_ref, far_ref):
         k = lax.axis_index("core")
+        far_ref[...] = jnp.where(k == 0, below_ref[...], above_ref[...])
+
+    return call(kernel, [array(*above.shape)], [above, below], after)[0]
+
+
+def together(above, below, after):
+    def kernel(above_ref, below_ref, both_ref):
         both_ref[0] = above_ref[...]
         both_ref[1] = below_ref[...]
-        far_ref[...] = jnp.where(k == 0, below_ref[...], above_ref[...])
-
-    return call(kernel, [array(*above.shape), array(2, *above.shape)], [above, below], after)
+
+    return call(kernel, [array(2, *above.shape)], [above, below], after)[0]
 
 
 def scatter(parts, stage):
@@ -356,9 +362,9 @@
 def on_device(gradient, stat_old, inv_root):
     Q = gradient.shape[0] // 8
 
-    partner = other_core(gradient)
     above = send(gradient, up(-1))
     below = send(gradient, up(1))
+    partner = other_core(gradient)
 
     tall = Q + Q // 2
     straight = [[[(r, 0, 0, tall)]] for r in range(N)]
@@ -379,8 +385,9 @@
     near_came = scatter(near, 0)
     product, token = multiply(inv_root, [gradient, partner], [(0, 0), (0, 1)], None, F32, [near[0]])
 
-    far, both = neighbours(above, below, [token, *near_came])
-    far = send(far, lambda z, k, x, y: (z + 1 - 2 * k, k, x, y))
+    passed = onward(above, below, [token])
+    both = together(above, below, [passed, *near_came])
+    far = send(passed, lambda z, k, x, y: (z + 1 - 2 * k, k, x, y))
     above_partner, below_partner = other_core(both)
     near = total(near_came, near[3], [both])
     near_came = scatter(near, 1)

time: 134 us -> 134 us (level)
    pallas_call x17 -> x18, Pallas kernels: 27.4 us -> 27.4 us  [call(): pl.pallas_call(body, out_shape=outs, in_specs=list(specs or [VMEM] * n) +...]
where the time goes in v5:
time: 134 us
  waiting for transfers between devices  53 us (40%)
  starting transfers between devices  50.8 us (38%)
  Pallas kernels  27.4 us (20%)
  local copies, waits for them, and re-layouts  1.49 us (1%)
    ppermute x30, waiting for transfers between devices, send(): lax.ppermute(value, AXES, [(source, linear(*to)) for source, to in pairs...  53 us
    ppermute x30, starting transfers between devices, send(): lax.ppermute(value, AXES, [(source, linear(*to)) for source, to in pairs...  50.8 us
    pallas_call x18, Pallas kernels, call(): pl.pallas_call(body, out_shape=outs, in_specs=list(specs or [VMEM] * n) +...  27.4 us
  transfers between devices with their start and end apart: 30, of which 19 were waited for; matrix products, arithmetic and copies ran while one was open for 0% of the time, Pallas kernels for 18%

profile of v5, /device:TPU:1, one launch (start us, length us, event | category | flops | bytes accessed | tf_op | source)
XLA Modules:
  0.0 133.5 jit_solution(16527711746692917301)
XLA Ops:
  2.1 3.9 %collective-permute-start.4 = (bf16[1024,512]{1,0:T(8,128)(2,1)}, bf16[1024,512]{1,0:T(8,128)(2,1)S(1)}, u32[]{:S(2)}, u32[]{:S(2)}) collective-permute-start(bf16[1024,512]{1,0:T(8,128)(2,1)} %refs_0_.10), channel_id=1, source_target_pairs={{0,96},{1,97},{2,98},{3,99},{4,100},{5,101},{6,102},{7,103},{8,104... | collective-permute-start | bytes 3145736 | tf_op jit(solution)/shard_map/ppermute | solution.py:48
  7.3 1.9 %shard_map.50 = (bf16[4,192,512]{2,1,0:T(8,128)(2,1)S(1)}, bf16[4,192,512]{2,1,0:T(8,128)(2,1)S(1)}, bf16[4,192,512]{2,1,0:T(8,128)(2,1)S(1)}, bf16[4,192,512]{2,1,0:T(8,128)(2,1)S(1)}) custom-call(bf16[1024,512]{1,0:T(8,128)(2,1)S(1)} %copy-done, bf16[1024,512]{1,0:T(8,128)(2,1)S(1)} %collective-permute-done.refs_1_.refs_3_.refs_2_, ...), custom_call_target="tpu_custom_call" | custom-call | flops 1 | bytes 1 | tf_op jit(solution)/shard_map/pallas_call | solution.py:69
  13.6 4.0 %shard_map.51 = (f32[1024,512]{1,0:T(8,128)S(1)}, f32[8,128]{1,0:T(8,128)S(1)}) custom-call(bf16[1024,8192]{1,0:T(8,128)(2,1)} %refs_0_.13, bf16[1024,512]{1,0:T(8,128)(2,1)S(1)} %copy-done.1, bf16[1024,512]{1,0:T(8,128)(2,1)S(1)} %collective-permute-done.refs_1_.refs_3_.refs_2_, bf16[4,192,512]{2,1,0:T(8,128)(2,1)S(1)} %get-tuple-element.40.refs_3_), custom_call_target="tpu_custom_call" | custom-call | flops 1 | bytes 1 | tf_op jit(solution)/shard_map/pallas_call | solution.py:69
  17.6 11.2 %collective-permute-done.4.refs_0_.refs_2_.refs_1_ = bf16[1024,512]{1,0:T(8,128)(2,1)S(1)} collective-permute-done((bf16[1024,512]{1,0:T(8,128)(2,1)}, bf16[1024,512]{1,0:T(8,128)(2,1)S(1)}, u32[]{:S(2)}, u32[]{:S(2)}) %collective-permute-start.4) | collective-permute-done | bytes 1048608 | tf_op jit(solution)/shard_map/ppermute | solution.py:48
  28.8 3.0 %collective-permute-done.5.refs_1_.refs_4_ = bf16[1024,512]{1,0:T(8,128)(2,1)S(1)} collective-permute-done((bf16[1024,512]{1,0:T(8,128)(2,1)}, bf16[1024,512]{1,0:T(8,128)(2,1)S(1)}, u32[]{:S(2)}, u32[]{:S(2)}) %collective-permute-start.5) | collective-permute-done | bytes 1048608 | tf_op jit(solution)/shard_map/ppermute | solution.py:48
  33.4 2.0 %collective-permute-start.12 = (bf16[1024,512]{1,0:T(8,128)(2,1)S(1)}, bf16[1024,512]{1,0:T(8,128)(2,1)S(1)}, u32[]{:S(2)}, u32[]{:S(2)}) collective-permute-start(bf16[1024,512]{1,0:T(8,128)(2,1)S(1)} %shard_map.52.refs_2_), channel_id=1, source_target_pairs={{0,32},{1,33},{2,34},{3,35},{4,36},{5,37},{6,38},{7,39},{8,40},{9,... | collective-permute-start | bytes 3145736 | tf_op jit(solution)/shard_map/ppermute | solution.py:48
  39.1 2.7 %shard_map.55 = (bf16[4,256,512]{2,1,0:T(8,128)(2,1)S(1)}, bf16[4,256,512]{2,1,0:T(8,128)(2,1)S(1)}, bf16[4,128,512]{2,1,0:T(8,128)(2,1)S(1)}, bf16[4,128,512]{2,1,0:T(8,128)(2,1)S(1)}, bf16[4,256,512]{2,1,0:T(8,128)(2,1)S(1)}) custom-call(bf16[1024,512]{1,0:T(8,128)(2,1)S(1)} %copy-done.1, ...), custom_call_target="tpu_custom_call" | custom-call | flops 1 | bytes 1 | tf_op jit(solution)/shard_map/pallas_call | solution.py:69
  44.6 2.7 %collective-permute-done.12.refs_0_ = bf16[1024,512]{1,0:T(8,128)(2,1)S(1)} collective-permute-done((bf16[1024,512]{1,0:T(8,128)(2,1)S(1)}, bf16[1024,512]{1,0:T(8,128)(2,1)S(1)}, u32[]{:S(2)}, u32[]{:S(2)}) %collective-permute-start.12) | collective-permute-done | bytes 1048608 | tf_op jit(solution)/shard_map/ppermute | solution.py:48
  47.4 2.2 %collective-permute-start.13 = (bf16[1024,512]{1,0:T(8,128)(2,1)S(1)}, bf16[1024,512]{1,0:T(8,128)(2,1)S(1)}, u32[]{:S(2)}, u32[]{:S(2)}) collective-permute-start(bf16[1024,512]{1,0:T(8,128)(2,1)S(1)} %shard_map.57.refs_2_.refs_1_), channel_id=1, source_target_pairs={{0,16},{1,17},{2,18},{3,19},{4,20},{5,21},{6,22},{7,23},{8,24},{9,... | collective-permute-start | bytes 3145736 | tf_op jit(solution)/shard_map/ppermute | solution.py:48
  56.4 3.0 %collective-permute-start.16 = (bf16[64,512]{1,0:T(8,128)(2,1)S(1)}, bf16[64,512]{1,0:T(8,128)(2,1)S(1)}, u32[]{:S(2)}, u32[]{:S(2)}) collective-permute-start(bf16[64,512]{1,0:T(8,128)(2,1)S(1)} %slice.25), channel_id=1, source_target_pairs={{16,0},{17,1},{18,2},{19,3},{20,4},{21,5},{22,6},{23,7},{24,8},{25... | collective-permute-start | bytes 196616 | tf_op jit(solution)/shard_map/ppermute | solution.py:48
  60.3 4.2 %shard_map.59 = (f32[1024,512]{1,0:T(8,128)S(1)}, f32[8,128]{1,0:T(8,128)S(1)}) custom-call(bf16[1024,8192]{1,0:T(8,128)(2,1)} %refs_0_.13, bf16[1024,512]{1,0:T(8,128)(2,1)S(1)} %shard_map.57.refs_2_.refs_1_, bf16[1024,512]{1,0:T(8,128)(2,1)S(1)} %collective-permute-done.13.refs_3_.refs_2_, f32[1024,512]{1,0:T(8,128)S(1)} %get-tuple-element.59.refs_3_, ...), custom_call_target="tpu_custom_call" | custom-call | flops 1 | bytes 1 | tf_op jit(solution)/shard_map/pallas_call | solution.py:69
  64.8 5.6 %collective-permute-done.14.refs_4_.refs_6_.refs_3_ = bf16[4,128,512]{2,1,0:T(8,128)(2,1)S(1)} collective-permute-done((bf16[4,128,512]{2,1,0:T(8,128)(2,1)S(1)}, bf16[4,128,512]{2,1,0:T(8,128)(2,1)S(1)}, u32[]{:S(2)}, u32[]{:S(2)}) %collective-permute-start.14) | collective-permute-done | bytes 524320 | tf_op jit(solution)/shard_map/ppermute | solution.py:48
  73.6 1.9 %collective-permute-start.19 = (bf16[128,512]{1,0:T(8,128)(2,1)S(1)}, bf16[128,512]{1,0:T(8,128)(2,1)S(1)}, u32[]{:S(2)}, u32[]{:S(2)}) collective-permute-start(bf16[128,512]{1,0:T(8,128)(2,1)S(1)} %slice.26), channel_id=1, source_target_pairs={{2,19},{3,16},{6,23},{7,20},{10,27},{11,24},{14,31},{15,28},{16,17... | collective-permute-start | bytes 393224 | tf_op jit(solution)/shard_map/ppermute | solution.py:48
  75.6 4.1 %shard_map.61 = (f32[1024,512]{1,0:T(8,128)S(1)}, f32[8,128]{1,0:T(8,128)S(1)}) custom-call(bf16[1024,8192]{1,0:T(8,128)(2,1)} %refs_0_.13, bf16[1024,512]{1,0:T(8,128)(2,1)S(1)} %collective-permute-done.4.refs_0_.refs_2_.refs_1_, bf16[1024,512]{1,0:T(8,128)(2,1)S(1)} %get-tuple-element.79.refs_3_.refs_2_, f32[1024,512]{1,0:T(8,128)S(1)} %get-tuple-element.63.refs_3_, ...), custom_call_target="tpu_custom_call" | custom-call | flops 1 | bytes 1 | tf_op jit(solution)/shard_map/pallas_call | solution.py:69
  79.7 3.9 %collective-permute-done.19.refs_9_.refs_3_ = bf16[128,512]{1,0:T(8,128)(2,1)S(1)} collective-permute-done((bf16[128,512]{1,0:T(8,128)(2,1)S(1)}, bf16[128,512]{1,0:T(8,128)(2,1)S(1)}, u32[]{:S(2)}, u32[]{:S(2)}) %collective-permute-start.19) | collective-permute-done | bytes 131104 | tf_op jit(solution)/shard_map/ppermute | solution.py:48
  89.2 4.2 %collective-permute-done.20.refs_0_ = bf16[384,512]{1,0:T(8,128)(2,1)S(1)} collective-permute-done((bf16[384,512]{1,0:T(8,128)(2,1)S(1)}, bf16[384,512]{1,0:T(8,128)(2,1)S(1)}, u32[]{:S(2)}, u32[]{:S(2)}) %collective-permute-start.20) | collective-permute-done | bytes 393248 | tf_op jit(solution)/shard_map/ppermute | solution.py:48
  93.4 3.5 %collective-permute-done.21.refs_1_ = bf16[384,512]{1,0:T(8,128)(2,1)S(1)} collective-permute-done((bf16[384,512]{1,0:T(8,128)(2,1)S(1)}, bf16[384,512]{1,0:T(8,128)(2,1)S(1)}, u32[]{:S(2)}, u32[]{:S(2)}) %collective-permute-start.21) | collective-permute-done | bytes 393248 | tf_op jit(solution)/shard_map/ppermute | solution.py:48
  98.8 3.6 %collective-permute-start.23 = (bf16[128,512]{1,0:T(8,128)(2,1)S(1)}, bf16[128,512]{1,0:T(8,128)(2,1)S(1)}, u32[]{:S(2)}, u32[]{:S(2)}) collective-permute-start(bf16[128,512]{1,0:T(8,128)(2,1)S(1)} %get-tuple-element.81), channel_id=1, source_target_pairs={{0,96},{1,113},{2,115},{3,112},{4,100},{5,117},{6,119},{7,116},{8,... | collective-permute-start | bytes 393224 | tf_op jit(solution)/shard_map/ppermute | solution.py:48
  104.3 2.1 %collective-permute-done.23.refs_4_ = bf16[128,512]{1,0:T(8,128)(2,1)S(1)} collective-permute-done((bf16[128,512]{1,0:T(8,128)(2,1)S(1)}, bf16[128,512]{1,0:T(8,128)(2,1)S(1)}, u32[]{:S(2)}, u32[]{:S(2)}) %collective-permute-start.23) | collective-permute-done | bytes 131104 | tf_op jit(solution)/shard_map/ppermute | solution.py:48
  106.3 4.6 %collective-permute-done.24.refs_5_ = bf16[128,512]{1,0:T(8,128)(2,1)S(1)} collective-permute-done((bf16[128,512]{1,0:T(8,128)(2,1)S(1)}, bf16[128,512]{1,0:T(8,128)(2,1)S(1)}, u32[]{:S(2)}, u32[]{:S(2)}) %collective-permute-start.24) | collective-permute-done | bytes 131104 | tf_op jit(solution)/shard_map/ppermute | solution.py:48
  113.9 3.2 %collective-permute-start.27 = (bf16[256,512]{1,0:T(8,128)(2,1)S(1)}, bf16[256,512]{1,0:T(8,128)(2,1)S(1)}, u32[]{:S(2)}, u32[]{:S(2)}) collective-permute-start(bf16[256,512]{1,0:T(8,128)(2,1)S(1)} %get-tuple-element.71), channel_id=1, source_target_pairs={{0,8},{1,9},{2,10},{3,11},{4,12},{5,13},{6,14},{7,15},{8,0},{9,1},... | collective-permute-start | bytes 786440 | tf_op jit(solution)/shard_map/ppermute | solution.py:48
  119.0 5.2 %shard_map.65 = (bf16[1024,512]{1,0:T(8,128)(2,1)}, f32[8,128]{1,0:T(8,128)S(1)}) custom-call(bf16[1024,8192]{1,0:T(8,128)(2,1)} %refs_0_.13, bf16[1024,512]{1,0:T(8,128)(2,1)S(1)} %collective-permute-done.5.refs_1_.refs_4_, bf16[1024,512]{1,0:T(8,128)(2,1)S(1)} %get-tuple-element.78.refs_5_.refs_2_, f32[1024,512]{1,0:T(8,128)S(1)} %get-tuple-element.73.refs_3_, ...), custom_call_target="tpu_custom_call" | custom-call | flops 1 | bytes 1 | tf_op jit(solution)/shard_map/pallas_call | solution.py:69
  124.2 2.3 %collective-permute-done.27.refs_2_ = bf16[256,512]{1,0:T(8,128)(2,1)S(1)} collective-permute-done((bf16[256,512]{1,0:T(8,128)(2,1)S(1)}, bf16[256,512]{1,0:T(8,128)(2,1)S(1)}, u32[]{:S(2)}, u32[]{:S(2)}) %collective-permute-start.27) | collective-permute-done | bytes 262176 | tf_op jit(solution)/shard_map/ppermute | solution.py:48
  126.6 3.6 %collective-permute-start.29 = (bf16[512,512]{1,0:T(8,128)(2,1)S(1)}, bf16[512,512]{1,0:T(8,128)(2,1)S(1)}, u32[]{:S(2)}, u32[]{:S(2)}) collective-permute-start(bf16[512,512]{1,0:T(8,128)(2,1)S(1)} %get-tuple-element.76), channel_id=1, source_target_pairs={{0,16},{1,17},{2,18},{3,19},{4,20},{5,21},{6,22},{7,23},{8,24},{9,... | collective-permute-start | bytes 1572872 | tf_op jit(solution)/shard_map/ppermute | solution.py:48
  (65 shorter events, 44.2 us)
Async XLA Ops:
  2.1 26.7 %collective-permute-start.4 = (bf16[1024,512]{1,0:T(8,128)(2,1)}, bf16[1024,512]{1,0:T(8,128)(2,1)S(1)}, u32[]{:S(2)}, u32[]{:S(2)}) collective-permute-start(bf16[1024,512]{1,0:T(8,128)(2,1)} %refs_0_.10), channel_id=1, source_target_pairs={{0,96},{1,97},{2,98},{3,99},{4,100},{5,101},{6,102},{7,103},{8,104... | collective-permute-start | bytes 3145736 | tf_op jit(solution)/shard_map/ppermute | solution.py:48
  6.0 25.8 %collective-permute-start.5 = (bf16[1024,512]{1,0:T(8,128)(2,1)}, bf16[1024,512]{1,0:T(8,128)(2,1)S(1)}, u32[]{:S(2)}, u32[]{:S(2)}) collective-permute-start(bf16[1024,512]{1,0:T(8,128)(2,1)} %refs_0_.10), channel_id=1, source_target_pairs={{0,32},{1,33},{2,34},{3,35},{4,36},{5,37},{6,38},{7,39},{8,40},{9,... | collective-permute-start | bytes 3145736 | tf_op jit(solution)/shard_map/ppermute | solution.py:48
  9.2 22.8 %collective-permute-start.1 = (bf16[4,192,512]{2,1,0:T(8,128)(2,1)S(1)}, bf16[4,192,512]{2,1,0:T(8,128)(2,1)S(1)}, u32[]{:S(2)}, u32[]{:S(2)}) collective-permute-start(bf16[4,192,512]{2,1,0:T(8,128)(2,1)S(1)} %get-tuple-element.40.refs_3_), channel_id=1, source_target_pairs={{0,4},{1,5},{2,6},{3,7},{4,8},{5,9},{6,10},{7,11},{8,12},{9,13},{1... | collective-permute-start | bytes 2359304 | tf_op jit(solution)/shard_map/ppermute | solution.py:48
  10.5 21.4 %collective-permute-start.2 = (bf16[4,192,512]{2,1,0:T(8,128)(2,1)S(1)}, bf16[4,192,512]{2,1,0:T(8,128)(2,1)S(1)}, u32[]{:S(2)}, u32[]{:S(2)}) collective-permute-start(bf16[4,192,512]{2,1,0:T(8,128)(2,1)S(1)} %get-tuple-element.41), channel_id=1, source_target_pairs={{0,12},{1,13},{2,14},{3,15},{4,0},{5,1},{6,2},{7,3},{8,4},{9,5},{1... | collective-permute-start | bytes 2359304 | tf_op jit(solution)/shard_map/ppermute | solution.py:48
  12.0 19.9 %collective-permute-start.3 = (bf16[4,192,512]{2,1,0:T(8,128)(2,1)S(1)}, bf16[4,192,512]{2,1,0:T(8,128)(2,1)S(1)}, u32[]{:S(2)}, u32[]{:S(2)}) collective-permute-start(bf16[4,192,512]{2,1,0:T(8,128)(2,1)S(1)} %get-tuple-element.42), channel_id=1, source_target_pairs={{0,8},{1,9},{2,10},{3,11},{4,12},{5,13},{6,14},{7,15},{8,0},{9,1},... | collective-permute-start | bytes 2359304 | tf_op jit(solution)/shard_map/ppermute | solution.py:48
  32.1 6.8 %collective-permute-start.9 = (bf16[2,1024,512]{2,1,0:T(8,128)(2,1)S(1)}, bf16[2,1024,512]{2,1,0:T(8,128)(2,1)S(1)}, u32[]{:S(2)}, u32[]{:S(2)}) collective-permute-start(bf16[2,1024,512]{2,1,0:T(8,128)(2,1)S(1)} %shard_map.53.refs_4_), channel_id=1, source_target_pairs={{0,16},{1,17},{2,18},{3,19},{4,20},{5,21},{6,22},{7,23},{8,24},{9,... | collective-permute-start | bytes 6291464 | tf_op jit(solution)/shard_map/ppermute | solution.py:48
  33.4 13.9 %collective-permute-start.12 = (bf16[1024,512]{1,0:T(8,128)(2,1)S(1)}, bf16[1024,512]{1,0:T(8,128)(2,1)S(1)}, u32[]{:S(2)}, u32[]{:S(2)}) collective-permute-start(bf16[1024,512]{1,0:T(8,128)(2,1)S(1)} %shard_map.52.refs_2_), channel_id=1, source_target_pairs={{0,32},{1,33},{2,34},{3,35},{4,36},{5,37},{6,38},{7,39},{8,40},{9,... | collective-permute-start | bytes 3145736 | tf_op jit(solution)/shard_map/ppermute | solution.py:48
  36.9 6.3 %collective-permute-start.7 = (bf16[192,512]{1,0:T(8,128)(2,1)S(1)}, bf16[192,512]{1,0:T(8,128)(2,1)S(1)}, u32[]{:S(2)}, u32[]{:S(2)}) collective-permute-start(bf16[192,512]{1,0:T(8,128)(2,1)S(1)} %get-tuple-element.46), channel_id=1, source_target_pairs={{0,3},{1,0},{2,1},{3,2},{4,7},{5,4},{6,5},{7,6},{8,11},{9,8},{10,9... | collective-permute-start | bytes 589832 | tf_op jit(solution)/shard_map/ppermute | solution.py:48
  49.6 15.2 %collective-permute-start.10 = (bf16[4,256,512]{2,1,0:T(8,128)(2,1)S(1)}, bf16[4,256,512]{2,1,0:T(8,128)(2,1)S(1)}, u32[]{:S(2)}, u32[]{:S(2)}) collective-permute-start(bf16[4,256,512]{2,1,0:T(8,128)(2,1)S(1)} %get-tuple-element.49.refs_4_), channel_id=1, source_target_pairs={{0,4},{1,5},{2,6},{3,7},{4,8},{5,9},{6,10},{7,11},{8,12},{9,13},{1... | collective-permute-start | bytes 3145736 | tf_op jit(solution)/shard_map/ppermute | solution.py:48
  50.9 13.9 %collective-permute-start.11 = (bf16[4,256,512]{2,1,0:T(8,128)(2,1)S(1)}, bf16[4,256,512]{2,1,0:T(8,128)(2,1)S(1)}, u32[]{:S(2)}, u32[]{:S(2)}) collective-permute-start(bf16[4,256,512]{2,1,0:T(8,128)(2,1)S(1)} %get-tuple-element.50), channel_id=1, source_target_pairs={{0,12},{1,13},{2,14},{3,15},{4,0},{5,1},{6,2},{7,3},{8,4},{9,5},{1... | collective-permute-start | bytes 3145736 | tf_op jit(solution)/shard_map/ppermute | solution.py:48
  53.7 16.8 %collective-permute-start.14 = (bf16[4,128,512]{2,1,0:T(8,128)(2,1)S(1)}, bf16[4,128,512]{2,1,0:T(8,128)(2,1)S(1)}, u32[]{:S(2)}, u32[]{:S(2)}) collective-permute-start(bf16[4,128,512]{2,1,0:T(8,128)(2,1)S(1)} %get-tuple-element.52.refs_4_), channel_id=1, source_target_pairs={{0,4},{1,5},{2,6},{3,7},{4,8},{5,9},{6,10},{7,11},{8,12},{9,13},{1... | collective-permute-start | bytes 1572872 | tf_op jit(solution)/shard_map/ppermute | solution.py:48
  54.6 15.9 %collective-permute-start.15 = (bf16[4,128,512]{2,1,0:T(8,128)(2,1)S(1)}, bf16[4,128,512]{2,1,0:T(8,128)(2,1)S(1)}, u32[]{:S(2)}, u32[]{:S(2)}) collective-permute-start(bf16[4,128,512]{2,1,0:T(8,128)(2,1)S(1)} %get-tuple-element.53), channel_id=1, source_target_pairs={{0,12},{1,13},{2,14},{3,15},{4,0},{5,1},{6,2},{7,3},{8,4},{9,5},{1... | collective-permute-start | bytes 1572872 | tf_op jit(solution)/shard_map/ppermute | solution.py:48
  70.8 13.8 %collective-permute-start.17 = (bf16[4,192,512]{2,1,0:T(8,128)(2,1)S(1)}, bf16[4,192,512]{2,1,0:T(8,128)(2,1)S(1)}, u32[]{:S(2)}, u32[]{:S(2)}) collective-permute-start(bf16[4,192,512]{2,1,0:T(8,128)(2,1)S(1)} %get-tuple-element.61), channel_id=1, source_target_pairs={{0,4},{1,5},{2,6},{3,7},{4,8},{5,9},{6,10},{7,11},{8,12},{9,13},{1... | collective-permute-start | bytes 2359304 | tf_op jit(solution)/shard_map/ppermute | solution.py:48
  72.2 12.5 %collective-permute-start.18 = (bf16[4,192,512]{2,1,0:T(8,128)(2,1)S(1)}, bf16[4,192,512]{2,1,0:T(8,128)(2,1)S(1)}, u32[]{:S(2)}, u32[]{:S(2)}) collective-permute-start(bf16[4,192,512]{2,1,0:T(8,128)(2,1)S(1)} %get-tuple-element.62), channel_id=1, source_target_pairs={{0,12},{1,13},{2,14},{3,15},{4,0},{5,1},{6,2},{7,3},{8,4},{9,5},{1... | collective-permute-start | bytes 2359304 | tf_op jit(solution)/shard_map/ppermute | solution.py:48
  73.6 9.9 %collective-permute-start.19 = (bf16[128,512]{1,0:T(8,128)(2,1)S(1)}, bf16[128,512]{1,0:T(8,128)(2,1)S(1)}, u32[]{:S(2)}, u32[]{:S(2)}) collective-permute-start(bf16[128,512]{1,0:T(8,128)(2,1)S(1)} %slice.26), channel_id=1, source_target_pairs={{2,19},{3,16},{6,23},{7,20},{10,27},{11,24},{14,31},{15,28},{16,17... | collective-permute-start | bytes 393224 | tf_op jit(solution)/shard_map/ppermute | solution.py:48
  85.2 8.2 %collective-permute-start.20 = (bf16[384,512]{1,0:T(8,128)(2,1)S(1)}, bf16[384,512]{1,0:T(8,128)(2,1)S(1)}, u32[]{:S(2)}, u32[]{:S(2)}) collective-permute-start(bf16[384,512]{1,0:T(8,128)(2,1)S(1)} %get-tuple-element.65), channel_id=1, source_target_pairs={{0,1},{1,2},{2,3},{3,0},{4,5},{5,6},{6,7},{7,4},{8,9},{9,10},{10,1... | collective-permute-start | bytes 1179656 | tf_op jit(solution)/shard_map/ppermute | solution.py:48
  86.2 10.7 %collective-permute-start.21 = (bf16[384,512]{1,0:T(8,128)(2,1)S(1)}, bf16[384,512]{1,0:T(8,128)(2,1)S(1)}, u32[]{:S(2)}, u32[]{:S(2)}) collective-permute-start(bf16[384,512]{1,0:T(8,128)(2,1)S(1)} %get-tuple-element.66), channel_id=1, source_target_pairs={{0,3},{1,0},{2,1},{3,2},{4,7},{5,4},{6,5},{7,6},{8,11},{9,8},{10,9... | collective-permute-start | bytes 1179656 | tf_op jit(solution)/shard_map/ppermute | solution.py:48
  88.0 10.7 %collective-permute-start.22 = (bf16[384,512]{1,0:T(8,128)(2,1)S(1)}, bf16[384,512]{1,0:T(8,128)(2,1)S(1)}, u32[]{:S(2)}, u32[]{:S(2)}) collective-permute-start(bf16[384,512]{1,0:T(8,128)(2,1)S(1)} %get-tuple-element.67), channel_id=1, source_target_pairs={{0,2},{1,3},{2,0},{3,1},{4,6},{5,7},{6,4},{7,5},{8,10},{9,11},{10,... | collective-permute-start | bytes 1179656 | tf_op jit(solution)/shard_map/ppermute | solution.py:48
  98.8 7.5 %collective-permute-start.23 = (bf16[128,512]{1,0:T(8,128)(2,1)S(1)}, bf16[128,512]{1,0:T(8,128)(2,1)S(1)}, u32[]{:S(2)}, u32[]{:S(2)}) collective-permute-start(bf16[128,512]{1,0:T(8,128)(2,1)S(1)} %get-tuple-element.81), channel_id=1, source_target_pairs={{0,96},{1,113},{2,115},{3,112},{4,100},{5,117},{6,119},{7,116},{8,... | collective-permute-start | bytes 393224 | tf_op jit(solution)/shard_map/ppermute | solution.py:48
  102.5 8.5 %collective-permute-start.24 = (bf16[128,512]{1,0:T(8,128)(2,1)S(1)}, bf16[128,512]{1,0:T(8,128)(2,1)S(1)}, u32[]{:S(2)}, u32[]{:S(2)}) collective-permute-start(bf16[128,512]{1,0:T(8,128)(2,1)S(1)} %get-tuple-element.82.refs_2_), channel_id=1, source_target_pairs={{0,64},{1,81},{2,83},{3,80},{4,68},{5,85},{6,87},{7,84},{8,72},{9,... | collective-permute-start | bytes 393224 | tf_op jit(solution)/shard_map/ppermute | solution.py:48
  103.1 9.7 %collective-permute-start.25 = (bf16[128,512]{1,0:T(8,128)(2,1)S(1)}, bf16[128,512]{1,0:T(8,128)(2,1)S(1)}, u32[]{:S(2)}, u32[]{:S(2)}) collective-permute-start(bf16[128,512]{1,0:T(8,128)(2,1)S(1)} %get-tuple-element.80), channel_id=1, source_target_pairs={{0,32},{1,49},{2,51},{3,48},{4,36},{5,53},{6,55},{7,52},{8,40},{9,... | collective-permute-start | bytes 393224 | tf_op jit(solution)/shard_map/ppermute | solution.py:48
  112.9 11.3 %collective-permute-start.26 = (bf16[256,512]{1,0:T(8,128)(2,1)S(1)}, bf16[256,512]{1,0:T(8,128)(2,1)S(1)}, u32[]{:S(2)}, u32[]{:S(2)}) collective-permute-start(bf16[256,512]{1,0:T(8,128)(2,1)S(1)} %get-tuple-element.70), channel_id=1, source_target_pairs={{0,4},{1,5},{2,6},{3,7},{4,8},{5,9},{6,10},{7,11},{8,12},{9,13},{1... | collective-permute-start | bytes 786440 | tf_op jit(solution)/shard_map/ppermute | solution.py:48
  113.9 12.5 %collective-permute-start.27 = (bf16[256,512]{1,0:T(8,128)(2,1)S(1)}, bf16[256,512]{1,0:T(8,128)(2,1)S(1)}, u32[]{:S(2)}, u32[]{:S(2)}) collective-permute-start(bf16[256,512]{1,0:T(8,128)(2,1)S(1)} %get-tuple-element.71), channel_id=1, source_target_pairs={{0,8},{1,9},{2,10},{3,11},{4,12},{5,13},{6,14},{7,15},{8,0},{9,1},... | collective-permute-start | bytes 786440 | tf_op jit(solution)/shard_map/ppermute | solution.py:48
  117.1 9.4 %collective-permute-start.28 = (bf16[256,512]{1,0:T(8,128)(2,1)S(1)}, bf16[256,512]{1,0:T(8,128)(2,1)S(1)}, u32[]{:S(2)}, u32[]{:S(2)}) collective-permute-start(bf16[256,512]{1,0:T(8,128)(2,1)S(1)} %get-tuple-element.72), channel_id=1, source_target_pairs={{0,12},{1,13},{2,14},{3,15},{4,0},{5,1},{6,2},{7,3},{8,4},{9,5},{1... | collective-permute-start | bytes 786440 | tf_op jit(solution)/shard_map/ppermute | solution.py:48
  (9 other events, 51.9 us)

commit v6 on v5

--- a/solution.py
+++ b/solution.py
@@ -196,7 +196,8 @@
     def where(z, k, x, y, n):
         return (z, k, x + n, y) if k == stage else (z, k, x, y + n)
 
-    return [send(parts[r], functools.partial(where, n=OFFSETS[r])) for r in range(N - 1)]
+    came = {r: send(parts[r], functools.partial(where, n=OFFSETS[r])) for r in (2, 0, 1)}
+    return [came[r] for r in range(N - 1)]
 
 
 def total(got, own, after=()):
@@ -420,13 +421,11 @@
     rest = last_step(came, own, far_came, far_own, came_again, [token, mirrored[0]])
     (rest,) = total(scatter(rest, 1), rest[3])
 
-    mirrored += [
-        send(rest[Q : 2 * Q], mirror(3)),
-        send(rest[2 * Q :], mirror(2)),
-        send(rest[:Q], mirror(1)),
-    ]
+    from_far = send(rest[2 * Q :], mirror(2))
+    mirrored += [send(rest[Q : 2 * Q], mirror(3)), from_far, send(rest[:Q], mirror(1))]
     out = messages(near, rest[: 2 * Q], rest[2 * Q :], mirrored, other_half)
-    got = [out[0]] + [send(out[d], lambda z, k, x, y, d=d: (z, k, x + d, y)) for d in range(1, N)]
+    came = {d: send(out[d], lambda z, k, x, y, d=d: (z, k, x + d, y)) for d in (2, 1, 3)}
+    got = [out[0]] + [came[d] for d in range(1, N)]
     product, token = multiply(inv_root, [below, below_partner], [(3, 0), (3, 1)], product, BF16, [out[0]])
     both, wanted = gathered(got, [token])
     return finish(both, other_core(wanted), stat_old), product

time: 134 us -> 134 us (level)
  no operation moved by 1% of the time
where the time goes in v6:
time: 134 us
  waiting for transfers between devices  53 us (40%)
  starting transfers between devices  50.8 us (38%)
  Pallas kernels  27.4 us (20%)
  local copies, waits for them, and re-layouts  1.49 us (1%)
    ppermute x30, waiting for transfers between devices, send(): lax.ppermute(value, AXES, [(source, linear(*to)) for source, to in pairs...  53 us
    ppermute x30, starting transfers between devices, send(): lax.ppermute(value, AXES, [(source, linear(*to)) for source, to in pairs...  50.8 us
    pallas_call x18, Pallas kernels, call(): pl.pallas_call(body, out_shape=outs, in_specs=list(specs or [VMEM] * n) +...  27.4 us
  transfers between devices with their start and end apart: 30, of which 19 were waited for; matrix products, arithmetic and copies ran while one was open for 0% of the time, Pallas kernels for 18%

profile of v6, /device:TPU:1, one launch (start us, length us, event | category | flops | bytes accessed | tf_op | source)
XLA Modules:
  0.0 133.5 jit_solution(16527711746692917301)
XLA Ops:
  2.1 3.9 %collective-permute-start.4 = (bf16[1024,512]{1,0:T(8,128)(2,1)}, bf16[1024,512]{1,0:T(8,128)(2,1)S(1)}, u32[]{:S(2)}, u32[]{:S(2)}) collective-permute-start(bf16[1024,512]{1,0:T(8,128)(2,1)} %refs_0_.10), channel_id=1, source_target_pairs={{0,96},{1,97},{2,98},{3,99},{4,100},{5,101},{6,102},{7,103},{8,104... | collective-permute-start | bytes 3145736 | tf_op jit(solution)/shard_map/ppermute | solution.py:48
  7.3 1.9 %shard_map.50 = (bf16[4,192,512]{2,1,0:T(8,128)(2,1)S(1)}, bf16[4,192,512]{2,1,0:T(8,128)(2,1)S(1)}, bf16[4,192,512]{2,1,0:T(8,128)(2,1)S(1)}, bf16[4,192,512]{2,1,0:T(8,128)(2,1)S(1)}) custom-call(bf16[1024,512]{1,0:T(8,128)(2,1)S(1)} %copy-done, bf16[1024,512]{1,0:T(8,128)(2,1)S(1)} %collective-permute-done.refs_1_.refs_3_.refs_2_, ...), custom_call_target="tpu_custom_call" | custom-call | flops 1 | bytes 1 | tf_op jit(solution)/shard_map/pallas_call | solution.py:69
  13.6 4.0 %shard_map.51 = (f32[1024,512]{1,0:T(8,128)S(1)}, f32[8,128]{1,0:T(8,128)S(1)}) custom-call(bf16[1024,8192]{1,0:T(8,128)(2,1)} %refs_0_.13, bf16[1024,512]{1,0:T(8,128)(2,1)S(1)} %copy-done.1, bf16[1024,512]{1,0:T(8,128)(2,1)S(1)} %collective-permute-done.refs_1_.refs_3_.refs_2_, bf16[4,192,512]{2,1,0:T(8,128)(2,1)S(1)} %get-tuple-element.40.refs_3_), custom_call_target="tpu_custom_call" | custom-call | flops 1 | bytes 1 | tf_op jit(solution)/shard_map/pallas_call | solution.py:69
  17.6 11.2 %collective-permute-done.4.refs_0_.refs_2_.refs_1_ = bf16[1024,512]{1,0:T(8,128)(2,1)S(1)} collective-permute-done((bf16[1024,512]{1,0:T(8,128)(2,1)}, bf16[1024,512]{1,0:T(8,128)(2,1)S(1)}, u32[]{:S(2)}, u32[]{:S(2)}) %collective-permute-start.4) | collective-permute-done | bytes 1048608 | tf_op jit(solution)/shard_map/ppermute | solution.py:48
  28.8 3.0 %collective-permute-done.5.refs_1_.refs_4_ = bf16[1024,512]{1,0:T(8,128)(2,1)S(1)} collective-permute-done((bf16[1024,512]{1,0:T(8,128)(2,1)}, bf16[1024,512]{1,0:T(8,128)(2,1)S(1)}, u32[]{:S(2)}, u32[]{:S(2)}) %collective-permute-start.5) | collective-permute-done | bytes 1048608 | tf_op jit(solution)/shard_map/ppermute | solution.py:48
  33.4 2.0 %collective-permute-start.12 = (bf16[1024,512]{1,0:T(8,128)(2,1)S(1)}, bf16[1024,512]{1,0:T(8,128)(2,1)S(1)}, u32[]{:S(2)}, u32[]{:S(2)}) collective-permute-start(bf16[1024,512]{1,0:T(8,128)(2,1)S(1)} %shard_map.52.refs_2_), channel_id=1, source_target_pairs={{0,32},{1,33},{2,34},{3,35},{4,36},{5,37},{6,38},{7,39},{8,40},{9,... | collective-permute-start | bytes 3145736 | tf_op jit(solution)/shard_map/ppermute | solution.py:48
  39.1 2.7 %shard_map.55 = (bf16[4,256,512]{2,1,0:T(8,128)(2,1)S(1)}, bf16[4,256,512]{2,1,0:T(8,128)(2,1)S(1)}, bf16[4,128,512]{2,1,0:T(8,128)(2,1)S(1)}, bf16[4,128,512]{2,1,0:T(8,128)(2,1)S(1)}, bf16[4,256,512]{2,1,0:T(8,128)(2,1)S(1)}) custom-call(bf16[1024,512]{1,0:T(8,128)(2,1)S(1)} %copy-done.1, ...), custom_call_target="tpu_custom_call" | custom-call | flops 1 | bytes 1 | tf_op jit(solution)/shard_map/pallas_call | solution.py:69
  44.6 2.7 %collective-permute-done.12.refs_0_ = bf16[1024,512]{1,0:T(8,128)(2,1)S(1)} collective-permute-done((bf16[1024,512]{1,0:T(8,128)(2,1)S(1)}, bf16[1024,512]{1,0:T(8,128)(2,1)S(1)}, u32[]{:S(2)}, u32[]{:S(2)}) %collective-permute-start.12) | collective-permute-done | bytes 1048608 | tf_op jit(solution)/shard_map/ppermute | solution.py:48
  47.4 2.2 %collective-permute-start.13 = (bf16[1024,512]{1,0:T(8,128)(2,1)S(1)}, bf16[1024,512]{1,0:T(8,128)(2,1)S(1)}, u32[]{:S(2)}, u32[]{:S(2)}) collective-permute-start(bf16[1024,512]{1,0:T(8,128)(2,1)S(1)} %shard_map.57.refs_2_.refs_1_), channel_id=1, source_target_pairs={{0,16},{1,17},{2,18},{3,19},{4,20},{5,21},{6,22},{7,23},{8,24},{9,... | collective-permute-start | bytes 3145736 | tf_op jit(solution)/shard_map/ppermute | solution.py:48
  56.4 3.0 %collective-permute-start.16 = (bf16[64,512]{1,0:T(8,128)(2,1)S(1)}, bf16[64,512]{1,0:T(8,128)(2,1)S(1)}, u32[]{:S(2)}, u32[]{:S(2)}) collective-permute-start(bf16[64,512]{1,0:T(8,128)(2,1)S(1)} %slice.25), channel_id=1, source_target_pairs={{16,0},{17,1},{18,2},{19,3},{20,4},{21,5},{22,6},{23,7},{24,8},{25... | collective-permute-start | bytes 196616 | tf_op jit(solution)/shard_map/ppermute | solution.py:48
  60.3 4.2 %shard_map.59 = (f32[1024,512]{1,0:T(8,128)S(1)}, f32[8,128]{1,0:T(8,128)S(1)}) custom-call(bf16[1024,8192]{1,0:T(8,128)(2,1)} %refs_0_.13, bf16[1024,512]{1,0:T(8,128)(2,1)S(1)} %shard_map.57.refs_2_.refs_1_, bf16[1024,512]{1,0:T(8,128)(2,1)S(1)} %collective-permute-done.13.refs_3_.refs_2_, f32[1024,512]{1,0:T(8,128)S(1)} %get-tuple-element.59.refs_3_, ...), custom_call_target="tpu_custom_call" | custom-call | flops 1 | bytes 1 | tf_op jit(solution)/shard_map/pallas_call | solution.py:69
  64.8 5.6 %collective-permute-done.14.refs_4_.refs_6_.refs_3_ = bf16[4,128,512]{2,1,0:T(8,128)(2,1)S(1)} collective-permute-done((bf16[4,128,512]{2,1,0:T(8,128)(2,1)S(1)}, bf16[4,128,512]{2,1,0:T(8,128)(2,1)S(1)}, u32[]{:S(2)}, u32[]{:S(2)}) %collective-permute-start.14) | collective-permute-done | bytes 524320 | tf_op jit(solution)/shard_map/ppermute | solution.py:48
  73.6 1.9 %collective-permute-start.19 = (bf16[128,512]{1,0:T(8,128)(2,1)S(1)}, bf16[128,512]{1,0:T(8,128)(2,1)S(1)}, u32[]{:S(2)}, u32[]{:S(2)}) collective-permute-start(bf16[128,512]{1,0:T(8,128)(2,1)S(1)} %slice.26), channel_id=1, source_target_pairs={{2,19},{3,16},{6,23},{7,20},{10,27},{11,24},{14,31},{15,28},{16,17... | collective-permute-start | bytes 393224 | tf_op jit(solution)/shard_map/ppermute | solution.py:48
  75.6 4.1 %shard_map.61 = (f32[1024,512]{1,0:T(8,128)S(1)}, f32[8,128]{1,0:T(8,128)S(1)}) custom-call(bf16[1024,8192]{1,0:T(8,128)(2,1)} %refs_0_.13, bf16[1024,512]{1,0:T(8,128)(2,1)S(1)} %collective-permute-done.4.refs_0_.refs_2_.refs_1_, bf16[1024,512]{1,0:T(8,128)(2,1)S(1)} %get-tuple-element.79.refs_3_.refs_2_, f32[1024,512]{1,0:T(8,128)S(1)} %get-tuple-element.63.refs_3_, ...), custom_call_target="tpu_custom_call" | custom-call | flops 1 | bytes 1 | tf_op jit(solution)/shard_map/pallas_call | solution.py:69
  79.7 3.9 %collective-permute-done.19.refs_9_.refs_3_ = bf16[128,512]{1,0:T(8,128)(2,1)S(1)} collective-permute-done((bf16[128,512]{1,0:T(8,128)(2,1)S(1)}, bf16[128,512]{1,0:T(8,128)(2,1)S(1)}, u32[]{:S(2)}, u32[]{:S(2)}) %collective-permute-start.19) | collective-permute-done | bytes 131104 | tf_op jit(solution)/shard_map/ppermute | solution.py:48
  89.2 4.2 %collective-permute-done.20.refs_0_ = bf16[384,512]{1,0:T(8,128)(2,1)S(1)} collective-permute-done((bf16[384,512]{1,0:T(8,128)(2,1)S(1)}, bf16[384,512]{1,0:T(8,128)(2,1)S(1)}, u32[]{:S(2)}, u32[]{:S(2)}) %collective-permute-start.20) | collective-permute-done | bytes 393248 | tf_op jit(solution)/shard_map/ppermute | solution.py:48
  93.4 3.5 %collective-permute-done.21.refs_1_ = bf16[384,512]{1,0:T(8,128)(2,1)S(1)} collective-permute-done((bf16[384,512]{1,0:T(8,128)(2,1)S(1)}, bf16[384,512]{1,0:T(8,128)(2,1)S(1)}, u32[]{:S(2)}, u32[]{:S(2)}) %collective-permute-start.21) | collective-permute-done | bytes 393248 | tf_op jit(solution)/shard_map/ppermute | solution.py:48
  98.8 3.6 %collective-permute-start.23 = (bf16[128,512]{1,0:T(8,128)(2,1)S(1)}, bf16[128,512]{1,0:T(8,128)(2,1)S(1)}, u32[]{:S(2)}, u32[]{:S(2)}) collective-permute-start(bf16[128,512]{1,0:T(8,128)(2,1)S(1)} %get-tuple-element.81), channel_id=1, source_target_pairs={{0,96},{1,113},{2,115},{3,112},{4,100},{5,117},{6,119},{7,116},{8,... | collective-permute-start | bytes 393224 | tf_op jit(solution)/shard_map/ppermute | solution.py:48
  104.3 2.1 %collective-permute-done.23.refs_4_ = bf16[128,512]{1,0:T(8,128)(2,1)S(1)} collective-permute-done((bf16[128,512]{1,0:T(8,128)(2,1)S(1)}, bf16[128,512]{1,0:T(8,128)(2,1)S(1)}, u32[]{:S(2)}, u32[]{:S(2)}) %collective-permute-start.23) | collective-permute-done | bytes 131104 | tf_op jit(solution)/shard_map/ppermute | solution.py:48
  106.3 4.6 %collective-permute-done.24.refs_5_ = bf16[128,512]{1,0:T(8,128)(2,1)S(1)} collective-permute-done((bf16[128,512]{1,0:T(8,128)(2,1)S(1)}, bf16[128,512]{1,0:T(8,128)(2,1)S(1)}, u32[]{:S(2)}, u32[]{:S(2)}) %collective-permute-start.24) | collective-permute-done | bytes 131104 | tf_op jit(solution)/shard_map/ppermute | solution.py:48
  113.9 3.2 %collective-permute-start.27 = (bf16[256,512]{1,0:T(8,128)(2,1)S(1)}, bf16[256,512]{1,0:T(8,128)(2,1)S(1)}, u32[]{:S(2)}, u32[]{:S(2)}) collective-permute-start(bf16[256,512]{1,0:T(8,128)(2,1)S(1)} %get-tuple-element.71), channel_id=1, source_target_pairs={{0,8},{1,9},{2,10},{3,11},{4,12},{5,13},{6,14},{7,15},{8,0},{9,1},... | collective-permute-start | bytes 786440 | tf_op jit(solution)/shard_map/ppermute | solution.py:48
  119.0 5.2 %shard_map.65 = (bf16[1024,512]{1,0:T(8,128)(2,1)}, f32[8,128]{1,0:T(8,128)S(1)}) custom-call(bf16[1024,8192]{1,0:T(8,128)(2,1)} %refs_0_.13, bf16[1024,512]{1,0:T(8,128)(2,1)S(1)} %collective-permute-done.5.refs_1_.refs_4_, bf16[1024,512]{1,0:T(8,128)(2,1)S(1)} %get-tuple-element.78.refs_5_.refs_2_, f32[1024,512]{1,0:T(8,128)S(1)} %get-tuple-element.73.refs_3_, ...), custom_call_target="tpu_custom_call" | custom-call | flops 1 | bytes 1 | tf_op jit(solution)/shard_map/pallas_call | solution.py:69
  124.2 2.3 %collective-permute-done.27.refs_2_ = bf16[256,512]{1,0:T(8,128)(2,1)S(1)} collective-permute-done((bf16[256,512]{1,0:T(8,128)(2,1)S(1)}, bf16[256,512]{1,0:T(8,128)(2,1)S(1)}, u32[]{:S(2)}, u32[]{:S(2)}) %collective-permute-start.27) | collective-permute-done | bytes 262176 | tf_op jit(solution)/shard_map/ppermute | solution.py:48
  126.6 3.6 %collective-permute-start.29 = (bf16[512,512]{1,0:T(8,128)(2,1)S(1)}, bf16[512,512]{1,0:T(8,128)(2,1)S(1)}, u32[]{:S(2)}, u32[]{:S(2)}) collective-permute-start(bf16[512,512]{1,0:T(8,128)(2,1)S(1)} %get-tuple-element.76), channel_id=1, source_target_pairs={{0,16},{1,17},{2,18},{3,19},{4,20},{5,21},{6,22},{7,23},{8,24},{9,... | collective-permute-start | bytes 1572872 | tf_op jit(solution)/shard_map/ppermute | solution.py:48
  (65 shorter events, 44.2 us)
Async XLA Ops:
  2.1 26.7 %collective-permute-start.4 = (bf16[1024,512]{1,0:T(8,128)(2,1)}, bf16[1024,512]{1,0:T(8,128)(2,1)S(1)}, u32[]{:S(2)}, u32[]{:S(2)}) collective-permute-start(bf16[1024,512]{1,0:T(8,128)(2,1)} %refs_0_.10), channel_id=1, source_target_pairs={{0,96},{1,97},{2,98},{3,99},{4,100},{5,101},{6,102},{7,103},{8,104... | collective-permute-start | bytes 3145736 | tf_op jit(solution)/shard_map/ppermute | solution.py:48
  6.0 25.8 %collective-permute-start.5 = (bf16[1024,512]{1,0:T(8,128)(2,1)}, bf16[1024,512]{1,0:T(8,128)(2,1)S(1)}, u32[]{:S(2)}, u32[]{:S(2)}) collective-permute-start(bf16[1024,512]{1,0:T(8,128)(2,1)} %refs_0_.10), channel_id=1, source_target_pairs={{0,32},{1,33},{2,34},{3,35},{4,36},{5,37},{6,38},{7,39},{8,40},{9,... | collective-permute-start | bytes 3145736 | tf_op jit(solution)/shard_map/ppermute | solution.py:48
  9.2 22.8 %collective-permute-start.1 = (bf16[4,192,512]{2,1,0:T(8,128)(2,1)S(1)}, bf16[4,192,512]{2,1,0:T(8,128)(2,1)S(1)}, u32[]{:S(2)}, u32[]{:S(2)}) collective-permute-start(bf16[4,192,512]{2,1,0:T(8,128)(2,1)S(1)} %get-tuple-element.40.refs_3_), channel_id=1, source_target_pairs={{0,4},{1,5},{2,6},{3,7},{4,8},{5,9},{6,10},{7,11},{8,12},{9,13},{1... | collective-permute-start | bytes 2359304 | tf_op jit(solution)/shard_map/ppermute | solution.py:48
  10.5 21.4 %collective-permute-start.2 = (bf16[4,192,512]{2,1,0:T(8,128)(2,1)S(1)}, bf16[4,192,512]{2,1,0:T(8,128)(2,1)S(1)}, u32[]{:S(2)}, u32[]{:S(2)}) collective-permute-start(bf16[4,192,512]{2,1,0:T(8,128)(2,1)S(1)} %get-tuple-element.41), channel_id=1, source_target_pairs={{0,12},{1,13},{2,14},{3,15},{4,0},{5,1},{6,2},{7,3},{8,4},{9,5},{1... | collective-permute-start | bytes 2359304 | tf_op jit(solution)/shard_map/ppermute | solution.py:48
  12.0 19.9 %collective-permute-start.3 = (bf16[4,192,512]{2,1,0:T(8,128)(2,1)S(1)}, bf16[4,192,512]{2,1,0:T(8,128)(2,1)S(1)}, u32[]{:S(2)}, u32[]{:S(2)}) collective-permute-start(bf16[4,192,512]{2,1,0:T(8,128)(2,1)S(1)} %get-tuple-element.42), channel_id=1, source_target_pairs={{0,8},{1,9},{2,10},{3,11},{4,12},{5,13},{6,14},{7,15},{8,0},{9,1},... | collective-permute-start | bytes 2359304 | tf_op jit(solution)/shard_map/ppermute | solution.py:48
  32.1 6.8 %collective-permute-start.9 = (bf16[2,1024,512]{2,1,0:T(8,128)(2,1)S(1)}, bf16[2,1024,512]{2,1,0:T(8,128)(2,1)S(1)}, u32[]{:S(2)}, u32[]{:S(2)}) collective-permute-start(bf16[2,1024,512]{2,1,0:T(8,128)(2,1)S(1)} %shard_map.53.refs_4_), channel_id=1, source_target_pairs={{0,16},{1,17},{2,18},{3,19},{4,20},{5,21},{6,22},{7,23},{8,24},{9,... | collective-permute-start | bytes 6291464 | tf_op jit(solution)/shard_map/ppermute | solution.py:48
  33.4 13.9 %collective-permute-start.12 = (bf16[1024,512]{1,0:T(8,128)(2,1)S(1)}, bf16[1024,512]{1,0:T(8,128)(2,1)S(1)}, u32[]{:S(2)}, u32[]{:S(2)}) collective-permute-start(bf16[1024,512]{1,0:T(8,128)(2,1)S(1)} %shard_map.52.refs_2_), channel_id=1, source_target_pairs={{0,32},{1,33},{2,34},{3,35},{4,36},{5,37},{6,38},{7,39},{8,40},{9,... | collective-permute-start | bytes 3145736 | tf_op jit(solution)/shard_map/ppermute | solution.py:48
  36.9 6.3 %collective-permute-start.7 = (bf16[192,512]{1,0:T(8,128)(2,1)S(1)}, bf16[192,512]{1,0:T(8,128)(2,1)S(1)}, u32[]{:S(2)}, u32[]{:S(2)}) collective-permute-start(bf16[192,512]{1,0:T(8,128)(2,1)S(1)} %get-tuple-element.46), channel_id=1, source_target_pairs={{0,3},{1,0},{2,1},{3,2},{4,7},{5,4},{6,5},{7,6},{8,11},{9,8},{10,9... | collective-permute-start | bytes 589832 | tf_op jit(solution)/shard_map/ppermute | solution.py:48
  49.6 15.2 %collective-permute-start.10 = (bf16[4,256,512]{2,1,0:T(8,128)(2,1)S(1)}, bf16[4,256,512]{2,1,0:T(8,128)(2,1)S(1)}, u32[]{:S(2)}, u32[]{:S(2)}) collective-permute-start(bf16[4,256,512]{2,1,0:T(8,128)(2,1)S(1)} %get-tuple-element.49.refs_4_), channel_id=1, source_target_pairs={{0,4},{1,5},{2,6},{3,7},{4,8},{5,9},{6,10},{7,11},{8,12},{9,13},{1... | collective-permute-start | bytes 3145736 | tf_op jit(solution)/shard_map/ppermute | solution.py:48
  50.9 13.9 %collective-permute-start.11 = (bf16[4,256,512]{2,1,0:T(8,128)(2,1)S(1)}, bf16[4,256,512]{2,1,0:T(8,128)(2,1)S(1)}, u32[]{:S(2)}, u32[]{:S(2)}) collective-permute-start(bf16[4,256,512]{2,1,0:T(8,128)(2,1)S(1)} %get-tuple-element.50), channel_id=1, source_target_pairs={{0,12},{1,13},{2,14},{3,15},{4,0},{5,1},{6,2},{7,3},{8,4},{9,5},{1... | collective-permute-start | bytes 3145736 | tf_op jit(solution)/shard_map/ppermute | solution.py:48
  53.7 16.8 %collective-permute-start.14 = (bf16[4,128,512]{2,1,0:T(8,128)(2,1)S(1)}, bf16[4,128,512]{2,1,0:T(8,128)(2,1)S(1)}, u32[]{:S(2)}, u32[]{:S(2)}) collective-permute-start(bf16[4,128,512]{2,1,0:T(8,128)(2,1)S(1)} %get-tuple-element.52.refs_4_), channel_id=1, source_target_pairs={{0,4},{1,5},{2,6},{3,7},{4,8},{5,9},{6,10},{7,11},{8,12},{9,13},{1... | collective-permute-start | bytes 1572872 | tf_op jit(solution)/shard_map/ppermute | solution.py:48
  54.6 15.9 %collective-permute-start.15 = (bf16[4,128,512]{2,1,0:T(8,128)(2,1)S(1)}, bf16[4,128,512]{2,1,0:T(8,128)(2,1)S(1)}, u32[]{:S(2)}, u32[]{:S(2)}) collective-permute-start(bf16[4,128,512]{2,1,0:T(8,128)(2,1)S(1)} %get-tuple-element.53), channel_id=1, source_target_pairs={{0,12},{1,13},{2,14},{3,15},{4,0},{5,1},{6,2},{7,3},{8,4},{9,5},{1... | collective-permute-start | bytes 1572872 | tf_op jit(solution)/shard_map/ppermute | solution.py:48
  70.8 13.8 %collective-permute-start.17 = (bf16[4,192,512]{2,1,0:T(8,128)(2,1)S(1)}, bf16[4,192,512]{2,1,0:T(8,128)(2,1)S(1)}, u32[]{:S(2)}, u32[]{:S(2)}) collective-permute-start(bf16[4,192,512]{2,1,0:T(8,128)(2,1)S(1)} %get-tuple-element.61), channel_id=1, source_target_pairs={{0,4},{1,5},{2,6},{3,7},{4,8},{5,9},{6,10},{7,11},{8,12},{9,13},{1... | collective-permute-start | bytes 2359304 | tf_op jit(solution)/shard_map/ppermute | solution.py:48
  72.2 12.5 %collective-permute-start.18 = (bf16[4,192,512]{2,1,0:T(8,128)(2,1)S(1)}, bf16[4,192,512]{2,1,0:T(8,128)(2,1)S(1)}, u32[]{:S(2)}, u32[]{:S(2)}) collective-permute-start(bf16[4,192,512]{2,1,0:T(8,128)(2,1)S(1)} %get-tuple-element.62), channel_id=1, source_target_pairs={{0,12},{1,13},{2,14},{3,15},{4,0},{5,1},{6,2},{7,3},{8,4},{9,5},{1... | collective-permute-start | bytes 2359304 | tf_op jit(solution)/shard_map/ppermute | solution.py:48
  73.6 9.9 %collective-permute-start.19 = (bf16[128,512]{1,0:T(8,128)(2,1)S(1)}, bf16[128,512]{1,0:T(8,128)(2,1)S(1)}, u32[]{:S(2)}, u32[]{:S(2)}) collective-permute-start(bf16[128,512]{1,0:T(8,128)(2,1)S(1)} %slice.26), channel_id=1, source_target_pairs={{2,19},{3,16},{6,23},{7,20},{10,27},{11,24},{14,31},{15,28},{16,17... | collective-permute-start | bytes 393224 | tf_op jit(solution)/shard_map/ppermute | solution.py:48
  85.2 8.2 %collective-permute-start.20 = (bf16[384,512]{1,0:T(8,128)(2,1)S(1)}, bf16[384,512]{1,0:T(8,128)(2,1)S(1)}, u32[]{:S(2)}, u32[]{:S(2)}) collective-permute-start(bf16[384,512]{1,0:T(8,128)(2,1)S(1)} %get-tuple-element.65), channel_id=1, source_target_pairs={{0,1},{1,2},{2,3},{3,0},{4,5},{5,6},{6,7},{7,4},{8,9},{9,10},{10,1... | collective-permute-start | bytes 1179656 | tf_op jit(solution)/shard_map/ppermute | solution.py:48
  86.2 10.7 %collective-permute-start.21 = (bf16[384,512]{1,0:T(8,128)(2,1)S(1)}, bf16[384,512]{1,0:T(8,128)(2,1)S(1)}, u32[]{:S(2)}, u32[]{:S(2)}) collective-permute-start(bf16[384,512]{1,0:T(8,128)(2,1)S(1)} %get-tuple-element.66), channel_id=1, source_target_pairs={{0,3},{1,0},{2,1},{3,2},{4,7},{5,4},{6,5},{7,6},{8,11},{9,8},{10,9... | collective-permute-start | bytes 1179656 | tf_op jit(solution)/shard_map/ppermute | solution.py:48
  88.0 10.7 %collective-permute-start.22 = (bf16[384,512]{1,0:T(8,128)(2,1)S(1)}, bf16[384,512]{1,0:T(8,128)(2,1)S(1)}, u32[]{:S(2)}, u32[]{:S(2)}) collective-permute-start(bf16[384,512]{1,0:T(8,128)(2,1)S(1)} %get-tuple-element.67), channel_id=1, source_target_pairs={{0,2},{1,3},{2,0},{3,1},{4,6},{5,7},{6,4},{7,5},{8,10},{9,11},{10,... | collective-permute-start | bytes 1179656 | tf_op jit(solution)/shard_map/ppermute | solution.py:48
  98.8 7.5 %collective-permute-start.23 = (bf16[128,512]{1,0:T(8,128)(2,1)S(1)}, bf16[128,512]{1,0:T(8,128)(2,1)S(1)}, u32[]{:S(2)}, u32[]{:S(2)}) collective-permute-start(bf16[128,512]{1,0:T(8,128)(2,1)S(1)} %get-tuple-element.81), channel_id=1, source_target_pairs={{0,96},{1,113},{2,115},{3,112},{4,100},{5,117},{6,119},{7,116},{8,... | collective-permute-start | bytes 393224 | tf_op jit(solution)/shard_map/ppermute | solution.py:48
  102.5 8.5 %collective-permute-start.24 = (bf16[128,512]{1,0:T(8,128)(2,1)S(1)}, bf16[128,512]{1,0:T(8,128)(2,1)S(1)}, u32[]{:S(2)}, u32[]{:S(2)}) collective-permute-start(bf16[128,512]{1,0:T(8,128)(2,1)S(1)} %get-tuple-element.82.refs_2_), channel_id=1, source_target_pairs={{0,64},{1,81},{2,83},{3,80},{4,68},{5,85},{6,87},{7,84},{8,72},{9,... | collective-permute-start | bytes 393224 | tf_op jit(solution)/shard_map/ppermute | solution.py:48
  103.1 9.7 %collective-permute-start.25 = (bf16[128,512]{1,0:T(8,128)(2,1)S(1)}, bf16[128,512]{1,0:T(8,128)(2,1)S(1)}, u32[]{:S(2)}, u32[]{:S(2)}) collective-permute-start(bf16[128,512]{1,0:T(8,128)(2,1)S(1)} %get-tuple-element.80), channel_id=1, source_target_pairs={{0,32},{1,49},{2,51},{3,48},{4,36},{5,53},{6,55},{7,52},{8,40},{9,... | collective-permute-start | bytes 393224 | tf_op jit(solution)/shard_map/ppermute | solution.py:48
  112.9 11.3 %collective-permute-start.26 = (bf16[256,512]{1,0:T(8,128)(2,1)S(1)}, bf16[256,512]{1,0:T(8,128)(2,1)S(1)}, u32[]{:S(2)}, u32[]{:S(2)}) collective-permute-start(bf16[256,512]{1,0:T(8,128)(2,1)S(1)} %get-tuple-element.70), channel_id=1, source_target_pairs={{0,4},{1,5},{2,6},{3,7},{4,8},{5,9},{6,10},{7,11},{8,12},{9,13},{1... | collective-permute-start | bytes 786440 | tf_op jit(solution)/shard_map/ppermute | solution.py:48
  113.9 12.5 %collective-permute-start.27 = (bf16[256,512]{1,0:T(8,128)(2,1)S(1)}, bf16[256,512]{1,0:T(8,128)(2,1)S(1)}, u32[]{:S(2)}, u32[]{:S(2)}) collective-permute-start(bf16[256,512]{1,0:T(8,128)(2,1)S(1)} %get-tuple-element.71), channel_id=1, source_target_pairs={{0,8},{1,9},{2,10},{3,11},{4,12},{5,13},{6,14},{7,15},{8,0},{9,1},... | collective-permute-start | bytes 786440 | tf_op jit(solution)/shard_map/ppermute | solution.py:48
  117.1 9.4 %collective-permute-start.28 = (bf16[256,512]{1,0:T(8,128)(2,1)S(1)}, bf16[256,512]{1,0:T(8,128)(2,1)S(1)}, u32[]{:S(2)}, u32[]{:S(2)}) collective-permute-start(bf16[256,512]{1,0:T(8,128)(2,1)S(1)} %get-tuple-element.72), channel_id=1, source_target_pairs={{0,12},{1,13},{2,14},{3,15},{4,0},{5,1},{6,2},{7,3},{8,4},{9,5},{1... | collective-permute-start | bytes 786440 | tf_op jit(solution)/shard_map/ppermute | solution.py:48
  (9 other events, 51.9 us)
